TPU v7x, 32 devices: a whole 2x2x4 slice. The times are simulated.
32 devices in a mesh: gx: 4 (over y, x), gy: 4 (over z), af: 2 (over core).
Axes of the slice: x: 2, y: 2, z: 4, core: 2. Of those that a mesh axis runs over, the one named last changes fastest.
Arguments:
- model: float32 [128, 128, 128], P('gx', 'gy'), may hold values from 0.5 to 2
- freq_sq: float32 [4], P('af'), may hold values from 0.5 to 3
- source: float32 [4, 2, 128, 128, 128], P('af', None, 'gx', 'gy'), may hold values from -20 to 20
- observed: float32 [4, 2, 128, 128], P('af', None, 'gx', 'gy'), may hold values from -6 to 6
- receiver_depth: int32 [128, 128], P('gx', 'gy'), may hold values from 0 to 3
Outputs:
- wavefield: float32 [4, 2, 128, 128, 128], P('af', None, 'gx', 'gy')
- gradient: float32 [128, 128, 128], P('gx', 'gy')
Inputs may be any that keep to these rules, and one draw needn't show every extreme that they name: `receiver_depth`: every surface column holds one receiver, at the given depth index.
All inputs are finite; a program needn't handle non-finite values.
Results may differ from a plain program's by a relative error of at most 0.00012.
Values sent between devices are 32-bit elements; how exact they have to be, the bound alone decides.
No kernel may reach another device: no remote copies, remote signals or barrier semaphores. Data moves between devices by JAX's collectives and lax.ppermute only.
A program may use at most 64 MiB of HBM per device.

v0:
```python
import jax
import jax.numpy as jnp
from jax import lax
from jax.sharding import PartitionSpec as P

ITERS = 2


attenuation = 0.2
penalty = 4.0


def padded_2(cells, sides, width):
    for axis, dim in sides:
        count = lax.axis_size(axis)
        ends = count - 1
        head = lax.slice_in_dim(cells, 0, width, axis=dim)
        tail = lax.slice_in_dim(cells, cells.shape[dim] - width, cells.shape[dim], axis=dim)
        cells = jnp.concatenate(
            [
                lax.ppermute(tail, axis, [(i, (i + 1) % count) for i in range(ends)]),
                cells,
                lax.ppermute(head, axis, [((i + 1) % count, i) for i in range(ends)]),
            ],
            axis=dim,
        )
    return cells


def stencil_sum(padded):
    center = padded[:, :, 1:-1, 1:-1]
    total = padded[:, :, 2:, 1:-1] + padded[:, :, :-2, 1:-1]
    total = total + padded[:, :, 1:-1, 2:] + padded[:, :, 1:-1, :-2]
    upper = jnp.pad(center[..., 1:], ((0, 0), (0, 0), (0, 0), (0, 0), (0, 1)))
    lower = jnp.pad(center[..., :-1], ((0, 0), (0, 0), (0, 0), (0, 0), (1, 0)))
    return (center, total + upper + lower)


def apply_coef(coef_real, coef_imag, field, sign):
    real_part = coef_real * field[:, 0] - sign * coef_imag * field[:, 1]
    imag_part = coef_real * field[:, 1] + sign * coef_imag * field[:, 0]
    return jnp.stack([real_part, imag_part], axis=1)


def beside(field):
    padded = padded_2(field, (("gx", 2), ("gy", 3)), 1)
    center, total = stencil_sum(padded)
    return total


def inner(left, right):
    return jnp.sum(left * right, axis=(1, 2, 3, 4))


def expand(values):
    return values[:, None, None, None, None]


def two_products(resid, image):
    return lax.psum((inner(resid, resid), inner(resid, image)), ("gx", "gy"))


def on_device(model, freq_sq, source, observed, receiver_depth):
    squared = freq_sq[:, None, None, None]
    coef_real = 6.0 - squared * model[None]
    coef_imag = attenuation * squared * model[None]
    levels = lax.broadcasted_iota(jnp.int32, model.shape, 2)
    onehot = (levels == receiver_depth[:, :, None]).astype(jnp.float32)
    weights = penalty * onehot

    def forward(field):
        return apply_coef(coef_real, coef_imag, field, 1.0) - beside(field)

    def adjoint(field):
        return apply_coef(coef_real, coef_imag, field, -1.0) - beside(field)

    def normal(field):
        return adjoint(forward(field)) + weights * field

    rhs = adjoint(source) + weights * observed[:, :, :, :, None]
    field = jnp.zeros_like(rhs)
    resid = rhs
    image = normal(resid)
    norm_now, product = two_products(resid, image)
    alpha = norm_now / product
    direction = resid
    along = image
    for sweep in range(ITERS):
        field = field + expand(alpha) * direction
        resid = resid - expand(alpha) * along
        if sweep + 1 < ITERS:
            image = normal(resid)
            norm_next, product = two_products(resid, image)
            ratio = norm_next / norm_now
            alpha = norm_next / (product - ratio * norm_next / alpha)
            direction = resid + expand(ratio) * direction
            along = image + expand(ratio) * along
            norm_now = norm_next
    misfit = forward(field) - source
    deriv_real = -squared
    deriv_imag = attenuation * squared
    wave_real = deriv_real * field[:, 0] - deriv_imag * field[:, 1]
    wave_imag = deriv_real * field[:, 1] + deriv_imag * field[:, 0]
    local_terms = jnp.sum(wave_real * misfit[:, 0] + wave_imag * misfit[:, 1], axis=0)
    gradient = lax.psum(local_terms, "af")
    return (field, gradient)


def solution(mesh):
    in_specs = (
        P("gx", "gy", None),
        P("af"),
        P("af", None, "gx", "gy", None),
        P("af", None, "gx", "gy"),
        P("gx", "gy"),
    )
    out_specs = (P("af", None, "gx", "gy", None), P("gx", "gy", None))
    return jax.shard_map(
        on_device, mesh=mesh, in_specs=in_specs, out_specs=out_specs, check_vma=False
    )
```

profile of v0, /device:TPU:0, one launch (start us, length us, event | category | flops | bytes accessed | tf_op | source)
XLA Modules:
  0.0 261.4 jit_solution(4293541968087813163)
XLA Ops:
  8.2 1.3 collective-permute-start
  9.6 5.6 %collective-permute-start.1 = (f32[2,2,1,32,128]{4,2,3,0,1:T(1,128)S(1)}, f32[2,2,1,32,128]{4,2,3,0,1:T(1,128)S(1)}, u32[]{:S(2)}, u32[]{:S(2)}) collective-permute-start(f32[2,2,1,32,128]{4,2,3,0,1:T(1,128)S(1)} %copy.52), channel_id=1, source_target_pairs={{0,8},{8,16},{16,24},{1,9},{9,17},{17,25},{2,10},{10,18},{18,26},{... | collective-permute-start | bytes 196616 | tf_op jit(solution)/shard_map/ppermute | solution.py:21
  15.2 2.8 %copy.48 = f32[2,2,32,32,128]{4,2,3,0,1:T(8,128)S(1)} copy(f32[2,2,32,32,128]{4,3,2,1,0:T(8,128)} %param.7) | data formatting | bytes 4194304 | tf_op args[2]
  18.4 2.8 %fusion.79 = (f32[2,2,32,32,127]{4,2,3,0,1:T(8,128)}, f32[2,2,32,32,127]{4,2,3,0,1:T(8,128)}) fusion(f32[2,2,32,32,128]{4,2,3,0,1:T(8,128)S(1)} %copy.48), kind=kLoop, calls=%fused_computation.163 | loop fusion | bytes 8323072 | tf_op jit(solution)/shard_map/slice | solution.py:34
  21.2 1.9 fusion.48
  23.8 1.3 collective-permute-start.2
  25.1 4.6 %collective-permute-start.3 = (f32[2,2,34,1,128]{4,2,3,0,1:T(8,128)}, f32[2,2,34,1,128]{4,2,3,0,1:T(8,128)S(1)}, u32[]{:S(2)}, u32[]{:S(2)}) collective-permute-start(f32[2,2,34,1,128]{4,2,3,0,1:T(8,128)} %get-tuple-element.40), channel_id=1, source_target_pairs={{0,2},{2,4},{4,6},{1,3},{3,5},{5,7},{8,10},{10,12},{12,14},{9,11},... | collective-permute-start | bytes 208904 | tf_op jit(solution)/shard_map/ppermute | solution.py:21
  30.9 1.2 collective-permute-done.3
  32.1 7.4 %fusion.45 = f32[2,2,32,32,128]{4,2,3,0,1:T(8,128)S(1)} fusion(f32[2,2,34,1,128]{4,2,3,0,1:T(8,128)S(1)} %collective-permute-done.3, f32[2,2,1,32,128]{4,2,3,0,1:T(1,128)S(1)} %collective-permute-done, f32[2,2,32,32,128]{4,2,3,0,1:T(8,128)} %copy-done.2, f32[2,2,1,32,128]{4,2,3,0,1:T(1,128)S(1)} %collective-permute-done.1, ...), kind=kLoop, calls=%fused_computation.92 | loop fusion | flops 8912896 | bytes 11264000 | tf_op jit(solution)/shard_map/add | solution.py:80
  39.6 1.3 collective-permute-start.4
  40.9 5.4 %collective-permute-start.5 = (f32[2,2,1,32,128]{4,2,3,0,1:T(1,128)S(1)}, f32[2,2,1,32,128]{4,2,3,0,1:T(1,128)S(1)}, u32[]{:S(2)}, u32[]{:S(2)}) collective-permute-start(f32[2,2,1,32,128]{4,2,3,0,1:T(1,128)S(1)} %get-tuple-element.59), channel_id=1, source_target_pairs={{0,8},{8,16},{16,24},{1,9},{9,17},{17,25},{2,10},{10,18},{18,26},{... | collective-permute-start | bytes 196616 | tf_op jit(solution)/shard_map/ppermute | solution.py:21
  48.2 1.3 collective-permute-start.6
  49.5 4.8 %collective-permute-start.7 = (f32[2,2,34,1,128]{4,2,3,0,1:T(8,128)S(1)}, f32[2,2,34,1,128]{4,2,3,0,1:T(8,128)S(1)}, u32[]{:S(2)}, u32[]{:S(2)}) collective-permute-start(f32[2,2,34,1,128]{4,2,3,0,1:T(8,128)S(1)} %get-tuple-element.38), channel_id=1, source_target_pairs={{0,2},{2,4},{4,6},{1,3},{3,5},{5,7},{8,10},{10,12},{12,14},{9,11},... | collective-permute-start | bytes 208904 | tf_op jit(solution)/shard_map/ppermute | solution.py:21
  54.8 1.6 collective-permute-done.7
  56.3 2.1 fusion.38
  58.6 1.3 collective-permute-start.8
  59.9 5.4 %collective-permute-start.9 = (f32[2,2,1,32,128]{4,2,3,0,1:T(1,128)S(1)}, f32[2,2,1,32,128]{4,2,3,0,1:T(1,128)S(1)}, u32[]{:S(2)}, u32[]{:S(2)}) collective-permute-start(f32[2,2,1,32,128]{4,2,3,0,1:T(1,128)S(1)} %get-tuple-element.53), channel_id=1, source_target_pairs={{0,8},{8,16},{16,24},{1,9},{9,17},{17,25},{2,10},{10,18},{18,26},{... | collective-permute-start | bytes 196616 | tf_op jit(solution)/shard_map/ppermute | solution.py:21
  67.2 1.3 collective-permute-start.10
  68.5 4.9 %collective-permute-start.11 = (f32[2,2,34,1,128]{4,2,3,0,1:T(8,128)S(1)}, f32[2,2,34,1,128]{4,2,3,0,1:T(8,128)S(1)}, u32[]{:S(2)}, u32[]{:S(2)}) collective-permute-start(f32[2,2,34,1,128]{4,2,3,0,1:T(8,128)S(1)} %get-tuple-element.36), channel_id=1, source_target_pairs={{0,2},{2,4},{4,6},{1,3},{3,5},{5,7},{8,10},{10,12},{12,14},{9,11},... | collective-permute-start | bytes 208904 | tf_op jit(solution)/shard_map/ppermute | solution.py:21
  73.9 1.6 collective-permute-done.11
  75.5 4.1 %multiply_reduce_fusion.1 = (f32[2]{0:T(128)S(1)}, f32[2]{0:T(128)S(1)}, f32[2,2,32,32,128]{4,2,3,0,1:T(8,128)}) fusion(f32[2,2,32,32,128]{4,2,3,0,1:T(8,128)S(1)} %fusion.45, f32[32,32,128]{2,0,1:T(8,128)S(1)} %fusion.66, f32[2,2,32,32,127]{4,2,3,0,1:T(8,128)S(1)} %get-tuple-element.56, f32[2,2,32,32,127]{4,2,3,0,1:T(8,128)S(1)} %get-tuple-element.55, ...), kind=kLoop, calls=%fused_computation.106 | loop fusion | flops 11010044 | bytes 13344784 | tf_op jit(solution)/shard_map/reduce_sum | solution.py:52
  79.6 47.1 %all-reduce.13 = (f32[2]{0:T(128)S(1)}, f32[2]{0:T(128)S(1)}) all-reduce(f32[2]{0:T(128)S(1)} %get-tuple-element.9, f32[2]{0:T(128)S(1)} %get-tuple-element.8), channel_id=1, replica_groups=mesh['gx'=4,'gy'=4,'af'=2] {'gx','gy'}, use_global_device_ids=true, to_apply=%region_1.2 | all-reduce | flops 4 | bytes 32 | tf_op jit(solution)/shard_map/psum | solution.py:60
  126.7 2.1 multiply_subtract_fusion
  129.0 1.3 collective-permute-start.12
  130.3 4.7 %collective-permute-start.13 = (f32[2,2,1,32,128]{4,2,3,0,1:T(1,128)S(1)}, f32[2,2,1,32,128]{4,2,3,0,1:T(1,128)S(1)}, u32[]{:S(2)}, u32[]{:S(2)}) collective-permute-start(f32[2,2,1,32,128]{4,2,3,0,1:T(1,128)S(1)} %get-tuple-element.51), channel_id=1, source_target_pairs={{0,8},{8,16},{16,24},{1,9},{9,17},{17,25},{2,10},{10,18},{18,26},{... | collective-permute-start | bytes 196616 | tf_op jit(solution)/shard_map/ppermute | solution.py:21
  136.8 1.3 collective-permute-start.14
  138.1 4.6 %collective-permute-start.15 = (f32[2,2,34,1,128]{4,2,3,0,1:T(8,128)S(1)}, f32[2,2,34,1,128]{4,2,3,0,1:T(8,128)S(1)}, u32[]{:S(2)}, u32[]{:S(2)}) collective-permute-start(f32[2,2,34,1,128]{4,2,3,0,1:T(8,128)S(1)} %get-tuple-element.34), channel_id=1, source_target_pairs={{0,2},{2,4},{4,6},{1,3},{3,5},{5,7},{8,10},{10,12},{12,14},{9,11},... | collective-permute-start | bytes 208904 | tf_op jit(solution)/shard_map/ppermute | solution.py:21
  143.1 1.6 collective-permute-done.15
  144.7 2.0 fusion.25
  146.8 1.3 collective-permute-start.16
  148.1 5.0 %collective-permute-start.17 = (f32[2,2,1,32,128]{4,2,3,0,1:T(1,128)S(1)}, f32[2,2,1,32,128]{4,2,3,0,1:T(1,128)S(1)}, u32[]{:S(2)}, u32[]{:S(2)}) collective-permute-start(f32[2,2,1,32,128]{4,2,3,0,1:T(1,128)S(1)} %get-tuple-element.47), channel_id=1, source_target_pairs={{0,8},{8,16},{16,24},{1,9},{9,17},{17,25},{2,10},{10,18},{18,26},{... | collective-permute-start | bytes 196616 | tf_op jit(solution)/shard_map/ppermute | solution.py:21
  155.0 1.3 collective-permute-start.18
  156.3 4.9 %collective-permute-start.19 = (f32[2,2,34,1,128]{4,2,3,0,1:T(8,128)S(1)}, f32[2,2,34,1,128]{4,2,3,0,1:T(8,128)S(1)}, u32[]{:S(2)}, u32[]{:S(2)}) collective-permute-start(f32[2,2,34,1,128]{4,2,3,0,1:T(8,128)S(1)} %get-tuple-element.32), channel_id=1, source_target_pairs={{0,2},{2,4},{4,6},{1,3},{3,5},{5,7},{8,10},{10,12},{12,14},{9,11},... | collective-permute-start | bytes 208904 | tf_op jit(solution)/shard_map/ppermute | solution.py:21
  161.7 1.6 collective-permute-done.19
  163.2 3.1 %fusion.19 = (f32[2]{0:T(128)S(1)}, f32[2]{0:T(128)S(1)}) fusion(f32[2,2,32,32,128]{4,2,3,0,1:T(8,128)S(1)} %multiply_subtract_fusion, f32[2,2,34,1,128]{4,2,3,0,1:T(8,128)S(1)} %collective-permute-done.19, f32[2,2,1,32,128]{4,2,3,0,1:T(1,128)S(1)} %collective-permute-done.16, f32[2,2,32,32,128]{4,2,3,0,1:T(8,128)S(1)} %fusion.25, ...), kind=kLoop, calls=%fused_computation.34 | loop fusion | flops 11010044 | bytes 11247632 | tf_op jit(solution)/shard_map/reduce_sum | solution.py:52
  166.3 43.2 %all-reduce.12 = (f32[2]{0:T(128)S(1)}, f32[2]{0:T(128)S(1)}) all-reduce(f32[2]{0:T(128)S(1)} %get-tuple-element.7, f32[2]{0:T(128)S(1)} %get-tuple-element.6), channel_id=1, replica_groups=mesh['gx'=4,'gy'=4,'af'=2] {'gx','gy'}, use_global_device_ids=true, to_apply=%region_5.6 | all-reduce | flops 4 | bytes 32 | tf_op jit(solution)/shard_map/psum | solution.py:60
  209.5 2.2 multiply_add_fusion
  213.0 1.3 collective-permute-start.20
  214.3 4.5 %collective-permute-start.21 = (f32[2,2,1,32,128]{4,2,3,0,1:T(1,128)S(1)}, f32[2,2,1,32,128]{4,2,3,0,1:T(1,128)S(1)}, u32[]{:S(2)}, u32[]{:S(2)}) collective-permute-start(f32[2,2,1,32,128]{4,2,3,0,1:T(1,128)S(1)} %get-tuple-element.43), channel_id=1, source_target_pairs={{0,8},{8,16},{16,24},{1,9},{9,17},{17,25},{2,10},{10,18},{18,26},{... | collective-permute-start | bytes 196616 | tf_op jit(solution)/shard_map/ppermute | solution.py:21
  219.1 1.6 collective-permute-done.21
  220.7 1.3 collective-permute-start.22
  222.0 4.7 %collective-permute-start.23 = (f32[2,2,34,1,128]{4,2,3,1,0:T(8,128)S(1)}, f32[2,2,34,1,128]{4,2,3,1,0:T(8,128)S(1)}, u32[]{:S(2)}, u32[]{:S(2)}) collective-permute-start(f32[2,2,34,1,128]{4,2,3,1,0:T(8,128)S(1)} %get-tuple-element.30), channel_id=1, source_target_pairs={{0,2},{2,4},{4,6},{1,3},{3,5},{5,7},{8,10},{10,12},{12,14},{9,11},... | collective-permute-start | bytes 208904 | tf_op jit(solution)/shard_map/ppermute | solution.py:21
  227.1 1.6 collective-permute-done.23
  228.8 2.8 %fusion.10 = f32[2,2,32,32,128]{4,2,3,1,0:T(8,128)S(1)} fusion(f32[2,2,34,1,128]{4,2,3,1,0:T(8,128)S(1)} %collective-permute-done.23, f32[2,2,32,32,128]{4,3,2,1,0:T(8,128)S(1)} %copy-done.3, f32[2,2,32,32,128]{4,2,3,0,1:T(8,128)S(1)} %pad_maximum_fusion.47, f32[2,2,1,32,128]{4,2,3,0,1:T(1,128)S(1)} %collective-permute-done.20, ...), kind=kLoop, calls=%fused_computation.19 | loop fusion | flops 6815744 | bytes 15048704 | tf_op jit(solution)/shard_map/sub | solution.py:99
  231.6 1.4 fusion.62
  233.0 4.1 %copy.70 = f32[2,2,32,32,128]{4,3,2,1,0:T(8,128)} copy(f32[2,2,32,32,128]{4,2,3,0,1:T(8,128)} %copy-done) | data formatting | bytes 4194304
  237.2 15.2 %all-reduce.16.cloned.1.call-done = f32[32,32,128]{2,0,1:T(8,128)} async-done(((f32[32,32,128]{2,0,1:T(8,128)}), f32[32,32,128]{2,0,1:T(8,128)}) %all-reduce.16.cloned.1.call-update) | async-done | bytes 524304 | tf_op jit(solution)/shard_map/psum | solution.py:105
  252.4 2.1 copy.71
  (66 shorter events, 14.9 us)
Async XLA Ops:
  7.2 245.2 %all-reduce.16.cloned.1.call-start = ((), (), s32[]{:S(2)}) async-start(), calls=%async_computation | async-start | bytes 1048576 | tf_op jit(solution)/shard_map/psum | solution.py:105
  8.2 14.9 %collective-permute-start = (f32[2,2,1,32,128]{4,2,3,0,1:T(1,128)S(1)}, f32[2,2,1,32,128]{4,2,3,0,1:T(1,128)S(1)}, u32[]{:S(2)}, u32[]{:S(2)}) collective-permute-start(f32[2,2,1,32,128]{4,2,3,0,1:T(1,128)S(1)} %copy.50), channel_id=1, source_target_pairs={{8,0},{16,8},{24,16},{9,1},{17,9},{25,17},{10,2},{18,10},{26,18},{... | collective-permute-start | bytes 196616 | tf_op jit(solution)/shard_map/ppermute | solution.py:23
  9.6 8.5 %copy-start.5 = (f32[2]{0:T(128)S(1)}, f32[2]{0:T(128)}, u32[]{:S(2)}) copy-start(f32[2]{0:T(128)} %param.6) | copy-start | bytes 28
  9.6 8.5 %copy-start.4 = (f32[32,32,128]{2,1,0:T(8,128)S(1)}, f32[32,32,128]{2,1,0:T(8,128)}, u32[]{:S(2)}) copy-start(f32[32,32,128]{2,1,0:T(8,128)} %param.5) | copy-start | bytes 1572868
  9.6 13.5 %collective-permute-start.1 = (f32[2,2,1,32,128]{4,2,3,0,1:T(1,128)S(1)}, f32[2,2,1,32,128]{4,2,3,0,1:T(1,128)S(1)}, u32[]{:S(2)}, u32[]{:S(2)}) collective-permute-start(f32[2,2,1,32,128]{4,2,3,0,1:T(1,128)S(1)} %copy.52), channel_id=1, source_target_pairs={{0,8},{8,16},{16,24},{1,9},{9,17},{17,25},{2,10},{10,18},{18,26},{... | collective-permute-start | bytes 196616 | tf_op jit(solution)/shard_map/ppermute | solution.py:21
  18.0 5.1 %copy-start.2 = (f32[2,2,32,32,128]{4,2,3,0,1:T(8,128)}, f32[2,2,32,32,128]{4,2,3,0,1:T(8,128)S(1)}, u32[]{:S(2)}) copy-start(f32[2,2,32,32,128]{4,2,3,0,1:T(8,128)S(1)} %copy.48) | copy-start | bytes 6291460
  21.2 1.9 copy-start.6
  23.8 7.1 %collective-permute-start.2 = (f32[2,2,34,1,128]{4,2,3,0,1:T(8,128)}, f32[2,2,34,1,128]{4,2,3,0,1:T(8,128)S(1)}, u32[]{:S(2)}, u32[]{:S(2)}) collective-permute-start(f32[2,2,34,1,128]{4,2,3,0,1:T(8,128)} %get-tuple-element.39), channel_id=1, source_target_pairs={{2,0},{4,2},{6,4},{3,1},{5,3},{7,5},{10,8},{12,10},{14,12},{11,9},... | collective-permute-start | bytes 208904 | tf_op jit(solution)/shard_map/ppermute | solution.py:23
  25.1 7.0 %collective-permute-start.3 = (f32[2,2,34,1,128]{4,2,3,0,1:T(8,128)}, f32[2,2,34,1,128]{4,2,3,0,1:T(8,128)S(1)}, u32[]{:S(2)}, u32[]{:S(2)}) collective-permute-start(f32[2,2,34,1,128]{4,2,3,0,1:T(8,128)} %get-tuple-element.40), channel_id=1, source_target_pairs={{0,2},{2,4},{4,6},{1,3},{3,5},{5,7},{8,10},{10,12},{12,14},{9,11},... | collective-permute-start | bytes 208904 | tf_op jit(solution)/shard_map/ppermute | solution.py:21
  39.6 7.4 %collective-permute-start.4 = (f32[2,2,1,32,128]{4,2,3,0,1:T(1,128)S(1)}, f32[2,2,1,32,128]{4,2,3,0,1:T(1,128)S(1)}, u32[]{:S(2)}, u32[]{:S(2)}) collective-permute-start(f32[2,2,1,32,128]{4,2,3,0,1:T(1,128)S(1)} %get-tuple-element.60), channel_id=1, source_target_pairs={{8,0},{16,8},{24,16},{9,1},{17,9},{25,17},{10,2},{18,10},{26,18},{... | collective-permute-start | bytes 196616 | tf_op jit(solution)/shard_map/ppermute | solution.py:23
  40.9 7.3 %collective-permute-start.5 = (f32[2,2,1,32,128]{4,2,3,0,1:T(1,128)S(1)}, f32[2,2,1,32,128]{4,2,3,0,1:T(1,128)S(1)}, u32[]{:S(2)}, u32[]{:S(2)}) collective-permute-start(f32[2,2,1,32,128]{4,2,3,0,1:T(1,128)S(1)} %get-tuple-element.59), channel_id=1, source_target_pairs={{0,8},{8,16},{16,24},{1,9},{9,17},{17,25},{2,10},{10,18},{18,26},{... | collective-permute-start | bytes 196616 | tf_op jit(solution)/shard_map/ppermute | solution.py:21
  48.2 6.6 %collective-permute-start.6 = (f32[2,2,34,1,128]{4,2,3,0,1:T(8,128)S(1)}, f32[2,2,34,1,128]{4,2,3,0,1:T(8,128)S(1)}, u32[]{:S(2)}, u32[]{:S(2)}) collective-permute-start(f32[2,2,34,1,128]{4,2,3,0,1:T(8,128)S(1)} %get-tuple-element.37), channel_id=1, source_target_pairs={{2,0},{4,2},{6,4},{3,1},{5,3},{7,5},{10,8},{12,10},{14,12},{11,9},... | collective-permute-start | bytes 208904 | tf_op jit(solution)/shard_map/ppermute | solution.py:23
  49.5 6.9 %collective-permute-start.7 = (f32[2,2,34,1,128]{4,2,3,0,1:T(8,128)S(1)}, f32[2,2,34,1,128]{4,2,3,0,1:T(8,128)S(1)}, u32[]{:S(2)}, u32[]{:S(2)}) collective-permute-start(f32[2,2,34,1,128]{4,2,3,0,1:T(8,128)S(1)} %get-tuple-element.38), channel_id=1, source_target_pairs={{0,2},{2,4},{4,6},{1,3},{3,5},{5,7},{8,10},{10,12},{12,14},{9,11},... | collective-permute-start | bytes 208904 | tf_op jit(solution)/shard_map/ppermute | solution.py:21
  58.6 7.5 %collective-permute-start.8 = (f32[2,2,1,32,128]{4,2,3,0,1:T(1,128)S(1)}, f32[2,2,1,32,128]{4,2,3,0,1:T(1,128)S(1)}, u32[]{:S(2)}, u32[]{:S(2)}) collective-permute-start(f32[2,2,1,32,128]{4,2,3,0,1:T(1,128)S(1)} %get-tuple-element.54), channel_id=1, source_target_pairs={{8,0},{16,8},{24,16},{9,1},{17,9},{25,17},{10,2},{18,10},{26,18},{... | collective-permute-start | bytes 196616 | tf_op jit(solution)/shard_map/ppermute | solution.py:23
  59.9 7.3 %collective-permute-start.9 = (f32[2,2,1,32,128]{4,2,3,0,1:T(1,128)S(1)}, f32[2,2,1,32,128]{4,2,3,0,1:T(1,128)S(1)}, u32[]{:S(2)}, u32[]{:S(2)}) collective-permute-start(f32[2,2,1,32,128]{4,2,3,0,1:T(1,128)S(1)} %get-tuple-element.53), channel_id=1, source_target_pairs={{0,8},{8,16},{16,24},{1,9},{9,17},{17,25},{2,10},{10,18},{18,26},{... | collective-permute-start | bytes 196616 | tf_op jit(solution)/shard_map/ppermute | solution.py:21
  67.2 6.7 %collective-permute-start.10 = (f32[2,2,34,1,128]{4,2,3,0,1:T(8,128)S(1)}, f32[2,2,34,1,128]{4,2,3,0,1:T(8,128)S(1)}, u32[]{:S(2)}, u32[]{:S(2)}) collective-permute-start(f32[2,2,34,1,128]{4,2,3,0,1:T(8,128)S(1)} %get-tuple-element.35), channel_id=1, source_target_pairs={{2,0},{4,2},{6,4},{3,1},{5,3},{7,5},{10,8},{12,10},{14,12},{11,9},... | collective-permute-start | bytes 208904 | tf_op jit(solution)/shard_map/ppermute | solution.py:23
  68.5 7.0 %collective-permute-start.11 = (f32[2,2,34,1,128]{4,2,3,0,1:T(8,128)S(1)}, f32[2,2,34,1,128]{4,2,3,0,1:T(8,128)S(1)}, u32[]{:S(2)}, u32[]{:S(2)}) collective-permute-start(f32[2,2,34,1,128]{4,2,3,0,1:T(8,128)S(1)} %get-tuple-element.36), channel_id=1, source_target_pairs={{0,2},{2,4},{4,6},{1,3},{3,5},{5,7},{8,10},{10,12},{12,14},{9,11},... | collective-permute-start | bytes 208904 | tf_op jit(solution)/shard_map/ppermute | solution.py:21
  128.9 34.3 %copy-start.1 = (f32[2,2,32,32,128]{4,2,3,0,1:T(8,128)}, f32[2,2,32,32,128]{4,2,3,0,1:T(8,128)S(1)}, u32[]{:S(2)}) copy-start(f32[2,2,32,32,128]{4,2,3,0,1:T(8,128)S(1)} %multiply_subtract_fusion) | copy-start | bytes 6291460
  129.0 6.8 %collective-permute-start.12 = (f32[2,2,1,32,128]{4,2,3,0,1:T(1,128)S(1)}, f32[2,2,1,32,128]{4,2,3,0,1:T(1,128)S(1)}, u32[]{:S(2)}, u32[]{:S(2)}) collective-permute-start(f32[2,2,1,32,128]{4,2,3,0,1:T(1,128)S(1)} %get-tuple-element.52), channel_id=1, source_target_pairs={{8,0},{16,8},{24,16},{9,1},{17,9},{25,17},{10,2},{18,10},{26,18},{... | collective-permute-start | bytes 196616 | tf_op jit(solution)/shard_map/ppermute | solution.py:23
  130.3 6.4 %collective-permute-start.13 = (f32[2,2,1,32,128]{4,2,3,0,1:T(1,128)S(1)}, f32[2,2,1,32,128]{4,2,3,0,1:T(1,128)S(1)}, u32[]{:S(2)}, u32[]{:S(2)}) collective-permute-start(f32[2,2,1,32,128]{4,2,3,0,1:T(1,128)S(1)} %get-tuple-element.51), channel_id=1, source_target_pairs={{0,8},{8,16},{16,24},{1,9},{9,17},{17,25},{2,10},{10,18},{18,26},{... | collective-permute-start | bytes 196616 | tf_op jit(solution)/shard_map/ppermute | solution.py:21
  136.8 6.3 %collective-permute-start.14 = (f32[2,2,34,1,128]{4,2,3,0,1:T(8,128)S(1)}, f32[2,2,34,1,128]{4,2,3,0,1:T(8,128)S(1)}, u32[]{:S(2)}, u32[]{:S(2)}) collective-permute-start(f32[2,2,34,1,128]{4,2,3,0,1:T(8,128)S(1)} %get-tuple-element.33), channel_id=1, source_target_pairs={{2,0},{4,2},{6,4},{3,1},{5,3},{7,5},{10,8},{12,10},{14,12},{11,9},... | collective-permute-start | bytes 208904 | tf_op jit(solution)/shard_map/ppermute | solution.py:23
  138.1 6.6 %collective-permute-start.15 = (f32[2,2,34,1,128]{4,2,3,0,1:T(8,128)S(1)}, f32[2,2,34,1,128]{4,2,3,0,1:T(8,128)S(1)}, u32[]{:S(2)}, u32[]{:S(2)}) collective-permute-start(f32[2,2,34,1,128]{4,2,3,0,1:T(8,128)S(1)} %get-tuple-element.34), channel_id=1, source_target_pairs={{0,2},{2,4},{4,6},{1,3},{3,5},{5,7},{8,10},{10,12},{12,14},{9,11},... | collective-permute-start | bytes 208904 | tf_op jit(solution)/shard_map/ppermute | solution.py:21
  146.8 7.0 %collective-permute-start.16 = (f32[2,2,1,32,128]{4,2,3,0,1:T(1,128)S(1)}, f32[2,2,1,32,128]{4,2,3,0,1:T(1,128)S(1)}, u32[]{:S(2)}, u32[]{:S(2)}) collective-permute-start(f32[2,2,1,32,128]{4,2,3,0,1:T(1,128)S(1)} %get-tuple-element.48), channel_id=1, source_target_pairs={{8,0},{16,8},{24,16},{9,1},{17,9},{25,17},{10,2},{18,10},{26,18},{... | collective-permute-start | bytes 196616 | tf_op jit(solution)/shard_map/ppermute | solution.py:23
  148.1 6.9 %collective-permute-start.17 = (f32[2,2,1,32,128]{4,2,3,0,1:T(1,128)S(1)}, f32[2,2,1,32,128]{4,2,3,0,1:T(1,128)S(1)}, u32[]{:S(2)}, u32[]{:S(2)}) collective-permute-start(f32[2,2,1,32,128]{4,2,3,0,1:T(1,128)S(1)} %get-tuple-element.47), channel_id=1, source_target_pairs={{0,8},{8,16},{16,24},{1,9},{9,17},{17,25},{2,10},{10,18},{18,26},{... | collective-permute-start | bytes 196616 | tf_op jit(solution)/shard_map/ppermute | solution.py:21
  155.0 6.7 %collective-permute-start.18 = (f32[2,2,34,1,128]{4,2,3,0,1:T(8,128)S(1)}, f32[2,2,34,1,128]{4,2,3,0,1:T(8,128)S(1)}, u32[]{:S(2)}, u32[]{:S(2)}) collective-permute-start(f32[2,2,34,1,128]{4,2,3,0,1:T(8,128)S(1)} %get-tuple-element.31), channel_id=1, source_target_pairs={{2,0},{4,2},{6,4},{3,1},{5,3},{7,5},{10,8},{12,10},{14,12},{11,9},... | collective-permute-start | bytes 208904 | tf_op jit(solution)/shard_map/ppermute | solution.py:23
  156.3 7.0 %collective-permute-start.19 = (f32[2,2,34,1,128]{4,2,3,0,1:T(8,128)S(1)}, f32[2,2,34,1,128]{4,2,3,0,1:T(8,128)S(1)}, u32[]{:S(2)}, u32[]{:S(2)}) collective-permute-start(f32[2,2,34,1,128]{4,2,3,0,1:T(8,128)S(1)} %get-tuple-element.32), channel_id=1, source_target_pairs={{0,2},{2,4},{4,6},{1,3},{3,5},{5,7},{8,10},{10,12},{12,14},{9,11},... | collective-permute-start | bytes 208904 | tf_op jit(solution)/shard_map/ppermute | solution.py:21
  211.7 19.9 %copy-start = (f32[2,2,32,32,128]{4,2,3,0,1:T(8,128)}, f32[2,2,32,32,128]{4,2,3,0,1:T(8,128)S(1)}, u32[]{:S(2)}) copy-start(f32[2,2,32,32,128]{4,2,3,0,1:T(8,128)S(1)} %multiply_add_fusion) | copy-start | bytes 6291460
  213.0 6.2 %collective-permute-start.20 = (f32[2,2,1,32,128]{4,2,3,0,1:T(1,128)S(1)}, f32[2,2,1,32,128]{4,2,3,0,1:T(1,128)S(1)}, u32[]{:S(2)}, u32[]{:S(2)}) collective-permute-start(f32[2,2,1,32,128]{4,2,3,0,1:T(1,128)S(1)} %get-tuple-element.44), channel_id=1, source_target_pairs={{8,0},{16,8},{24,16},{9,1},{17,9},{25,17},{10,2},{18,10},{26,18},{... | collective-permute-start | bytes 196616 | tf_op jit(solution)/shard_map/ppermute | solution.py:23
  214.3 6.4 %collective-permute-start.21 = (f32[2,2,1,32,128]{4,2,3,0,1:T(1,128)S(1)}, f32[2,2,1,32,128]{4,2,3,0,1:T(1,128)S(1)}, u32[]{:S(2)}, u32[]{:S(2)}) collective-permute-start(f32[2,2,1,32,128]{4,2,3,0,1:T(1,128)S(1)} %get-tuple-element.43), channel_id=1, source_target_pairs={{0,8},{8,16},{16,24},{1,9},{9,17},{17,25},{2,10},{10,18},{18,26},{... | collective-permute-start | bytes 196616 | tf_op jit(solution)/shard_map/ppermute | solution.py:21
  220.7 6.4 %collective-permute-start.22 = (f32[2,2,34,1,128]{4,2,3,1,0:T(8,128)S(1)}, f32[2,2,34,1,128]{4,2,3,1,0:T(8,128)S(1)}, u32[]{:S(2)}, u32[]{:S(2)}) collective-permute-start(f32[2,2,34,1,128]{4,2,3,1,0:T(8,128)S(1)} %get-tuple-element.29), channel_id=1, source_target_pairs={{2,0},{4,2},{6,4},{3,1},{5,3},{7,5},{10,8},{12,10},{14,12},{11,9},... | collective-permute-start | bytes 208904 | tf_op jit(solution)/shard_map/ppermute | solution.py:23
  222.0 6.7 %copy-start.3 = (f32[2,2,32,32,128]{4,3,2,1,0:T(8,128)S(1)}, f32[2,2,32,32,128]{4,3,2,1,0:T(8,128)}, u32[]{:S(2)}) copy-start(f32[2,2,32,32,128]{4,3,2,1,0:T(8,128)} %param.7) | copy-start | bytes 6291460
  222.0 6.7 %collective-permute-start.23 = (f32[2,2,34,1,128]{4,2,3,1,0:T(8,128)S(1)}, f32[2,2,34,1,128]{4,2,3,1,0:T(8,128)S(1)}, u32[]{:S(2)}, u32[]{:S(2)}) collective-permute-start(f32[2,2,34,1,128]{4,2,3,1,0:T(8,128)S(1)} %get-tuple-element.30), channel_id=1, source_target_pairs={{0,2},{2,4},{4,6},{1,3},{3,5},{5,7},{8,10},{10,12},{12,14},{9,11},... | collective-permute-start | bytes 208904 | tf_op jit(solution)/shard_map/ppermute | solution.py:21
Sparse Core Ops, SparseCore 0:
  233.2 19.1 all-reduce.15
where the time goes:
time: 262 us; the launch traced here: 261 us
  blocking collectives  90.3 us (34%)
  starting transfers between devices  74.7 us (29%)
  other arithmetic  32.8 us (13%)
  waiting for transfers between devices  30.6 us (12%)
  local copies, waits for them, and re-layouts  18.5 us (7%)
  between operations  14.6 us (6%)
    psum x2, blocking collectives, two_products(): return lax.psum((inner(resid, resid), inner(resid, image)), ('gx', 'gy'))  90.3 us
    ppermute x12, starting transfers between devices, padded_2(): lax.ppermute(tail, axis, [(i, (i + 1) % count) for i in range(ends)])  59.2 us
    ppermute x12, starting transfers between devices, padded_2(): lax.ppermute(head, axis, [((i + 1) % count, i) for i in range(ends)])  15.5 us
    psum x1, waiting for transfers between devices, on_device(): gradient = lax.psum(local_terms, 'af')  15.2 us
    ppermute x12, waiting for transfers between devices, padded_2(): lax.ppermute(tail, axis, [(i, (i + 1) % count) for i in range(ends)])  14.9 us
    unnamed x20, local copies, waits for them, and re-layouts  10.4 us
    add x1, other arithmetic, on_device(): rhs = adjoint(source) + weights * observed[:, :, :, :, None]  7.37 us
    reduce_sum x2, other arithmetic, inner(): return jnp.sum(left * right, axis=(1, 2, 3, 4))  7.18 us
  transfers between devices with their start and end apart: 25, of which 15 were waited for; matrix products, arithmetic and copies ran while one was open for 7% of the time, Pallas kernels for 0%

commit v1 on v0

v1 whole, which is shorter than its diff:
```python
import functools

import jax
import jax.numpy as jnp
from jax import lax
from jax.experimental import pallas as pl
from jax.experimental.pallas import tpu as pltpu
from jax.sharding import PartitionSpec as P

ITERS = 2
attenuation = 0.2
penalty = 4.0

HALO = 2 * ITERS
INNER = HALO - 1
F32 = jnp.float32
ANY = pl.BlockSpec(memory_space=pl.ANY)
VMEM = pl.BlockSpec(memory_space=pltpu.VMEM)
SMEM = pl.BlockSpec(memory_space=pltpu.SMEM)
MIB = 1 << 20


def params(mib):
    return pltpu.CompilerParams(vmem_limit_bytes=mib * MIB)


def parity(axis):
    return lax.rem(lax.axis_index(axis), 2) == 0


def run_all(copies):
    for copy in copies:
        copy.start()
    for copy in copies:
        copy.wait()


def pack_kernel(source, model, observed, depth, xe, xo, ye, yo, table, slab, sem):
    freqs, _, nx, ny, nz = source.shape
    fields = 2 * freqs
    for f in range(freqs):
        for p in range(2):
            table[2 * f + p, :, 0:nx] = observed[f, p].T
    table[fields, :, 0:nx] = depth[...].astype(F32).T
    lane = lax.broadcasted_iota(jnp.int32, (ny, nz), 1)
    even_x, even_y = parity("gx"), parity("gy")
    copies = []
    count = iter(range(64))

    def copy(src, dst):
        copies.append(pltpu.make_async_copy(src, dst, sem.at[next(count)]))
        copies[-1].start()

    for side, (xb, yb) in enumerate(((xe, ye), (xo, yo))):
        last_x = even_x if side == 0 else jnp.logical_not(even_x)
        last_y = even_y if side == 0 else jnp.logical_not(even_y)
        at_x = jnp.where(last_x, nx - HALO, 0)
        at_m = jnp.where(last_x, nx - INNER, 0)
        at_y = pl.multiple_of(jnp.where(last_y, ny - HALO, 0), HALO)
        for f in range(freqs):
            for p in range(2):
                k = 2 * f + p
                copy(source.at[f, p, pl.ds(at_x, HALO)], xb.at[pl.ds(k * HALO, HALO)])
                copy(
                    source.at[f, p, :, pl.ds(at_y, HALO), :],
                    yb.at[pl.ds(k * nx, nx)],
                )
        copy(model.at[pl.ds(at_m, INNER)], xb.at[pl.ds(fields * HALO, INNER)])
        copy(model.at[:, pl.ds(at_y, HALO), :], yb.at[pl.ds(fields * nx, nx)])
        copy(
            table.at[:, pl.ds(at_y, HALO), :],
            yb.at[pl.ds((fields + 1) * nx, fields + 1)],
        )
        lanes = jnp.zeros((ny, nz), F32)
        for k in range(fields + 1):
            inside = (lane >= 8 * k) & (lane < 8 * k + INNER)
            head = pltpu.roll(table[k], 8 * k, axis=1)
            tail = pltpu.roll(table[k], (8 * k - (nx - INNER)) % nz, axis=1)
            lanes = jnp.where(inside, jnp.where(last_x, tail, head), lanes)
        slab[side, 0] = lanes
        copy(slab.at[side], xb.at[pl.ds(fields * HALO + INNER, 1)])
    for c in copies:
        c.wait()


def pack(source, model, observed, depth):
    freqs, _, nx, ny, nz = source.shape
    fields = 2 * freqs
    xs = jax.ShapeDtypeStruct((fields * HALO + INNER + 1, ny, nz), F32)
    ys = jax.ShapeDtypeStruct(((fields + 1) * nx + fields + 1, HALO, nz), F32)
    return pl.pallas_call(
        pack_kernel,
        out_shape=(xs, xs, ys, ys, jax.ShapeDtypeStruct((fields + 1, ny, nz), F32)),
        in_specs=[ANY, ANY, VMEM, VMEM],
        out_specs=(ANY, ANY, ANY, ANY, VMEM),
        scratch_shapes=[
            pltpu.VMEM((2, 1, ny, nz), F32),
            pltpu.SemaphoreType.DMA((64,)),
        ],
        compiler_params=params(8),
        name="pack",
    )(source, model, observed, depth)


def corner_kernel(fields, nx, ye, yo, ce, co, sem):
    even_x = parity("gx")
    copies = []
    count = iter(range(64))
    size = (fields + 1) * HALO + fields + 1
    for side, cb in enumerate((ce, co)):
        last_x = even_x if side == 0 else jnp.logical_not(even_x)
        at_x = jnp.where(last_x, nx - HALO, 0)
        for half, yb in enumerate((ye, yo)):
            base = half * size
            for k in range(fields + 1):
                copies.append(
                    pltpu.make_async_copy(
                        yb.at[pl.ds(k * nx + at_x, HALO)],
                        cb.at[pl.ds(base + k * HALO, HALO)],
                        sem.at[next(count)],
                    )
                )
            copies.append(
                pltpu.make_async_copy(
                    yb.at[pl.ds((fields + 1) * nx, fields + 1)],
                    cb.at[pl.ds(base + (fields + 1) * HALO, fields + 1)],
                    sem.at[next(count)],
                )
            )
    run_all(copies)


def corners(fields, nx, ye, yo):
    size = (fields + 1) * HALO + fields + 1
    out = jax.ShapeDtypeStruct((2 * size, HALO, ye.shape[2]), F32)
    return pl.pallas_call(
        functools.partial(corner_kernel, fields, nx),
        out_shape=(out, out),
        in_specs=[ANY, ANY],
        out_specs=(ANY, ANY),
        scratch_shapes=[pltpu.SemaphoreType.DMA((64,))],
        compiler_params=params(4),
        name="corners",
    )(ye, yo)


class Sweep:
    def __init__(self, nx, ny, nz, freqs, freq_sq, refs):
        self.nx, self.ny, self.nz, self.freqs = nx, ny, nz, freqs
        self.xe, self.ye = nx + 2 * HALO, ny + 2 * HALO
        self.tiles = self.ye // 8
        self.freq_sq = freq_sq
        self.s, self.v0, self.u0, self.v1, self.u1, self.cr, self.ci, self.w = refs
        lane = lax.broadcasted_iota(jnp.int32, (8, nz), 1)
        self.first = lane == 0
        self.last = lane == nz - 1
        self.depths = lane.astype(F32)
        sub = lax.broadcasted_iota(jnp.int32, (8, nz), 0)
        self.sub = sub
        has_left = lax.axis_index("gy") > 0
        has_right = lax.axis_index("gy") < lax.axis_size("gy") - 1
        left = jnp.where(has_left, 1.0, 0.0)
        right = jnp.where(has_right, 1.0, 0.0)
        self.inside = []
        for t in range(self.tiles):
            y = sub * self.tiles + t
            self.inside.append(
                jnp.where(y < ny, 1.0, jnp.where(y < ny + HALO, right, left))
            )
        self.groups = {}
        for t in range(self.tiles):
            owned = -((t - ny) // self.tiles)
            self.groups.setdefault(owned, []).append(t)

    def rows(self, ref, f, p, i):
        return [
            ref[f, p, i, pl.ds(t, 8, stride=self.tiles), :] for t in range(self.tiles)
        ]

    def put(self, ref, f, p, i, values):
        for t in range(self.tiles):
            ref[f, p, i, pl.ds(t, 8, stride=self.tiles), :] = values[t]

    def around(self, ref, f, p, i, lo, hi):
        mid = self.rows(ref, f, p, i)
        below = self.rows(ref, f, p, lo)
        above = self.rows(ref, f, p, hi)
        total = []
        n = self.tiles
        for t in range(n):
            up = mid[t + 1] if t + 1 < n else pltpu.roll(mid[0], 7, axis=0)
            down = mid[t - 1] if t else pltpu.roll(mid[n - 1], 1, axis=0)
            left = jnp.where(self.first, 0.0, pltpu.roll(mid[t], 1, axis=1))
            right = jnp.where(self.last, 0.0, pltpu.roll(mid[t], self.nz - 1, axis=1))
            total.append(((below[t] + above[t]) + (up + down)) + (left + right))
        return mid, total

    def coef(self, f, i):
        return (
            [self.cr[f, i, t] for t in range(self.tiles)],
            [self.ci[f, i, t] for t in range(self.tiles)],
        )

    def apply(self, src, f, i, lo, hi, sign, coef):
        cr, ci = coef
        re, nre = self.around(src, f, 0, i, lo, hi)
        im, nim = self.around(src, f, 1, i, lo, hi)
        out_re, out_im = [], []
        for t in range(self.tiles):
            if sign > 0:
                out_re.append(cr[t] * re[t] - ci[t] * im[t] - nre[t])
                out_im.append(cr[t] * im[t] + ci[t] * re[t] - nim[t])
            else:
                out_re.append(cr[t] * re[t] + ci[t] * im[t] - nre[t])
                out_im.append(cr[t] * im[t] - ci[t] * re[t] - nim[t])
        return re, im, out_re, out_im

    def masks(self, scale):
        if scale is None:
            return self.inside
        return [m * scale for m in self.inside]

    def squares(self, re, im, weight=None):
        out = []
        for t in range(self.tiles):
            value = re[t] * re[t] + im[t] * im[t]
            out.append(value if weight is None else weight[t] * value)
        return out

    def gather(self, acc, values):
        return tuple(
            a + functools.reduce(jnp.add, [values[t] for t in ts])
            for a, ts in zip(acc, self.groups.values())
        )

    def zero(self):
        return tuple(jnp.zeros((8, self.nz), F32) for _ in self.groups)

    def total(self, acc):
        return functools.reduce(
            jnp.add,
            [jnp.where(self.sub < n, a, 0.0) for a, n in zip(acc, self.groups)],
        )

    def prepare(self, i, model_rows, column):
        depth = column(2 * self.freqs)
        weight, terms = [], []
        coefs = []
        for t in range(self.tiles):
            weight.append(jnp.where(self.depths == depth[t], penalty, 0.0))
            self.w[i, t] = weight[t]
        for f in range(self.freqs):
            cr, ci = [], []
            for t in range(self.tiles):
                scaled = self.freq_sq[f] * model_rows[t]
                cr.append(6.0 - scaled)
                ci.append(attenuation * scaled)
                self.cr[f, i, t] = cr[t]
                self.ci[f, i, t] = ci[t]
            coefs.append((cr, ci))
            parts = []
            for p in range(2):
                seen = column(2 * f + p)
                parts.append([weight[t] * seen[t] for t in range(self.tiles)])
            terms.append(parts)
        return coefs, terms

    def weights(self, i):
        return [self.w[i, t] for t in range(self.tiles)]

    def step_v0(self, f, i, lo, hi, coef, terms, scale=None):
        _, _, re, im = self.apply(self.s, f, i, lo, hi, -1, coef)
        mask = self.masks(scale)
        re = [(re[t] + terms[0][t]) * mask[t] for t in range(self.tiles)]
        im = [(im[t] + terms[1][t]) * mask[t] for t in range(self.tiles)]
        self.put(self.v0, f, 0, i, re)
        self.put(self.v0, f, 1, i, im)
        return self.squares(re, im)

    def step_u0(self, f, i, lo, hi, scale=None, own=True):
        vr, vi, re, im = self.apply(self.v0, f, i, lo, hi, 1, self.coef(f, i))
        mask = self.masks(scale)
        re = [re[t] * mask[t] for t in range(self.tiles)]
        im = [im[t] * mask[t] for t in range(self.tiles)]
        self.put(self.u0, f, 0, i, re)
        self.put(self.u0, f, 1, i, im)
        if not own:
            return None
        a = self.squares(re, im)
        b = self.squares(vr, vi, self.weights(i))
        return [a[t] + b[t] for t in range(self.tiles)]

    def step_v1(self, f, i, lo, hi, scale=None, own=True):
        _, _, re, im = self.apply(self.u0, f, i, lo, hi, -1, self.coef(f, i))
        mask = self.masks(scale)
        weight = self.weights(i)
        vr = self.rows(self.v0, f, 0, i)
        vi = self.rows(self.v0, f, 1, i)
        re = [(re[t] + weight[t] * vr[t]) * mask[t] for t in range(self.tiles)]
        im = [(im[t] + weight[t] * vi[t]) * mask[t] for t in range(self.tiles)]
        self.put(self.v1, f, 0, i, re)
        self.put(self.v1, f, 1, i, im)
        return self.squares(re, im) if own else None

    def step_u1(self, f, i, lo, hi):
        vr, vi, re, im = self.apply(self.v1, f, i, lo, hi, 1, self.coef(f, i))
        self.put(self.u1, f, 0, i, re)
        self.put(self.u1, f, 1, i, im)
        a = self.squares(re, im)
        b = self.squares(vr, vi, self.weights(i))
        return [a[t] + b[t] for t in range(self.tiles)]


def inner_kernel(
    freq_sq, source, model, table, ye, yo, *refs
):
    state, moments, (cells, aux, sem) = refs[:8], refs[8], refs[9:]
    freqs, _, nx, ny, nz = source.shape
    fields = 2 * freqs
    sweep = Sweep(nx, ny, nz, freqs, freq_sq, state)
    s = sweep.s
    even_y = parity("gy")
    copies = []
    count = iter(range(64))

    def copy(src, dst):
        copies.append(pltpu.make_async_copy(src, dst, sem.at[next(count)]))

    at_e = pl.multiple_of(jnp.where(even_y, ny, ny + HALO), HALO)
    at_o = pl.multiple_of(jnp.where(even_y, ny + HALO, ny), HALO)
    copy(model, cells.at[:, pl.ds(0, ny), :])
    copy(table, aux.at[:, pl.ds(0, ny), :])
    for yb, at in ((ye, at_e), (yo, at_o)):
        copy(yb.at[pl.ds(fields * nx, nx)], cells.at[:, pl.ds(at, HALO), :])
        copy(yb.at[pl.ds((fields + 1) * nx, fields + 1)], aux.at[:, pl.ds(at, HALO), :])
    for k in range(fields):
        f, p = k // 2, k % 2
        copy(source.at[f, p], s.at[f, p, pl.ds(0, nx), pl.ds(0, ny), :])
        for yb, at in ((ye, at_e), (yo, at_o)):
            copy(
                yb.at[pl.ds(k * nx, nx)],
                s.at[f, p, pl.ds(0, nx), pl.ds(at, HALO), :],
            )
    run_all(copies)

    tiles = sweep.tiles

    def prepare(i):
        def column(k):
            pick = jnp.full((8, nz), i, jnp.int32)
            return [
                jnp.take_along_axis(
                    aux[k, pl.ds(t, 8, stride=tiles), :], pick, axis=1
                )
                for t in range(tiles)
            ]

        rows = [cells[i, pl.ds(t, 8, stride=tiles), :] for t in range(tiles)]
        return sweep.prepare(i, rows, column)

    for i in (0, nx - 1):
        _, terms = prepare(i)
        for f in range(freqs):
            for p in range(2):
                sweep.put(sweep.v0, f, p, i, terms[f][p])

    def step(j, acc, active):
        acc = [list(a) for a in acc]
        if 3 in active:
            i = j - 6
            for f in range(freqs):
                acc[f][3] = sweep.gather(acc[f][3], sweep.step_u1(f, i, i - 1, i + 1))
        if 2 in active:
            i = j - 4
            for f in range(freqs):
                acc[f][2] = sweep.gather(acc[f][2], sweep.step_v1(f, i, i - 1, i + 1))
        if 1 in active:
            i = j - 2
            for f in range(freqs):
                acc[f][1] = sweep.gather(acc[f][1], sweep.step_u0(f, i, i - 1, i + 1))
        if 0 in active:
            coefs, terms = prepare(j)
            for f in range(freqs):
                acc[f][0] = sweep.gather(
                    acc[f][0], sweep.step_v0(f, j, j - 1, j + 1, coefs[f], terms[f])
                )
        return tuple(tuple(a) for a in acc)

    spans = [(1 + 3 * k, nx - 1 + k) for k in range(4)]
    edges = sorted({e for span in spans for e in span})
    acc = tuple(tuple(sweep.zero() for _ in range(4)) for _ in range(freqs))
    for lo, hi in zip(edges[:-1], edges[1:]):
        active = [k for k, (a, b) in enumerate(spans) if a <= lo and hi <= b]
        acc = lax.fori_loop(lo, hi, functools.partial(step, active=active), acc)
    for f in range(freqs):
        for m in range(4):
            moments[f, m] = sweep.total(acc[f][m])


def state_shapes(freqs, nx, ny, nz):
    xe, ye = nx + 2 * HALO, ny + 2 * HALO
    field = pltpu.VMEM((freqs, 2, xe, ye, nz), F32)
    coef = pltpu.VMEM((freqs, xe, ye // 8, 8, nz), F32)
    weight = pltpu.VMEM((xe, ye // 8, 8, nz), F32)
    return (field,) * 5 + (coef, coef, weight)


def inner_part(freq_sq, source, model, table, ye, yo):
    freqs, _, nx, ny, nz = source.shape
    return pl.pallas_call(
        inner_kernel,
        out_shape=state_shapes(freqs, nx, ny, nz)
        + (pltpu.VMEM((freqs, 4, 8, nz), F32),),
        in_specs=[SMEM, ANY, ANY, VMEM, ANY, ANY],
        scratch_shapes=[
            pltpu.VMEM((nx, ny + 2 * HALO, nz), F32),
            pltpu.VMEM((2 * freqs + 1, ny + 2 * HALO, nz), F32),
            pltpu.SemaphoreType.DMA((64,)),
        ],
        compiler_params=params(8),
        name="inner_part",
    )(freq_sq, source, model, table, ye, yo)


def edge_kernel(peers, nx, ny, freq_sq, xe, xo, ce, co, *refs):
    moments, part = refs[8], refs[17]
    state, (cells, aux, near, sem) = refs[9:17], refs[18:]
    freqs, _, _, _, nz = state[0].shape
    fields = 2 * freqs
    sweep = Sweep(nx, ny, nz, freqs, freq_sq, state)
    s, tiles = sweep.s, sweep.tiles
    even_x, even_y = parity("gx"), parity("gy")
    at_e = pl.multiple_of(jnp.where(even_y, ny, ny + HALO), HALO)
    at_o = pl.multiple_of(jnp.where(even_y, ny + HALO, ny), HALO)
    low_e = pl.multiple_of(jnp.where(even_y, 0, HALO), HALO)
    low_o = pl.multiple_of(jnp.where(even_y, HALO, 0), HALO)
    size = (fields + 1) * HALO + fields + 1
    copies = []
    count = iter(range(128))

    def copy(src, dst):
        copies.append(pltpu.make_async_copy(src, dst, sem.at[next(count)]))

    for side, (xb, cb) in enumerate(((xe, ce), (xo, co))):
        above = even_x if side == 0 else jnp.logical_not(even_x)
        slot = jnp.where(above, nx, nx + HALO)
        skip = jnp.where(above, 0, 1)
        half = jnp.where(above, 0, 1)
        for k in range(fields):
            f, p = k // 2, k % 2
            copy(
                xb.at[pl.ds(k * HALO, HALO)],
                s.at[f, p, pl.ds(slot, HALO), pl.ds(0, ny), :],
            )
            for h, at in enumerate((at_e, at_o)):
                copy(
                    cb.at[pl.ds(h * size + k * HALO, HALO)],
                    s.at[f, p, pl.ds(slot, HALO), pl.ds(at, HALO), :],
                )
        copy(
            xb.at[pl.ds(fields * HALO, INNER)],
            cells.at[half, pl.ds(0, INNER), pl.ds(0, ny), :],
        )
        copy(xb.at[fields * HALO + INNER], aux.at[half, pl.ds(0, ny), :])
        for h, (at, low) in enumerate(((at_e, low_e), (at_o, low_o))):
            copy(
                cb.at[pl.ds(h * size + fields * HALO + skip, INNER)],
                cells.at[half, pl.ds(0, INNER), pl.ds(at, HALO), :],
            )
            copy(
                cb.at[pl.ds(h * size + (fields + 1) * HALO, fields + 1)],
                near.at[half, :, pl.ds(low, HALO), :],
            )
    run_all(copies)

    lane = lax.broadcasted_iota(jnp.int32, (8, nz), 1)
    for half in range(2):
        base = 0 if half == 0 else nx - INNER
        lanes = jnp.zeros((8, nz), F32)
        for k in range(fields + 1):
            inside = (lane >= 8 * k) & (lane < 8 * k + INNER)
            moved = pltpu.roll(near[half, k], (8 * k - base) % nz, axis=1)
            lanes = jnp.where(inside, moved, lanes)
        aux[half, ny:, :] = lanes

    for half in range(2):
        for layer in range(INNER):
            i = nx + layer if half == 0 else nx + HALO + 1 + layer

            def column(k):
                pick = jnp.full((8, nz), 8 * k + layer, jnp.int32)
                return [
                    jnp.take_along_axis(
                        aux[half, pl.ds(t, 8, stride=tiles), :], pick, axis=1
                    )
                    for t in range(tiles)
                ]

            rows = [
                cells[half, layer, pl.ds(t, 8, stride=tiles), :] for t in range(tiles)
            ]
            _, terms = sweep.prepare(i, rows, column)
            for f in range(freqs):
                for p in range(2):
                    sweep.put(sweep.v0, f, p, i, terms[f][p])

    left = jnp.where(lax.axis_index("gx") > 0, 1.0, 0.0)
    right = jnp.where(lax.axis_index("gx") < lax.axis_size("gx") - 1, 1.0, 0.0)
    wrap = sweep.xe

    def place(x):
        return x % wrap, (x - 1) % wrap, (x + 1) % wrap

    def scale(x):
        return None if 0 <= x < nx else (left if x < 0 else right)

    acc = [[sweep.zero() for _ in range(4)] for _ in range(freqs)]
    for stage in range(4):
        for k in range(HALO):
            for x in (k - INNER + stage, nx - 1 - stage + k):
                i, lo, hi = place(x)
                own = 0 <= x < nx
                for f in range(freqs):
                    if stage == 0:
                        terms = [sweep.rows(sweep.v0, f, p, i) for p in range(2)]
                        got = sweep.step_v0(
                            f, i, lo, hi, sweep.coef(f, i), terms, scale(x)
                        )
                    elif stage == 1:
                        got = sweep.step_u0(f, i, lo, hi, scale(x), own)
                    elif stage == 2:
                        got = sweep.step_v1(f, i, lo, hi, scale(x), own)
                    else:
                        got = sweep.step_u1(f, i, lo, hi)
                    if own:
                        acc[f][stage] = sweep.gather(acc[f][stage], got)

    rows = []
    for f in range(freqs):
        for m in range(4):
            both = sweep.total(acc[f][m]) + moments[f, m]
            rows.append(jnp.sum(both, axis=0, keepdims=True))
    sums = jnp.sum(jnp.concatenate(rows, axis=0), axis=1, keepdims=True)
    sums = jnp.broadcast_to(sums, (4 * freqs, nz))
    for peer in range(peers):
        part[peer] = sums


def edge_part(peers, nx, ny, freq_sq, xe, xo, ce, co, state, moments):
    freqs, _, _, _, nz = state[0].shape
    outs = state_shapes(freqs, nx, ny, nz)
    return pl.pallas_call(
        functools.partial(edge_kernel, peers, nx, ny),
        out_shape=outs + (jax.ShapeDtypeStruct((peers, 4 * freqs, nz), F32),),
        in_specs=[SMEM] + [ANY] * 4 + [VMEM] * 9,
        input_output_aliases={5 + k: k for k in range(8)},
        scratch_shapes=[
            pltpu.VMEM((2, INNER, ny + 2 * HALO, nz), F32),
            pltpu.VMEM((2, ny + 2 * HALO, nz), F32),
            pltpu.VMEM((2, 2 * freqs + 1, 2 * HALO, nz), F32),
            pltpu.SemaphoreType.DMA((128,)),
        ],
        compiler_params=params(8),
        name="edge_part",
    )(freq_sq, xe, xo, ce, co, *state, moments)


def steps(sums, f):
    total = jnp.sum(sums[...], axis=0)
    shape = (8, total.shape[1])
    m0, m1, m2, m3 = (
        jnp.broadcast_to(total[4 * f + k : 4 * f + k + 1, :], shape) for k in range(4)
    )
    first = m0 / m1
    new = first * (first * m2 - m1)
    product = m1 - first * (2.0 * m2 - first * m3)
    ratio = new / m0
    second = new / (product - ratio * new / first)
    return first + second * (1.0 + ratio), -first * second


def gradient_kernel(nx, ny, freq_sq, sums, s, v0, u0, v1, u1, out):
    freqs = s.shape[0]
    weights = [steps(sums, f) for f in range(freqs)]

    def row(x, _):
        for y in range(0, ny, 8):
            at = pl.ds(y, 8)
            total = None
            for f in range(freqs):
                a, b = weights[f]
                wave_re = a * v0[f, 0, x, at, :] + b * v1[f, 0, x, at, :]
                wave_im = a * v0[f, 1, x, at, :] + b * v1[f, 1, x, at, :]
                miss_re = a * u0[f, 0, x, at, :] + b * u1[f, 0, x, at, :]
                miss_im = a * u0[f, 1, x, at, :] + b * u1[f, 1, x, at, :]
                miss_re = miss_re - s[f, 0, x, at, :]
                miss_im = miss_im - s[f, 1, x, at, :]
                left = (wave_re + attenuation * wave_im) * miss_re
                right = (wave_im - attenuation * wave_re) * miss_im
                term = -freq_sq[f] * (left + right)
                total = term if total is None else total + term
            out[x, at, :] = total
        return 0

    lax.fori_loop(0, nx, row, 0)


def wave_kernel(nx, ny, sums, v0, v1, out):
    step = pl.program_id(0)
    freqs = v0.shape[0]
    weights = [steps(sums, f) for f in range(freqs)]
    a, b = weights[0]
    f, p = step // 2, step % 2
    for k in range(1, freqs):
        a = jnp.where(f == k, weights[k][0], a)
        b = jnp.where(f == k, weights[k][1], b)

    def row(x, _):
        for y in range(0, ny, 8):
            at = pl.ds(y, 8)
            out[0, 0, x, at, :] = a * v0[f, p, x, at, :] + b * v1[f, p, x, at, :]
        return 0

    lax.fori_loop(0, nx, row, 0)


def results(nx, ny, freq_sq, sums, state):
    s, v0, u0, v1, u1 = state[:5]
    freqs, _, _, _, nz = s.shape
    gradient = pl.pallas_call(
        functools.partial(gradient_kernel, nx, ny),
        out_shape=jax.ShapeDtypeStruct((nx, ny, nz), F32),
        in_specs=[SMEM] + [VMEM] * 6,
        out_specs=VMEM,
        compiler_params=params(8),
        name="gradient_part",
    )(freq_sq, sums, s, v0, u0, v1, u1)
    wave = pl.pallas_call(
        functools.partial(wave_kernel, nx, ny),
        grid=(2 * freqs,),
        out_shape=jax.ShapeDtypeStruct((freqs, 2, nx, ny, nz), F32),
        in_specs=[VMEM] * 3,
        out_specs=pl.BlockSpec(
            (1, 1, nx, ny, nz), lambda k: (k // 2, k % 2, 0, 0, 0)
        ),
        compiler_params=params(8),
        name="wavefield",
    )(sums, v0, v1)
    return gradient, wave


def swap(cells, axis, odd):
    count = lax.axis_size(axis)
    pairs = []
    for i in range(odd, count - 1, 2):
        pairs += [(i, i + 1), (i + 1, i)]
    return lax.ppermute(cells, axis, pairs)


def on_device(model, freq_sq, source, observed, receiver_depth):
    nx, ny, nz = model.shape
    freqs = freq_sq.shape[0]
    xe, xo, ye, yo, table = pack(source, model, observed, receiver_depth)
    ye, yo = swap(ye, "gy", 0), swap(yo, "gy", 1)
    xe, xo = swap(xe, "gx", 0), swap(xo, "gx", 1)
    ce, co = corners(2 * freqs, nx, ye, yo)
    ce, co = swap(ce, "gx", 0), swap(co, "gx", 1)
    *state, moments = inner_part(freq_sq, source, model, table, ye, yo)
    peers = lax.axis_size("gx") * lax.axis_size("gy")
    *state, part = edge_part(peers, nx, ny, freq_sq, xe, xo, ce, co, state, moments)
    sums = lax.all_to_all(part, ("gx", "gy"), 0, 0)
    gradient, wave = results(nx, ny, freq_sq, sums, state)
    if lax.axis_size("af") == 2:
        gradient = gradient + lax.ppermute(gradient, "af", [(0, 1), (1, 0)])
    else:
        gradient = lax.psum(gradient, "af")
    return wave, gradient


def solution(mesh):
    in_specs = (
        P("gx", "gy", None),
        P("af"),
        P("af", None, "gx", "gy", None),
        P("af", None, "gx", "gy"),
        P("gx", "gy"),
    )
    out_specs = (P("af", None, "gx", "gy", None), P("gx", "gy", None))
    return jax.shard_map(
        on_device, mesh=mesh, in_specs=in_specs, out_specs=out_specs, check_vma=False
    )
```

time: 262 us -> 59.5 us (0.23)
  blocking collectives: 90.3 us -> 18 us
  starting transfers between devices: 74.7 us -> 8.43 us
  other arithmetic: 32.8 us -> 0.88 us
  waiting for transfers between devices: 30.6 us -> 5.03 us
  Pallas kernels: 0 us -> 21.8 us
  local copies, waits for them, and re-layouts: 18.5 us -> 4.18 us
  between operations: 14.6 us -> 0.76 us
    psum x2 -> x0, blocking collectives: 90.3 us -> none  [two_products(): return lax.psum((inner(resid, resid), inner(resid, image)), ('gx', 'gy'))]
    ppermute x24 -> x7, starting transfers between devices: 74.7 us -> 8.43 us  [the longest x6 8.36 us: swap(): return lax.ppermute(cells, axis, pairs)]
    pallas_call x0 -> x6, Pallas kernels: none -> 21.8 us  [the longest x1 10.5 us: inner_part(): pl.pallas_call(inner_kernel, out_shape=state_shapes(freqs, nx, ny, nz) +...]
    all_to_all x0 -> x1, blocking collectives: none -> 18 us  [on_device(): sums = lax.all_to_all(part, ('gx', 'gy'), 0, 0)]
    psum x1 -> x0, waiting for transfers between devices: 15.2 us -> none  [on_device(): gradient = lax.psum(local_terms, 'af')]
    sub x10 -> x0, other arithmetic: 13 us -> none  [the longest x2 4.14 us: forward(): return apply_coef(coef_real, coef_imag, field, 1.0) - beside(field)]
    ppermute x24 -> x7, waiting for transfers between devices: 15.3 us -> 5.03 us  [the longest x6 5.03 us: swap(): return lax.ppermute(cells, axis, pairs)]
    add x2 -> x1, other arithmetic: 9.55 us -> 0.88 us  [on_device(): gradient = gradient + lax.ppermute(gradient, 'af', [(0, 1), (1, 0)])]
  transfers between devices with their start and end apart: 25 -> 7, of which waited for: 15 -> 1; matrix products, arithmetic and copies ran while one was open for 7% -> 0% of each run, Pallas kernels for 0% -> 24%
where the time goes in v1:
time: 59.5 us; the launch traced here: 59.1 us
  Pallas kernels  21.8 us (37%)
  blocking collectives  18 us (30%)
  starting transfers between devices  8.43 us (14%)
  waiting for transfers between devices  5.03 us (8%)
  local copies, waits for them, and re-layouts  4.18 us (7%)
  other arithmetic  0.88 us (1%)
  between operations  0.76 us (1%)
    all_to_all x1, blocking collectives, on_device(): sums = lax.all_to_all(part, ('gx', 'gy'), 0, 0)  18 us
    pallas_call x1, Pallas kernels, inner_part(): pl.pallas_call(inner_kernel, out_shape=state_shapes(freqs, nx, ny, nz) +...  10.5 us
    ppermute x6, starting transfers between devices, swap(): return lax.ppermute(cells, axis, pairs)  8.36 us
    ppermute x6, waiting for transfers between devices, swap(): return lax.ppermute(cells, axis, pairs)  5.03 us
    pallas_call x1, Pallas kernels, edge_part(): pl.pallas_call(functools.partial(edge_kernel, peers, nx, ny), out_shape=o...  4.3 us
    unnamed x10, local copies, waits for them, and re-layouts  4.18 us
    pallas_call x1, Pallas kernels, results(): pl.pallas_call(functools.partial(wave_kernel, nx, ny), grid=(2 * freqs,),...  2.61 us
    pallas_call x1, Pallas kernels, pack(): pl.pallas_call(pack_kernel, out_shape=(xs, xs, ys, ys, jax.ShapeDtypeStru...  1.9 us
  transfers between devices with their start and end apart: 7, of which 1 were waited for; matrix products, arithmetic and copies ran while one was open for 0% of the time, Pallas kernels for 24%

profile of v1, /device:TPU:0, one launch (start us, length us, event | category | flops | bytes accessed | tf_op | source)
XLA Modules:
  0.0 59.1 jit_solution(18372089359030868107)
XLA Ops:
  0.6 0.0 copy-start
  0.6 1.6 %copy-done = f32[2,2,32,32,128]{4,3,2,1,0:T(8,128)S(1)} copy-done((f32[2,2,32,32,128]{4,3,2,1,0:T(8,128)S(1)}, f32[2,2,32,32,128]{4,3,2,1,0:T(8,128)}, u32[]{:S(2)}) %copy-start) | copy-done | bytes 2097176
  2.2 0.0 copy-start.1
  2.2 1.0 %copy-done.1 = f32[32,32,128]{2,1,0:T(8,128)S(1)} copy-done((f32[32,32,128]{2,1,0:T(8,128)S(1)}, f32[32,32,128]{2,1,0:T(8,128)}, u32[]{:S(2)}) %copy-start.1) | copy-done | bytes 524312
  3.3 0.0 copy-start.2
  3.3 0.8 %copy-done.2 = f32[2,2,32,32]{3,2,1,0:T(8,128)S(1)} copy-done((f32[2,2,32,32]{3,2,1,0:T(8,128)S(1)}, f32[2,2,32,32]{3,2,1,0:T(8,128)}, u32[]{:S(2)}) %copy-start.2) | copy-done | bytes 16408
  4.1 0.0 copy-start.3
  4.1 0.7 %copy-done.3 = s32[32,32]{1,0:T(8,128)S(1)} copy-done((s32[32,32]{1,0:T(8,128)S(1)}, s32[32,32]{1,0:T(8,128)}, u32[]{:S(2)}) %copy-start.3) | copy-done | bytes 4120
  4.8 0.0 copy-start.4
  4.8 1.9 %pack.1 = (f32[20,32,128]{2,1,0:T(8,128)S(1)}, f32[20,32,128]{2,1,0:T(8,128)S(1)}, f32[165,4,128]{2,1,0:T(4,128)S(1)}, f32[165,4,128]{2,1,0:T(4,128)S(1)}, f32[5,32,128]{2,1,0:T(8,128)S(1)}) custom-call(f32[2,2,32,32,128]{4,3,2,1,0:T(8,128)S(1)} %copy-done, f32[32,32,128]{2,1,0:T(8,128)S(1)} %copy-done.1, f32[2,2,32,32]{3,2,1,0:T(8,128)S(1)} %copy-done.2, ...), custom_call_target="tpu_custom_call" | custom-call | tf_op jit(solution)/shard_map/pack/pallas_call | solution.py:91
  6.7 3.1 %collective-permute-start.2 = (f32[165,4,128]{2,1,0:T(4,128)S(1)}, f32[165,4,128]{2,1,0:T(4,128)S(1)}, u32[]{:S(2)}, u32[]{:S(2)}) collective-permute-start(f32[165,4,128]{2,1,0:T(4,128)S(1)} %get-tuple-element.26), channel_id=1, source_target_pairs={{0,2},{2,0},{4,6},{6,4},{1,3},{3,1},{5,7},{7,5},{8,10},{10,8},{12,... | collective-permute-start | bytes 1013768 | tf_op jit(solution)/shard_map/ppermute | solution.py:657
  9.8 0.7 %collective-permute-start.3 = (f32[165,4,128]{2,1,0:T(4,128)S(1)}, f32[165,4,128]{2,1,0:T(4,128)S(1)}, u32[]{:S(2)}, u32[]{:S(2)}) collective-permute-start(f32[165,4,128]{2,1,0:T(4,128)S(1)} %get-tuple-element.27), channel_id=1, source_target_pairs={{2,4},{4,2},{3,5},{5,3},{10,12},{12,10},{11,13},{13,11},{18,20},{2... | collective-permute-start | bytes 1013768 | tf_op jit(solution)/shard_map/ppermute | solution.py:657
  10.5 1.6 %collective-permute-start = (f32[20,32,128]{2,1,0:T(8,128)S(1)}, f32[20,32,128]{2,1,0:T(8,128)S(1)}, u32[]{:S(2)}, u32[]{:S(2)}) collective-permute-start(f32[20,32,128]{2,1,0:T(8,128)S(1)} %get-tuple-element.24), channel_id=1, source_target_pairs={{0,8},{8,0},{16,24},{24,16},{1,9},{9,1},{17,25},{25,17},{2,10},{10... | collective-permute-start | bytes 983048 | tf_op jit(solution)/shard_map/ppermute | solution.py:657
  12.1 0.7 %collective-permute-start.1 = (f32[20,32,128]{2,1,0:T(8,128)S(1)}, f32[20,32,128]{2,1,0:T(8,128)S(1)}, u32[]{:S(2)}, u32[]{:S(2)}) collective-permute-start(f32[20,32,128]{2,1,0:T(8,128)S(1)} %get-tuple-element.25), channel_id=1, source_target_pairs={{8,16},{16,8},{9,17},{17,9},{10,18},{18,10},{11,19},{19,11},{12,20... | collective-permute-start | bytes 983048 | tf_op jit(solution)/shard_map/ppermute | solution.py:657
  12.7 5.0 %collective-permute-done.2.ye = f32[165,4,128]{2,1,0:T(4,128)S(1)} collective-permute-done((f32[165,4,128]{2,1,0:T(4,128)S(1)}, f32[165,4,128]{2,1,0:T(4,128)S(1)}, u32[]{:S(2)}, u32[]{:S(2)}) %collective-permute-start.2) | collective-permute-done | bytes 337952 | tf_op jit(solution)/shard_map/ppermute | solution.py:657
  17.8 0.0 collective-permute-done.3.yo
  17.8 0.9 %corners.1 = (f32[50,4,128]{2,1,0:T(4,128)S(1)}, f32[50,4,128]{2,1,0:T(4,128)S(1)}) custom-call(f32[165,4,128]{2,1,0:T(4,128)S(1)} %collective-permute-done.2.ye, f32[165,4,128]{2,1,0:T(4,128)S(1)} %collective-permute-done.3.yo), custom_call_target="tpu_custom_call" | custom-call | tf_op jit(solution)/shard_map/corners/pallas_call | solution.py:136
  18.6 1.7 %collective-permute-start.4 = (f32[50,4,128]{2,1,0:T(4,128)S(1)}, f32[50,4,128]{2,1,0:T(4,128)S(1)}, u32[]{:S(2)}, u32[]{:S(2)}) collective-permute-start(f32[50,4,128]{2,1,0:T(4,128)S(1)} %get-tuple-element.28), channel_id=1, source_target_pairs={{0,8},{8,0},{16,24},{24,16},{1,9},{9,1},{17,25},{25,17},{2,10},{10... | collective-permute-start | bytes 307208 | tf_op jit(solution)/shard_map/ppermute | solution.py:657
  20.3 0.7 %collective-permute-start.5 = (f32[50,4,128]{2,1,0:T(4,128)S(1)}, f32[50,4,128]{2,1,0:T(4,128)S(1)}, u32[]{:S(2)}, u32[]{:S(2)}) collective-permute-start(f32[50,4,128]{2,1,0:T(4,128)S(1)} %get-tuple-element.29), channel_id=1, source_target_pairs={{8,16},{16,8},{9,17},{17,9},{10,18},{18,10},{11,19},{19,11},{12,20... | collective-permute-start | bytes 307208 | tf_op jit(solution)/shard_map/ppermute | solution.py:657
  21.0 0.0 copy-done.4
  21.0 10.5 %inner_part.1 = (f32[2,2,40,40,128]{4,3,2,1,0:T(8,128)S(1)}, f32[2,2,40,40,128]{4,3,2,1,0:T(8,128)S(1)}, f32[2,2,40,40,128]{4,3,2,1,0:T(8,128)S(1)}, f32[2,2,40,...) custom-call(f32[2]{0:T(128)S(1)} %copy-done.4, ...), custom_call_target="tpu_custom_call" | custom-call | tf_op jit(solution)/shard_map/inner_part/pallas_call | solution.py:410
  31.5 0.0 collective-permute-done.xe
  31.5 0.0 collective-permute-done.1.xo
  31.5 0.0 collective-permute-done.4.ce
  31.5 0.0 collective-permute-done.5.co
  31.5 4.3 %edge_part.1 = (f32[2,2,40,40,128]{4,3,2,1,0:T(8,128)S(1)}, f32[2,2,40,40,128]{4,3,2,1,0:T(8,128)S(1)}, f32[2,2,40,40,128]{4,3,2,1,0:T(8,128)S(1)}, f32[2,2,40,4...) custom-call(f32[2]{0:T(128)S(1)} %copy-done.4, ...), custom_call_target="tpu_custom_call", output_to_operand_aliasing={{0}: (5, {}), {1}: (6, {}), {2}: (7, {}), {3}: (8, {}), {4}... | custom-call | tf_op jit(solution)/shard_map/edge_part/pallas_call | solution.py:552
  35.8 18.0 %all_to_all.5.sums = f32[16,8,128]{2,1,0:T(8,128)S(1)} all-to-all(f32[16,8,128]{2,1,0:T(8,128)S(1)} %get-tuple-element.40), channel_id=1, replica_groups=mesh['gx'=4,'gy'=4,'af'=2] {'gx','gy'}, dimensions={0} | all-to-all | bytes 131072 | tf_op jit(solution)/shard_map/all_to_all | solution.py:671
  53.9 1.6 %gradient_part.1 = f32[32,32,128]{2,1,0:T(8,128)S(1)} custom-call(f32[2]{0:T(128)S(1)} %copy-done.4, f32[16,8,128]{2,1,0:T(8,128)S(1)} %all_to_all.5.sums, f32[2,2,40,40,128]{4,3,2,1,0:T(8,128)S(1)} %get-tuple-element.43.s, f32[2,2,40,40,128]{4,3,2,1,0:T(8,128)S(1)} %get-tuple-element.41.v0, f32[2,2,40,40,128]{4,3,2,1,0:T(8,128)S(1)} %get-tuple-element.44.u0, ...), custom_call_target="tpu_custom_call" | custom-call | tf_op jit(solution)/shard_map/gradient_part/pallas_call | solution.py:630
  55.5 0.1 collective-permute-start.6
  55.6 2.6 %wavefield.1 = f32[2,2,32,32,128]{4,3,2,1,0:T(8,128)} custom-call(f32[16,8,128]{2,1,0:T(8,128)S(1)} %all_to_all.5.sums, f32[2,2,40,40,128]{4,3,2,1,0:T(8,128)S(1)} %get-tuple-element.41.v0, f32[2,2,40,40,128]{4,3,2,1,0:T(8,128)S(1)} %get-tuple-element.42.v1), custom_call_target="tpu_custom_call" | custom-call | tf_op jit(solution)/shard_map/wavefield/pallas_call | solution.py:638
  58.2 0.0 collective-permute-done.6
  58.2 0.9 %add.3 = f32[32,32,128]{2,1,0:T(8,128)} add(f32[32,32,128]{2,1,0:T(8,128)S(1)} %gradient_part.1, f32[32,32,128]{2,1,0:T(8,128)S(1)} %collective-permute-done.6) | non-fusion elementwise | flops 131072 | bytes 1572864 | tf_op jit(solution)/shard_map/add | solution.py:674
Async XLA Ops:
  0.6 1.6 %copy-start = (f32[2,2,32,32,128]{4,3,2,1,0:T(8,128)S(1)}, f32[2,2,32,32,128]{4,3,2,1,0:T(8,128)}, u32[]{:S(2)}) copy-start(f32[2,2,32,32,128]{4,3,2,1,0:T(8,128)} %source.3) | copy-start | bytes 6291460
  2.2 1.0 %copy-start.1 = (f32[32,32,128]{2,1,0:T(8,128)S(1)}, f32[32,32,128]{2,1,0:T(8,128)}, u32[]{:S(2)}) copy-start(f32[32,32,128]{2,1,0:T(8,128)} %model.3) | copy-start | bytes 1572868
  3.3 0.8 %copy-start.2 = (f32[2,2,32,32]{3,2,1,0:T(8,128)S(1)}, f32[2,2,32,32]{3,2,1,0:T(8,128)}, u32[]{:S(2)}) copy-start(f32[2,2,32,32]{3,2,1,0:T(8,128)} %observed.1) | copy-start | bytes 49156
  4.1 0.7 %copy-start.3 = (s32[32,32]{1,0:T(8,128)S(1)}, s32[32,32]{1,0:T(8,128)}, u32[]{:S(2)}) copy-start(s32[32,32]{1,0:T(8,128)} %depth.1) | copy-start | bytes 12292
  4.8 16.2 %copy-start.4 = (f32[2]{0:T(128)S(1)}, f32[2]{0:T(128)}, u32[]{:S(2)}) copy-start(f32[2]{0:T(128)} %freq_sq.5) | copy-start | bytes 28
  6.7 11.0 %collective-permute-start.2 = (f32[165,4,128]{2,1,0:T(4,128)S(1)}, f32[165,4,128]{2,1,0:T(4,128)S(1)}, u32[]{:S(2)}, u32[]{:S(2)}) collective-permute-start(f32[165,4,128]{2,1,0:T(4,128)S(1)} %get-tuple-element.26), channel_id=1, source_target_pairs={{0,2},{2,0},{4,6},{6,4},{1,3},{3,1},{5,7},{7,5},{8,10},{10,8},{12,... | collective-permute-start | bytes 1013768 | tf_op jit(solution)/shard_map/ppermute | solution.py:657
  9.8 7.9 %collective-permute-start.3 = (f32[165,4,128]{2,1,0:T(4,128)S(1)}, f32[165,4,128]{2,1,0:T(4,128)S(1)}, u32[]{:S(2)}, u32[]{:S(2)}) collective-permute-start(f32[165,4,128]{2,1,0:T(4,128)S(1)} %get-tuple-element.27), channel_id=1, source_target_pairs={{2,4},{4,2},{3,5},{5,3},{10,12},{12,10},{11,13},{13,11},{18,20},{2... | collective-permute-start | bytes 1013768 | tf_op jit(solution)/shard_map/ppermute | solution.py:657
  10.5 21.0 %collective-permute-start = (f32[20,32,128]{2,1,0:T(8,128)S(1)}, f32[20,32,128]{2,1,0:T(8,128)S(1)}, u32[]{:S(2)}, u32[]{:S(2)}) collective-permute-start(f32[20,32,128]{2,1,0:T(8,128)S(1)} %get-tuple-element.24), channel_id=1, source_target_pairs={{0,8},{8,0},{16,24},{24,16},{1,9},{9,1},{17,25},{25,17},{2,10},{10... | collective-permute-start | bytes 983048 | tf_op jit(solution)/shard_map/ppermute | solution.py:657
  12.1 19.4 %collective-permute-start.1 = (f32[20,32,128]{2,1,0:T(8,128)S(1)}, f32[20,32,128]{2,1,0:T(8,128)S(1)}, u32[]{:S(2)}, u32[]{:S(2)}) collective-permute-start(f32[20,32,128]{2,1,0:T(8,128)S(1)} %get-tuple-element.25), channel_id=1, source_target_pairs={{8,16},{16,8},{9,17},{17,9},{10,18},{18,10},{11,19},{19,11},{12,20... | collective-permute-start | bytes 983048 | tf_op jit(solution)/shard_map/ppermute | solution.py:657
  18.6 12.9 %collective-permute-start.4 = (f32[50,4,128]{2,1,0:T(4,128)S(1)}, f32[50,4,128]{2,1,0:T(4,128)S(1)}, u32[]{:S(2)}, u32[]{:S(2)}) collective-permute-start(f32[50,4,128]{2,1,0:T(4,128)S(1)} %get-tuple-element.28), channel_id=1, source_target_pairs={{0,8},{8,0},{16,24},{24,16},{1,9},{9,1},{17,25},{25,17},{2,10},{10... | collective-permute-start | bytes 307208 | tf_op jit(solution)/shard_map/ppermute | solution.py:657
  20.3 11.2 %collective-permute-start.5 = (f32[50,4,128]{2,1,0:T(4,128)S(1)}, f32[50,4,128]{2,1,0:T(4,128)S(1)}, u32[]{:S(2)}, u32[]{:S(2)}) collective-permute-start(f32[50,4,128]{2,1,0:T(4,128)S(1)} %get-tuple-element.29), channel_id=1, source_target_pairs={{8,16},{16,8},{9,17},{17,9},{10,18},{18,10},{11,19},{19,11},{12,20... | collective-permute-start | bytes 307208 | tf_op jit(solution)/shard_map/ppermute | solution.py:657
  55.5 2.7 %collective-permute-start.6 = (f32[32,32,128]{2,1,0:T(8,128)S(1)}, f32[32,32,128]{2,1,0:T(8,128)S(1)}, u32[]{:S(2)}, u32[]{:S(2)}) collective-permute-start(f32[32,32,128]{2,1,0:T(8,128)S(1)} %gradient_part.1), channel_id=1, source_target_pairs={{0,1},{1,0},{2,3},{3,2},{4,5},{5,4},{6,7},{7,6},{8,9},{9,8},{10,11... | collective-permute-start | bytes 1572872 | tf_op jit(solution)/shard_map/ppermute | solution.py:674

commit v2 on v0

v2 whole, which is shorter than its diff:
```python
import functools

import jax
import jax.numpy as jnp
from jax import lax
from jax.experimental import pallas as pl
from jax.experimental.pallas import tpu as pltpu
from jax.sharding import PartitionSpec as P

ITERS = 2
attenuation = 0.2
penalty = 4.0

HALO = 2 * ITERS
INNER = HALO - 1
F32 = jnp.float32
ANY = pl.BlockSpec(memory_space=pl.ANY)
HBM = pl.BlockSpec(memory_space=pltpu.HBM)
VMEM = pl.BlockSpec(memory_space=pltpu.VMEM)
SMEM = pl.BlockSpec(memory_space=pltpu.SMEM)
MIB = 1 << 20
LOAD_MIB = 55
SHIFT = 2


def params(mib):
    return pltpu.CompilerParams(vmem_limit_bytes=mib * MIB)


def cost(us):
    return pl.CostEstimate(
        flops=int(us * 1e3), bytes_accessed=int(us * 1e3), transcendentals=0
    )


def parity(axis):
    return lax.rem(lax.axis_index(axis), 2) == 0


class Copies:
    def __init__(self, sem):
        self.sem, self.all = sem, []

    def add(self, src, dst):
        copy = pltpu.make_async_copy(src, dst, self.sem.at[len(self.all)])
        copy.start()
        self.all.append(copy)

    def wait(self):
        for copy in self.all:
            copy.wait()


def lane_slab(table, fields, skip, rows, nz):
    lane = lax.broadcasted_iota(jnp.int32, (rows, nz), 1)
    lanes = jnp.zeros((rows, nz), F32)
    for k in range(fields + 1):
        inside = (lane >= 8 * k) & (lane < 8 * k + INNER)
        shift = lax.rem(8 * k + nz - skip, nz)
        lanes = jnp.where(inside, pltpu.roll(table[k], shift, axis=1), lanes)
    return lanes


def load_kernel(source, model, observed, depth, *refs):
    freqs, _, nx, ny, nz = source.shape
    fields = 2 * freqs
    s, (cells, aux, xe, xo, ye, yo, seen, sunk, table, slab, sem) = refs[:freqs], refs[freqs:]
    small = Copies(sem.at[0])
    small.add(observed, seen)
    small.add(depth, sunk)
    large = Copies(sem.at[1])
    large.add(model, cells.at[:, pl.ds(0, ny), :])
    for f in range(freqs):
        for p in range(2):
            large.add(source.at[f, p], s[f].at[p, pl.ds(0, nx), pl.ds(0, ny), :])
    even_x, even_y = parity("gx"), parity("gy")
    small.wait()
    for f in range(freqs):
        for p in range(2):
            table[2 * f + p, :, 0:nx] = seen[f, p].T
    table[fields, :, 0:nx] = sunk[...].astype(F32).T
    copies = Copies(sem.at[2])
    copies.add(table, aux.at[:, pl.ds(0, ny), :])
    faces = []
    for side, xb in enumerate((xe, xo)):
        last = even_x if side == 0 else jnp.logical_not(even_x)
        skip = jnp.where(last, nx - INNER, 0)
        faces.append((xb, skip, jnp.where(last, nx - HALO, 0)))
        slab[side] = lane_slab(table, fields, skip, ny, nz)
        copies.add(
            slab.at[pl.ds(side, 1)], xb.at[pl.ds(fields * HALO + INNER, 1)]
        )
    places = []
    for side, yb in enumerate((ye, yo)):
        last = even_y if side == 0 else jnp.logical_not(even_y)
        at = pl.multiple_of(jnp.where(last, ny - HALO, 0), HALO)
        places.append((yb, at))
        copies.add(
            table.at[:, pl.ds(at, HALO), :],
            yb.at[pl.ds((fields + 1) * nx, fields + 1)],
        )
    large.all[0].wait()
    for yb, at in places:
        copies.add(cells.at[:, pl.ds(at, HALO), :], yb.at[pl.ds(fields * nx, nx)])
    for xb, skip, _ in faces:
        copies.add(
            cells.at[pl.ds(skip, INNER), pl.ds(0, ny), :],
            xb.at[pl.ds(fields * HALO, INNER)],
        )
    for k in range(fields):
        large.all[1 + k].wait()
        block = s[k // 2].at[k % 2]
        for yb, at in places:
            copies.add(
                block.at[pl.ds(0, nx), pl.ds(at, HALO), :], yb.at[pl.ds(k * nx, nx)]
            )
        for xb, _, at in faces:
            copies.add(
                block.at[pl.ds(at, HALO), pl.ds(0, ny), :],
                xb.at[pl.ds(k * HALO, HALO)],
            )
    copies.wait()


def load(source, model, observed, depth):
    freqs, _, nx, ny, nz = source.shape
    fields = 2 * freqs
    xs = pltpu.VMEM((fields * HALO + INNER + 1, ny, nz), F32)
    ys = pltpu.VMEM(((fields + 1) * nx + fields + 1, HALO, nz), F32)
    return pl.pallas_call(
        load_kernel,
        out_shape=(pltpu.VMEM((2, nx + 2 * HALO, ny + 2 * HALO, nz), F32),) * freqs
        + (
            pltpu.VMEM((nx, ny + 2 * HALO, nz), F32),
            pltpu.VMEM((fields + 1, ny + 2 * HALO, nz), F32),
            xs,
            xs,
            ys,
            ys,
        ),
        in_specs=[HBM] * 4,
        scratch_shapes=[
            pltpu.VMEM(observed.shape, F32),
            pltpu.VMEM(depth.shape, jnp.int32),
            pltpu.VMEM((fields + 1, ny, nz), F32),
            pltpu.VMEM((2, ny, nz), F32),
            pltpu.SemaphoreType.DMA((3, 32)),
        ],
        compiler_params=params(LOAD_MIB),
        name="load",
    )(source, model, observed, depth)


def halo_places(ny):
    even_y = parity("gy")
    at_e = pl.multiple_of(jnp.where(even_y, ny, ny + HALO), HALO)
    at_o = pl.multiple_of(jnp.where(even_y, ny + HALO, ny), HALO)
    return at_e, at_o


class Grid:
    def __init__(self, nx, ny, nz):
        self.nx, self.ny, self.nz = nx, ny, nz
        self.xe, self.ye = nx + 2 * HALO, ny + 2 * HALO
        self.tiles = self.ye // 8
        lane = lax.broadcasted_iota(jnp.int32, (8, nz), 1)
        self.first = lane == 0
        self.last = lane == nz - 1
        self.depths = lane.astype(F32)
        self.sub = lax.broadcasted_iota(jnp.int32, (8, nz), 0)
        has_left = lax.axis_index("gy") > 0
        has_right = lax.axis_index("gy") < lax.axis_size("gy") - 1
        self.cut_left = jnp.where(
            self.sub == 0, jnp.where(has_left, 1.0, 0.0), jnp.ones((8, nz), F32)
        )
        self.cut_tile = (ny - 1) % self.tiles
        self.cut_right = jnp.where(
            self.sub == (ny - 1) // self.tiles,
            jnp.where(has_right, 1.0, 0.0),
            jnp.ones((8, nz), F32),
        )
        self.groups = {}
        for t in range(self.tiles):
            owned = -((t - ny) // self.tiles)
            self.groups.setdefault(owned, []).append(t)

    def rows(self, ref, p, i):
        return [
            ref[p, i, pl.ds(t, 8, stride=self.tiles), :] for t in range(self.tiles)
        ]

    def put(self, ref, p, i, values):
        for t in range(self.tiles):
            ref[p, i, pl.ds(t, 8, stride=self.tiles), :] = values[t]

    def beside(self, mid):
        out = []
        for t in range(self.tiles):
            left = jnp.where(self.first, 0.0, pltpu.roll(mid[t], 1, axis=1))
            right = jnp.where(self.last, 0.0, pltpu.roll(mid[t], self.nz - 1, axis=1))
            out.append(left + right)
        return out

    def around(self, mid, below, above, beside):
        total = []
        n = self.tiles
        for t in range(n):
            up = mid[t + 1] if t + 1 < n else pltpu.roll(mid[0], 7, axis=0)
            down = mid[t - 1] if t else pltpu.roll(mid[n - 1], 1, axis=0)
            if t == 0:
                down = down * self.cut_left
            if t == self.cut_tile:
                up = up * self.cut_right
            total.append(((below[t] + above[t]) + (up + down)) + beside[t])
        return total

    def apply(self, src, i, lo, hi, sign, coef, mid_im, beside_im, cut=None):
        cr, ci = coef
        mid_re = self.rows(src, 0, i)
        total = []
        for p, mid, beside in (
            (0, mid_re, self.beside(mid_re)),
            (1, mid_im, beside_im),
        ):
            below, above = self.rows(src, p, lo), self.rows(src, p, hi)
            if cut is not None and cut[0] < 0:
                below = [b * cut[1] for b in below]
            if cut is not None and cut[0] > 0:
                above = [a * cut[1] for a in above]
            total.append(self.around(mid, below, above, beside))
        out_re, out_im = [], []
        for t in range(self.tiles):
            re, im = mid_re[t], mid_im[t]
            if sign > 0:
                out_re.append(cr[t] * re - ci[t] * im - total[0][t])
                out_im.append(cr[t] * im + ci[t] * re - total[1][t])
            else:
                out_re.append(cr[t] * re + ci[t] * im - total[0][t])
                out_im.append(cr[t] * im - ci[t] * re - total[1][t])
        return out_re, out_im

    def squares(self, re, im):
        return [re[t] * re[t] + im[t] * im[t] for t in range(self.tiles)]

    def gather(self, acc, values):
        return tuple(
            a + functools.reduce(jnp.add, [values[t] for t in ts])
            for a, ts in zip(acc, self.groups.values())
        )

    def zero(self):
        return tuple(jnp.zeros((8, self.nz), F32) for _ in self.groups)

    def total(self, acc):
        return functools.reduce(
            jnp.add,
            [jnp.where(self.sub < n, a, 0.0) for a, n in zip(acc, self.groups)],
        )

    def tile_list(self, ref, i):
        return [ref[i, t] for t in range(self.tiles)]

    def weigh(self, i, w, depth):
        for t in range(self.tiles):
            w[i, t] = jnp.where(self.depths == depth[t], penalty, 0.0)

    def coefs(self, i, freq_sq, cells, cr, ci):
        for t in range(self.tiles):
            scaled = freq_sq * cells[t]
            cr[i, t] = 6.0 - scaled
            ci[i, t] = attenuation * scaled


class Field:
    def __init__(self, grid, refs, w):
        self.grid = grid
        self.s, self.v0, self.u0, self.v1, self.u1, self.cr, self.ci = refs
        self.w = w

    def source_of(self, stage):
        return (self.s, self.v0, self.u0, self.v1)[stage]

    def target_of(self, stage):
        return (self.v0, self.u0, self.v1, self.u1)[stage]

    def step(self, stage, i, lo, hi, mid_im, beside_im, terms=None, cut=None, acc=None):
        g = self.grid
        tiles = range(g.tiles)
        coef = (g.tile_list(self.cr, i), g.tile_list(self.ci, i))
        sign = -1 if stage in (0, 2) else 1
        re, im = g.apply(
            self.source_of(stage), i, lo, hi, sign, coef, mid_im, beside_im, cut
        )
        weight = g.tile_list(self.w, i) if stage in (0, 2) else None
        if stage == 0:
            re = [re[t] + terms[0][t] for t in tiles]
            im = [im[t] + terms[1][t] for t in tiles]
        if stage == 2:
            old_re, old_im = g.rows(self.v0, 0, i), g.rows(self.v0, 1, i)
            re = [re[t] + weight[t] * old_re[t] for t in tiles]
            im = [im[t] + weight[t] * old_im[t] for t in tiles]
        g.put(self.target_of(stage), 0, i, re)
        g.put(self.target_of(stage), 1, i, im)
        if acc is None:
            return None
        acc = list(acc)
        squares = g.squares(re, im)
        acc[stage] = g.gather(acc[stage], squares)
        if stage in (0, 2):
            weighted = [weight[t] * squares[t] for t in tiles]
            acc[stage + 1] = g.gather(acc[stage + 1], weighted)
        return tuple(acc)


def corner_faces(freqs, nx, ny, s, cells, aux, ce, co, slab, sem):
    fields = 2 * freqs
    nz = cells.shape[2]
    even_x = parity("gx")
    out = Copies(sem)
    rows = pl.ds(ny, 2 * HALO)
    for side, cb in enumerate((ce, co)):
        last = even_x if side == 0 else jnp.logical_not(even_x)
        skip = jnp.where(last, nx - INNER, 0)
        at = jnp.where(last, nx - HALO, 0)
        for k in range(fields):
            out.add(
                s[k // 2].at[k % 2, pl.ds(at, HALO), rows, :],
                cb.at[pl.ds(k * HALO, HALO)],
            )
        out.add(cells.at[pl.ds(skip, INNER), rows, :], cb.at[pl.ds(fields * HALO, INNER)])
        near = [aux[k, ny:, :] for k in range(fields + 1)]
        slab[side] = lane_slab(near, fields, skip, 2 * HALO, nz)
        out.add(
            slab.at[pl.ds(side, 1)], cb.at[pl.ds(fields * HALO + INNER, 1)]
        )
    return out


def inner_kernel(freqs, nx, ny, half, freq_sq, *refs):
    if half == 0:
        ye, yo = refs[:2]
        refs = refs[2 + freqs + 2 :]
        s, (cells, aux), refs = refs[:freqs], refs[freqs : freqs + 2], refs[freqs + 2 :]
        state, (w, moments, ce, co, slab, sem) = refs[: 6 * freqs], refs[6 * freqs :]
    else:
        (cells, aux), s = refs[:2], refs[2 : 2 + freqs]
        partial = refs[2 + freqs + 6 * freqs + 1]
        refs = refs[2 + 7 * freqs + 2 :]
        state, (w, moments) = refs[: 6 * freqs], refs[6 * freqs :]
    nz = cells.shape[2]
    fields = 2 * freqs
    if half == 0:
        copies = Copies(sem.at[0])
        for yb, at in zip((ye, yo), halo_places(ny)):
            rows = pl.ds(at, HALO)
            copies.add(
                yb.at[pl.ds((fields + 1) * nx, fields + 1)], aux.at[:, rows, :]
            )
            copies.add(yb.at[pl.ds(fields * nx, nx)], cells.at[:, rows, :])
            for k in range(fields):
                copies.add(
                    yb.at[pl.ds(k * nx, nx)],
                    s[k // 2].at[k % 2, pl.ds(0, nx), rows, :],
                )
    grid = Grid(nx, ny, nz)
    if half == 0:
        copies.wait()
        out = corner_faces(freqs, nx, ny, s, cells, aux, ce, co, slab, sem.at[1])
    tiles = grid.tiles
    many = [Field(grid, (s[f], *state[6 * f : 6 * f + 6]), w) for f in range(freqs)]

    def prepare(i):
        def column(k):
            pick = jnp.full((8, nz), i, jnp.int32)
            return [
                jnp.take_along_axis(
                    aux[k, pl.ds(t, 8, stride=tiles), :], pick, axis=1
                )
                for t in range(tiles)
            ]

        rows = [cells[i, pl.ds(t, 8, stride=tiles), :] for t in range(tiles)]
        grid.weigh(i, w, column(fields))
        weight = grid.tile_list(w, i)
        out = []
        for f in range(freqs):
            grid.coefs(i, freq_sq[f], rows, many[f].cr, many[f].ci)
            terms = []
            for p in range(2):
                seen = column(2 * f + p)
                terms.append([weight[t] * seen[t] for t in range(tiles)])
            out.append(terms)
        return out

    if half == 0:
        for i in (0, nx - 1):
            terms = prepare(i)
            for f in range(freqs):
                for p in range(2):
                    grid.put(many[f].v0, p, i, terms[f][p])

    def step(j, acc, active):
        acc = list(acc)
        for k in reversed(active):
            i = j - 2 * k
            terms = prepare(i) if k == 0 else [None] * freqs
            for f in range(freqs):
                mid = grid.rows(many[f].source_of(k), 1, i)
                acc[f] = many[f].step(
                    k, i, i - 1, i + 1, mid, grid.beside(mid), terms[f], acc=acc[f]
                )
        return tuple(acc)

    spans = [(1 + 3 * k, nx - 1 + k) for k in range(4)]
    middle = nx // 2 + SHIFT
    edges = sorted({e for span in spans for e in span} | {middle})
    acc = tuple(tuple(grid.zero() for _ in range(4)) for _ in range(freqs))
    for lo, hi in zip(edges[:-1], edges[1:]):
        if (lo < middle) != (half == 0):
            continue
        active = [k for k, (a, b) in enumerate(spans) if a <= lo and hi <= b]
        acc = lax.fori_loop(lo, hi, functools.partial(step, active=active), acc)
    for f in range(freqs):
        for m in range(4):
            value = grid.total(acc[f][m])
            moments[f, m] = value if half == 0 else value + partial[f, m]
    if half == 0:
        out.wait()


def inner_part(nx, ny, freq_sq, ye, yo, s, cells, aux):
    _, xe, ye_rows, nz = s[0].shape
    freqs = len(s)
    slabs = 2 * freqs * HALO + INNER + 1
    field = pltpu.VMEM(s[0].shape, F32)
    coef = pltpu.VMEM((xe, ye_rows // 8, 8, nz), F32)
    corner = pltpu.VMEM((slabs, 2 * HALO, nz), F32)
    kept = (*s, cells, aux)
    news = ((field,) * 4 + (coef, coef)) * freqs + (
        coef,
        pltpu.VMEM((freqs, 4, 8, nz), F32),
    )
    got = pl.pallas_call(
        functools.partial(inner_kernel, freqs, nx, ny, 0),
        out_shape=tuple(pltpu.VMEM(k.shape, F32) for k in kept)
        + news
        + (corner, corner),
        in_specs=[SMEM, ANY, ANY] + [VMEM] * len(kept),
        input_output_aliases={3 + k: k for k in range(len(kept))},
        scratch_shapes=[
            pltpu.VMEM((2, 2 * HALO, nz), F32),
            pltpu.SemaphoreType.DMA((2, 16)),
        ],
        compiler_params=params(8),
        name="inner_first",
    )(freq_sq, ye, yo, *kept)
    s, cells, aux = got[:freqs], got[freqs], got[freqs + 1]
    news_got, (ce, co) = got[freqs + 2 : -2], got[-2:]

    def rest():
        again = pl.pallas_call(
            functools.partial(inner_kernel, freqs, nx, ny, 1),
            out_shape=news,
            in_specs=[SMEM] + [VMEM] * (2 + freqs + len(news)),
            input_output_aliases={3 + freqs + k: k for k in range(len(news))},
            compiler_params=params(8),
            name="inner_second",
        )(freq_sq, cells, aux, *s, *news_got)
        state = []
        for f in range(freqs):
            state += [s[f], *again[6 * f : 6 * f + 6]]
        return state + [again[-2]], again[-1]

    return ce, co, rest


def edge_kernel(peers, freqs, nx, ny, freq_sq, xe, xo, ce, co, *refs):
    count = 7 * freqs + 1
    moments, refs = refs[count], refs[count + 1 :]
    state, (part, cells, aux, sem) = refs[:count], refs[count:]
    fields = 2 * freqs
    nz = state[0].shape[3]
    w = state[-1]
    copies = Copies(sem)
    even_x = parity("gx")
    pieces = (
        (xe, 0, 0, ny),
        (xo, 1, 0, ny),
        (ce, 0, ny, 2 * HALO),
        (co, 1, ny, 2 * HALO),
    )
    for block, side, at, size in pieces:
        above = even_x if side == 0 else jnp.logical_not(even_x)
        slot = jnp.where(above, nx, nx + HALO)
        half = jnp.where(above, 0, 1)
        rows = pl.ds(at, size)
        for k in range(fields):
            copies.add(
                block.at[pl.ds(k * HALO, HALO)],
                state[7 * (k // 2)].at[k % 2, pl.ds(slot, HALO), rows, :],
            )
        copies.add(
            block.at[pl.ds(fields * HALO, INNER)], cells.at[half, :, rows, :]
        )
        copies.add(
            block.at[pl.ds(fields * HALO + INNER, 1)],
            aux.at[pl.ds(half, 1), rows, :],
        )
    grid = Grid(nx, ny, nz)
    copies.wait()
    tiles = grid.tiles
    many = [Field(grid, state[7 * f : 7 * f + 7], w) for f in range(freqs)]

    for half in range(2):
        for layer in range(INNER):
            i = nx + layer if half == 0 else nx + HALO + 1 + layer

            def column(k):
                pick = jnp.full((8, nz), 8 * k + layer, jnp.int32)
                return [
                    jnp.take_along_axis(
                        aux[half, pl.ds(t, 8, stride=tiles), :], pick, axis=1
                    )
                    for t in range(tiles)
                ]

            rows = [
                cells[half, layer, pl.ds(t, 8, stride=tiles), :] for t in range(tiles)
            ]
            grid.weigh(i, w, column(fields))
            weight = grid.tile_list(w, i)
            for f in range(freqs):
                grid.coefs(i, freq_sq[f], rows, many[f].cr, many[f].ci)
                for p in range(2):
                    seen = column(2 * f + p)
                    grid.put(
                        many[f].v0, p, i, [weight[t] * seen[t] for t in range(tiles)]
                    )

    left = jnp.where(lax.axis_index("gx") > 0, 1.0, 0.0)
    right = jnp.where(lax.axis_index("gx") < lax.axis_size("gx") - 1, 1.0, 0.0)
    wrap = grid.xe
    acc = [tuple(grid.zero() for _ in range(4)) for _ in range(freqs)]
    for stage in range(4):
        for k in range(HALO):
            jobs = [
                (x, f)
                for x in (k - INNER + stage, nx - 1 - stage + k)
                for f in range(freqs)
            ]
            mids = [many[f].source_of(stage) for _, f in jobs]
            mids = [grid.rows(ref, 1, x % wrap) for ref, (x, _) in zip(mids, jobs)]
            sums = [grid.beside(mid) for mid in mids]
            for (x, f), mid, beside in zip(jobs, mids, sums):
                i, lo, hi = x % wrap, (x - 1) % wrap, (x + 1) % wrap
                own = 0 <= x < nx
                cut = None
                if x == 0:
                    cut = (-1, left)
                if x == nx - 1:
                    cut = (1, right)
                terms = None
                if stage == 0:
                    terms = [grid.rows(many[f].v0, p, i) for p in range(2)]
                got = many[f].step(
                    stage, i, lo, hi, mid, beside, terms, cut, acc[f] if own else None
                )
                if own:
                    acc[f] = got

    rows = []
    for f in range(freqs):
        for m in range(4):
            both = grid.total(acc[f][m]) + moments[f, m]
            rows.append(jnp.sum(both, axis=0, keepdims=True))
    sums = jnp.sum(jnp.concatenate(rows, axis=0), axis=1, keepdims=True)
    sums = jnp.broadcast_to(sums, (4 * freqs, nz))
    for peer in range(peers):
        part[peer] = sums


def edge_part(peers, freqs, nx, ny, freq_sq, xe, xo, ce, co, state, moments):
    nz = state[0].shape[3]
    outs = tuple(pltpu.VMEM(k.shape, F32) for k in state)
    return pl.pallas_call(
        functools.partial(edge_kernel, peers, freqs, nx, ny),
        out_shape=outs + (jax.ShapeDtypeStruct((peers, 4 * freqs, nz), F32),),
        in_specs=[SMEM] + [ANY] * 4 + [VMEM] * (len(state) + 1),
        input_output_aliases={5 + k: k for k in range(len(state))},
        scratch_shapes=[
            pltpu.VMEM((2, INNER, ny + 2 * HALO, nz), F32),
            pltpu.VMEM((2, ny + 2 * HALO, nz), F32),
            pltpu.SemaphoreType.DMA((64,)),
        ],
        compiler_params=params(8),
        name="edge_part",
    )(freq_sq, xe, xo, ce, co, *state, moments)


def steps(sums, freqs):
    total = jnp.sum(sums[...], axis=0)
    shape = (8, total.shape[1])
    out = []
    for f in range(freqs):
        m0, m1, m2, m3 = (
            jnp.broadcast_to(total[4 * f + k : 4 * f + k + 1, :], shape)
            for k in range(4)
        )
        first = m0 / m1
        new = first * (first * m2 - m1)
        product = m1 - first * (2.0 * m2 - first * m3)
        ratio = new / m0
        second = new / (product - ratio * new / first)
        out.append((first + second * (1.0 + ratio), -first * second))
    return out


def gradient_kernel(freqs, nx, ny, freq_sq, sums, *refs):
    out = refs[-1]
    weights = steps(sums, freqs)

    def row(x, _):
        for y in range(0, ny, 8):
            at = pl.ds(y, 8)
            total = None
            for f in range(freqs):
                s, v0, u0, v1, u1 = refs[5 * f : 5 * f + 5]
                a, b = weights[f]
                wave_re = a * v0[0, x, at, :] + b * v1[0, x, at, :]
                wave_im = a * v0[1, x, at, :] + b * v1[1, x, at, :]
                miss_re = a * u0[0, x, at, :] + b * u1[0, x, at, :]
                miss_im = a * u0[1, x, at, :] + b * u1[1, x, at, :]
                miss_re = miss_re - s[0, x, at, :]
                miss_im = miss_im - s[1, x, at, :]
                left = (wave_re + attenuation * wave_im) * miss_re
                right = (wave_im - attenuation * wave_re) * miss_im
                term = -freq_sq[f] * (left + right)
                total = term if total is None else total + term
            out[x, at, :] = total
        return 0

    lax.fori_loop(0, nx, row, 0)


def wave_kernel(freqs, nx, ny, sums, *refs):
    out, block, sem = refs[2 * freqs :]
    weights = steps(sums, freqs)
    copies = Copies(sem)
    for f in range(freqs):
        a, b = weights[f]
        v0, v1 = refs[2 * f : 2 * f + 2]
        for p in range(2):
            k = 2 * f + p

            def row(x, _):
                for y in range(0, ny, 8):
                    at = pl.ds(y, 8)
                    block[k, x, at, :] = a * v0[p, x, at, :] + b * v1[p, x, at, :]
                return 0

            lax.fori_loop(0, nx, row, 0)
            copies.add(block.at[k], out.at[f, p])
    copies.wait()


def results(freqs, nx, ny, freq_sq, sums, state):
    nz = state[0].shape[3]
    fields, pairs = [], []
    for f in range(freqs):
        s, v0, u0, v1, u1 = state[7 * f : 7 * f + 5]
        fields += [s, v0, u0, v1, u1]
        pairs += [v0, v1]
    gradient = pl.pallas_call(
        functools.partial(gradient_kernel, freqs, nx, ny),
        out_shape=jax.ShapeDtypeStruct((nx, ny, nz), F32),
        in_specs=[SMEM] + [VMEM] * (1 + len(fields)),
        out_specs=VMEM,
        compiler_params=params(8),
        name="gradient_part",
    )(freq_sq, sums, *fields)
    wave = pl.pallas_call(
        functools.partial(wave_kernel, freqs, nx, ny),
        out_shape=jax.ShapeDtypeStruct((freqs, 2, nx, ny, nz), F32),
        in_specs=[VMEM] * (1 + len(pairs)),
        out_specs=HBM,
        scratch_shapes=[
            pltpu.VMEM((2 * freqs, nx, ny, nz), F32),
            pltpu.SemaphoreType.DMA((2 * freqs,)),
        ],
        compiler_params=params(8),
        name="wavefield",
    )(sums, *pairs)
    return gradient, wave


def swap(cells, axis, odd):
    count = lax.axis_size(axis)
    pairs = []
    for i in range(odd, count - 1, 2):
        pairs += [(i, i + 1), (i + 1, i)]
    return lax.ppermute(cells, axis, pairs)


def on_device(model, freq_sq, source, observed, receiver_depth):
    nx, ny, nz = model.shape
    freqs = freq_sq.shape[0]
    *s, cells, aux, xe, xo, ye, yo = load(source, model, observed, receiver_depth)
    ye, yo = swap(ye, "gy", 0), swap(yo, "gy", 1)
    xe, xo = swap(xe, "gx", 0), swap(xo, "gx", 1)
    ce, co, rest = inner_part(nx, ny, freq_sq, ye, yo, s, cells, aux)
    ce, co = swap(ce, "gx", 0), swap(co, "gx", 1)
    state, moments = rest()
    peers = lax.axis_size("gx") * lax.axis_size("gy")
    *state, part = edge_part(
        peers, freqs, nx, ny, freq_sq, xe, xo, ce, co, state, moments
    )
    sums = lax.all_to_all(part, ("gx", "gy"), 0, 0)
    gradient, wave = results(freqs, nx, ny, freq_sq, sums, state)
    if lax.axis_size("af") == 2:
        gradient = gradient + lax.ppermute(gradient, "af", [(0, 1), (1, 0)])
    else:
        gradient = lax.psum(gradient, "af")
    return wave, gradient


def solution(mesh):
    in_specs = (
        P("gx", "gy", None),
        P("af"),
        P("af", None, "gx", "gy", None),
        P("af", None, "gx", "gy"),
        P("gx", "gy"),
    )
    out_specs = (P("af", None, "gx", "gy", None), P("gx", "gy", None))
    return jax.shard_map(
        on_device, mesh=mesh, in_specs=in_specs, out_specs=out_specs, check_vma=False
    )
```

time: 262 us -> 53.9 us (0.21)
  blocking collectives: 90.3 us -> 18.1 us
  starting transfers between devices: 74.7 us -> 8.43 us
  other arithmetic: 32.8 us -> 0.88 us
  waiting for transfers between devices: 30.6 us -> 5.18 us
  Pallas kernels: 0 us -> 20.4 us
  local copies, waits for them, and re-layouts: 18.5 us -> 0.01 us
  between operations: 14.6 us -> 0.75 us
    psum x2 -> x0, blocking collectives: 90.3 us -> none  [two_products(): return lax.psum((inner(resid, resid), inner(resid, image)), ('gx', 'gy'))]
    ppermute x24 -> x7, starting transfers between devices: 74.7 us -> 8.43 us  [the longest x6 8.36 us: swap(): return lax.ppermute(cells, axis, pairs)]
    pallas_call x0 -> x6, Pallas kernels: none -> 20.4 us  [the longest x1 5.67 us: inner_part(): pl.pallas_call(functools.partial(inner_kernel, freqs, nx, ny, 0), out_sha...]
    all_to_all x0 -> x1, blocking collectives: none -> 18.1 us  [on_device(): sums = lax.all_to_all(part, ('gx', 'gy'), 0, 0)]
    psum x1 -> x0, waiting for transfers between devices: 15.2 us -> none  [on_device(): gradient = lax.psum(local_terms, 'af')]
    sub x10 -> x0, other arithmetic: 13 us -> none  [the longest x2 4.14 us: forward(): return apply_coef(coef_real, coef_imag, field, 1.0) - beside(field)]
    unnamed x20 -> x2, local copies, waits for them, and re-layouts: 10.4 us -> 0.01 us
    ppermute x24 -> x7, waiting for transfers between devices: 15.3 us -> 5.18 us  [the longest x6 5.03 us: swap(): return lax.ppermute(cells, axis, pairs)]
  transfers between devices with their start and end apart: 25 -> 7, of which waited for: 15 -> 2; matrix products, arithmetic and copies ran while one was open for 7% -> 0% of each run, Pallas kernels for 0% -> 23%
where the time goes in v2:
time: 53.9 us; the launch traced here: 53.7 us
  Pallas kernels  20.4 us (38%)
  blocking collectives  18.1 us (34%)
  starting transfers between devices  8.43 us (16%)
  waiting for transfers between devices  5.18 us (10%)
  other arithmetic  0.88 us (2%)
  between operations  0.75 us (1%)
    all_to_all x1, blocking collectives, on_device(): sums = lax.all_to_all(part, ('gx', 'gy'), 0, 0)  18.1 us
    ppermute x6, starting transfers between devices, swap(): return lax.ppermute(cells, axis, pairs)  8.36 us
    pallas_call x1, Pallas kernels, inner_part(): pl.pallas_call(functools.partial(inner_kernel, freqs, nx, ny, 0), out_sha...  5.67 us
    ppermute x6, waiting for transfers between devices, swap(): return lax.ppermute(cells, axis, pairs)  5.03 us
    pallas_call x1, Pallas kernels, rest(): pl.pallas_call(functools.partial(inner_kernel, freqs, nx, ny, 1), out_sha...  5 us
    pallas_call x1, Pallas kernels, edge_part(): pl.pallas_call(functools.partial(edge_kernel, peers, freqs, nx, ny), out_...  3.58 us
    pallas_call x1, Pallas kernels, load(): pl.pallas_call(load_kernel, out_shape=(pltpu.VMEM((2, nx + 2 * HALO, ny +...  2.69 us
    pallas_call x1, Pallas kernels, results(): pl.pallas_call(functools.partial(wave_kernel, freqs, nx, ny), out_shape=j...  1.74 us
  transfers between devices with their start and end apart: 7, of which 2 were waited for; matrix products, arithmetic and copies ran while one was open for 0% of the time, Pallas kernels for 23%

profile of v2, /device:TPU:0, one launch (start us, length us, event | category | flops | bytes accessed | tf_op | source)
XLA Modules:
  0.0 53.7 jit_solution(8892818884620314054)
XLA Ops:
  0.6 0.0 copy-start
  0.6 2.7 %load.1 = (f32[2,40,40,128]{3,2,1,0:T(8,128)S(1)}, f32[2,40,40,128]{3,2,1,0:T(8,128)S(1)}, f32[32,40,128]{2,1,0:T(8,128)S(1)}, f32[5,40,128]{2,1,0:T(8,128)S(1)}...) custom-call(f32[2,2,32,32,128]{4,3,2,1,0:T(8,128)} %source.1, ...), custom_call_target="tpu_custom_call" | custom-call | tf_op jit(solution)/shard_map/load/pallas_call | solution.py:130
  3.3 3.1 %collective-permute-start.2 = (f32[165,4,128]{2,1,0:T(4,128)S(1)}, f32[165,4,128]{2,1,0:T(4,128)S(1)}, u32[]{:S(2)}, u32[]{:S(2)}) collective-permute-start(f32[165,4,128]{2,1,0:T(4,128)S(1)} %get-tuple-element.57), channel_id=1, source_target_pairs={{0,2},{2,0},{4,6},{6,4},{1,3},{3,1},{5,7},{7,5},{8,10},{10,8},{12,... | collective-permute-start | bytes 1013768 | tf_op jit(solution)/shard_map/ppermute | solution.py:701
  6.4 0.7 %collective-permute-start.3 = (f32[165,4,128]{2,1,0:T(4,128)S(1)}, f32[165,4,128]{2,1,0:T(4,128)S(1)}, u32[]{:S(2)}, u32[]{:S(2)}) collective-permute-start(f32[165,4,128]{2,1,0:T(4,128)S(1)} %get-tuple-element.58), channel_id=1, source_target_pairs={{2,4},{4,2},{3,5},{5,3},{10,12},{12,10},{11,13},{13,11},{18,20},{2... | collective-permute-start | bytes 1013768 | tf_op jit(solution)/shard_map/ppermute | solution.py:701
  7.1 1.6 %collective-permute-start = (f32[20,32,128]{2,1,0:T(8,128)S(1)}, f32[20,32,128]{2,1,0:T(8,128)S(1)}, u32[]{:S(2)}, u32[]{:S(2)}) collective-permute-start(f32[20,32,128]{2,1,0:T(8,128)S(1)} %get-tuple-element.55), channel_id=1, source_target_pairs={{0,8},{8,0},{16,24},{24,16},{1,9},{9,1},{17,25},{25,17},{2,10},{10... | collective-permute-start | bytes 983048 | tf_op jit(solution)/shard_map/ppermute | solution.py:701
  8.7 0.7 %collective-permute-start.1 = (f32[20,32,128]{2,1,0:T(8,128)S(1)}, f32[20,32,128]{2,1,0:T(8,128)S(1)}, u32[]{:S(2)}, u32[]{:S(2)}) collective-permute-start(f32[20,32,128]{2,1,0:T(8,128)S(1)} %get-tuple-element.56), channel_id=1, source_target_pairs={{8,16},{16,8},{9,17},{17,9},{10,18},{18,10},{11,19},{19,11},{12,20... | collective-permute-start | bytes 983048 | tf_op jit(solution)/shard_map/ppermute | solution.py:701
  9.3 5.0 %collective-permute-done.2.refs_0_ = f32[165,4,128]{2,1,0:T(4,128)S(1)} collective-permute-done((f32[165,4,128]{2,1,0:T(4,128)S(1)}, f32[165,4,128]{2,1,0:T(4,128)S(1)}, u32[]{:S(2)}, u32[]{:S(2)}) %collective-permute-start.2) | collective-permute-done | bytes 337952 | tf_op jit(solution)/shard_map/ppermute | solution.py:701
  14.4 0.0 collective-permute-done.3.refs_1_
  14.4 0.0 copy-done
  14.4 5.7 %inner_first.1 = (f32[2,40,40,128]{3,2,1,0:T(8,128)S(1)}, f32[2,40,40,128]{3,2,1,0:T(8,128)S(1)}, f32[32,40,128]{2,1,0:T(8,128)S(1)}, f32[5,40,128]{2,1,0:T(8,12...) custom-call(f32[2]{0:T(128)S(1)} %copy-done, ...), custom_call_target="tpu_custom_call", output_to_operand_aliasing={{0}: (3, {}), {1}: (4, {}), {2}: (5, {}), {3}: (6, {})} | custom-call | tf_op jit(solution)/shard_map/inner_first/pallas_call | solution.py:443
  20.0 1.7 %collective-permute-start.4 = (f32[20,8,128]{2,1,0:T(8,128)S(1)}, f32[20,8,128]{2,1,0:T(8,128)S(1)}, u32[]{:S(2)}, u32[]{:S(2)}) collective-permute-start(f32[20,8,128]{2,1,0:T(8,128)S(1)} %get-tuple-element.63), channel_id=1, source_target_pairs={{0,8},{8,0},{16,24},{24,16},{1,9},{9,1},{17,25},{25,17},{2,10},{10... | collective-permute-start | bytes 245768 | tf_op jit(solution)/shard_map/ppermute | solution.py:701
  21.8 0.7 %collective-permute-start.5 = (f32[20,8,128]{2,1,0:T(8,128)S(1)}, f32[20,8,128]{2,1,0:T(8,128)S(1)}, u32[]{:S(2)}, u32[]{:S(2)}) collective-permute-start(f32[20,8,128]{2,1,0:T(8,128)S(1)} %get-tuple-element.64), channel_id=1, source_target_pairs={{8,16},{16,8},{9,17},{17,9},{10,18},{18,10},{11,19},{19,11},{12,20... | collective-permute-start | bytes 245768 | tf_op jit(solution)/shard_map/ppermute | solution.py:701
  22.4 5.0 %inner_second.1 = (f32[2,40,40,128]{3,2,1,0:T(8,128)S(1)}, f32[2,40,40,128]{3,2,1,0:T(8,128)S(1)}, f32[2,40,40,128]{3,2,1,0:T(8,128)S(1)}, f32[2,40,40,128]{3,2,...) custom-call(f32[2]{0:T(128)S(1)} %copy-done, ...), custom_call_target="tpu_custom_call", output_to_operand_aliasing={{0}: (5, {}), {1}: (6, {}), {2}: (7, {}), {3}: (8, {}), {4}... | custom-call | tf_op jit(solution)/shard_map/inner_second/pallas_call | solution.py:461
  27.4 0.0 collective-permute-done.xe
  27.4 0.0 collective-permute-done.1.xo
  27.4 0.0 collective-permute-done.4.ce
  27.5 0.0 collective-permute-done.5.co
  27.5 3.6 %edge_part.1 = (f32[2,40,40,128]{3,2,1,0:T(8,128)S(1)}, f32[2,40,40,128]{3,2,1,0:T(8,128)S(1)}, f32[2,40,40,128]{3,2,1,0:T(8,128)S(1)}, f32[2,40,40,128]{3,2,1,0...) custom-call(f32[2]{0:T(128)S(1)} %copy-done, ...), custom_call_target="tpu_custom_call", output_to_operand_aliasing={{0}: (5, {}), {1}: (6, {}), {2}: (7, {}), {3}: (8, {}), {4}... | custom-call | tf_op jit(solution)/shard_map/edge_part/pallas_call | solution.py:585
  31.1 18.1 %all_to_all.5.sums = f32[16,8,128]{2,1,0:T(8,128)S(1)} all-to-all(f32[16,8,128]{2,1,0:T(8,128)S(1)} %get-tuple-element.97), channel_id=1, replica_groups=mesh['gx'=4,'gy'=4,'af'=2] {'gx','gy'}, dimensions={0} | all-to-all | bytes 131072 | tf_op jit(solution)/shard_map/all_to_all | solution.py:717
  49.1 1.7 %gradient_part.1 = f32[32,32,128]{2,1,0:T(8,128)S(1)} custom-call(f32[2]{0:T(128)S(1)} %copy-done, f32[16,8,128]{2,1,0:T(8,128)S(1)} %all_to_all.5.sums, f32[2,40,40,128]{3,2,1,0:T(8,128)S(1)} %get-tuple-element.102.refs_0_, f32[2,40,40,128]{3,2,1,0:T(8,128)S(1)} %get-tuple-element.98.refs_0_.refs_1_, f32[2,40,40,128]{3,2,1,0:T(8,128)S(1)} %get-tuple-element.103.refs_2_, ...), custom_call_target="tpu_custom_call" | custom-call | tf_op jit(solution)/shard_map/gradient_part/pallas_call | solution.py:673
  50.8 0.1 collective-permute-start.6
  50.9 1.7 %wavefield.1 = f32[2,2,32,32,128]{4,3,2,1,0:T(8,128)} custom-call(f32[16,8,128]{2,1,0:T(8,128)S(1)} %all_to_all.5.sums, f32[2,40,40,128]{3,2,1,0:T(8,128)S(1)} %get-tuple-element.98.refs_0_.refs_1_, f32[2,40,40,128]{3,2,1,0:T(8,128)S(1)} %get-tuple-element.99.refs_1_.refs_3_, f32[2,40,40,128]{3,2,1,0:T(8,128)S(1)} %get-tuple-element.100.refs_2_.refs_6_, ...), custom_call_target="tpu_custom_call" | custom-call | tf_op jit(solution)/shard_map/wavefield/pallas_call | solution.py:681
  52.6 0.1 collective-permute-done.6
  52.8 0.9 %add.3 = f32[32,32,128]{2,1,0:T(8,128)} add(f32[32,32,128]{2,1,0:T(8,128)S(1)} %gradient_part.1, f32[32,32,128]{2,1,0:T(8,128)S(1)} %collective-permute-done.6) | non-fusion elementwise | flops 131072 | bytes 1572864 | tf_op jit(solution)/shard_map/add | solution.py:720
Async XLA Ops:
  0.6 13.7 %copy-start = (f32[2]{0:T(128)S(1)}, f32[2]{0:T(128)}, u32[]{:S(2)}) copy-start(f32[2]{0:T(128)} %freq_sq.7) | copy-start | bytes 28
  3.3 11.0 %collective-permute-start.2 = (f32[165,4,128]{2,1,0:T(4,128)S(1)}, f32[165,4,128]{2,1,0:T(4,128)S(1)}, u32[]{:S(2)}, u32[]{:S(2)}) collective-permute-start(f32[165,4,128]{2,1,0:T(4,128)S(1)} %get-tuple-element.57), channel_id=1, source_target_pairs={{0,2},{2,0},{4,6},{6,4},{1,3},{3,1},{5,7},{7,5},{8,10},{10,8},{12,... | collective-permute-start | bytes 1013768 | tf_op jit(solution)/shard_map/ppermute | solution.py:701
  6.4 7.9 %collective-permute-start.3 = (f32[165,4,128]{2,1,0:T(4,128)S(1)}, f32[165,4,128]{2,1,0:T(4,128)S(1)}, u32[]{:S(2)}, u32[]{:S(2)}) collective-permute-start(f32[165,4,128]{2,1,0:T(4,128)S(1)} %get-tuple-element.58), channel_id=1, source_target_pairs={{2,4},{4,2},{3,5},{5,3},{10,12},{12,10},{11,13},{13,11},{18,20},{2... | collective-permute-start | bytes 1013768 | tf_op jit(solution)/shard_map/ppermute | solution.py:701
  7.1 20.3 %collective-permute-start = (f32[20,32,128]{2,1,0:T(8,128)S(1)}, f32[20,32,128]{2,1,0:T(8,128)S(1)}, u32[]{:S(2)}, u32[]{:S(2)}) collective-permute-start(f32[20,32,128]{2,1,0:T(8,128)S(1)} %get-tuple-element.55), channel_id=1, source_target_pairs={{0,8},{8,0},{16,24},{24,16},{1,9},{9,1},{17,25},{25,17},{2,10},{10... | collective-permute-start | bytes 983048 | tf_op jit(solution)/shard_map/ppermute | solution.py:701
  8.7 18.8 %collective-permute-start.1 = (f32[20,32,128]{2,1,0:T(8,128)S(1)}, f32[20,32,128]{2,1,0:T(8,128)S(1)}, u32[]{:S(2)}, u32[]{:S(2)}) collective-permute-start(f32[20,32,128]{2,1,0:T(8,128)S(1)} %get-tuple-element.56), channel_id=1, source_target_pairs={{8,16},{16,8},{9,17},{17,9},{10,18},{18,10},{11,19},{19,11},{12,20... | collective-permute-start | bytes 983048 | tf_op jit(solution)/shard_map/ppermute | solution.py:701
  20.0 7.4 %collective-permute-start.4 = (f32[20,8,128]{2,1,0:T(8,128)S(1)}, f32[20,8,128]{2,1,0:T(8,128)S(1)}, u32[]{:S(2)}, u32[]{:S(2)}) collective-permute-start(f32[20,8,128]{2,1,0:T(8,128)S(1)} %get-tuple-element.63), channel_id=1, source_target_pairs={{0,8},{8,0},{16,24},{24,16},{1,9},{9,1},{17,25},{25,17},{2,10},{10... | collective-permute-start | bytes 245768 | tf_op jit(solution)/shard_map/ppermute | solution.py:701
  21.8 5.7 %collective-permute-start.5 = (f32[20,8,128]{2,1,0:T(8,128)S(1)}, f32[20,8,128]{2,1,0:T(8,128)S(1)}, u32[]{:S(2)}, u32[]{:S(2)}) collective-permute-start(f32[20,8,128]{2,1,0:T(8,128)S(1)} %get-tuple-element.64), channel_id=1, source_target_pairs={{8,16},{16,8},{9,17},{17,9},{10,18},{18,10},{11,19},{19,11},{12,20... | collective-permute-start | bytes 245768 | tf_op jit(solution)/shard_map/ppermute | solution.py:701
  50.8 2.0 %collective-permute-start.6 = (f32[32,32,128]{2,1,0:T(8,128)S(1)}, f32[32,32,128]{2,1,0:T(8,128)S(1)}, u32[]{:S(2)}, u32[]{:S(2)}) collective-permute-start(f32[32,32,128]{2,1,0:T(8,128)S(1)} %gradient_part.1), channel_id=1, source_target_pairs={{0,1},{1,0},{2,3},{3,2},{4,5},{5,4},{6,7},{7,6},{8,9},{9,8},{10,11... | collective-permute-start | bytes 1572872 | tf_op jit(solution)/shard_map/ppermute | solution.py:720

commit v3 on v2

--- a/solution.py
+++ b/solution.py
@@ -694,11 +694,21 @@
 
 
 def swap(cells, axis, odd):
-    count = lax.axis_size(axis)
+    names = ("gx", "gy", "af")
+    sizes = [lax.axis_size(name) for name in names]
+    along = names.index(axis)
     pairs = []
-    for i in range(odd, count - 1, 2):
-        pairs += [(i, i + 1), (i + 1, i)]
-    return lax.ppermute(cells, axis, pairs)
+    for flat in range(sizes[0] * sizes[1] * sizes[2]):
+        place = [flat // (sizes[1] * sizes[2]), flat // sizes[2] % sizes[1], flat % sizes[2]]
+        mate = ((place[along] + odd) ^ 1) - odd
+        if 0 <= mate < sizes[along]:
+            place[along] = mate
+        elif sizes[2] % 2 == 0:
+            place[2] ^= 1
+        else:
+            continue
+        pairs.append((flat, (place[0] * sizes[1] + place[1]) * sizes[2] + place[2]))
+    return lax.ppermute(cells, names, pairs)
 
 
 def on_device(model, freq_sq, source, observed, receiver_depth):

time: 53.9 us -> 50 us (0.928)
  blocking collectives: 18.1 us -> 14.9 us
  starting transfers between devices: 8.43 us -> 6.6 us
  waiting for transfers between devices: 5.18 us -> 6.37 us
    all_to_all x1, blocking collectives: 18.1 us -> 14.9 us  [on_device(): sums = lax.all_to_all(part, ('gx', 'gy'), 0, 0)]
    ppermute x6, starting transfers between devices: 8.36 us -> 6.53 us  [swap(): return lax.ppermute(cells, names, pairs)]
    ppermute x6, waiting for transfers between devices: 5.03 us -> 6.22 us  [swap(): return lax.ppermute(cells, names, pairs)]
  transfers between devices with their start and end apart: 7 -> 7, of which waited for: 2 -> 2; matrix products, arithmetic and copies ran while one was open for 0% -> 0% of each run, Pallas kernels for 23% -> 25%
where the time goes in v3:
time: 50 us; the launch traced here: 49.8 us
  Pallas kernels  20.3 us (41%)
  blocking collectives  14.9 us (30%)
  starting transfers between devices  6.6 us (13%)
  waiting for transfers between devices  6.37 us (13%)
  other arithmetic  0.88 us (2%)
  between operations  0.73 us (1%)
    all_to_all x1, blocking collectives, on_device(): sums = lax.all_to_all(part, ('gx', 'gy'), 0, 0)  14.9 us
    ppermute x6, starting transfers between devices, swap(): return lax.ppermute(cells, names, pairs)  6.53 us
    ppermute x6, waiting for transfers between devices, swap(): return lax.ppermute(cells, names, pairs)  6.22 us
    pallas_call x1, Pallas kernels, inner_part(): pl.pallas_call(functools.partial(inner_kernel, freqs, nx, ny, 0), out_sha...  5.67 us
    pallas_call x1, Pallas kernels, rest(): pl.pallas_call(functools.partial(inner_kernel, freqs, nx, ny, 1), out_sha...  4.96 us
    pallas_call x1, Pallas kernels, edge_part(): pl.pallas_call(functools.partial(edge_kernel, peers, freqs, nx, ny), out_...  3.58 us
    pallas_call x1, Pallas kernels, load(): pl.pallas_call(load_kernel, out_shape=(pltpu.VMEM((2, nx + 2 * HALO, ny +...  2.69 us
    pallas_call x1, Pallas kernels, results(): pl.pallas_call(functools.partial(wave_kernel, freqs, nx, ny), out_shape=j...  1.74 us
  transfers between devices with their start and end apart: 7, of which 2 were waited for; matrix products, arithmetic and copies ran while one was open for 0% of the time, Pallas kernels for 25%

profile of v3, /device:TPU:0, one launch (start us, length us, event | category | flops | bytes accessed | tf_op | source)
XLA Modules:
  0.0 49.8 jit_solution(18359148334966206573)
XLA Ops:
  0.6 0.0 copy-start
  0.6 2.7 %load.1 = (f32[2,40,40,128]{3,2,1,0:T(8,128)S(1)}, f32[2,40,40,128]{3,2,1,0:T(8,128)S(1)}, f32[32,40,128]{2,1,0:T(8,128)S(1)}, f32[5,40,128]{2,1,0:T(8,128)S(1)}...) custom-call(f32[2,2,32,32,128]{4,3,2,1,0:T(8,128)} %source.1, ...), custom_call_target="tpu_custom_call" | custom-call | tf_op jit(solution)/shard_map/load/pallas_call | solution.py:130
  3.3 3.1 %collective-permute-start.2 = (f32[165,4,128]{2,1,0:T(4,128)S(1)}, f32[165,4,128]{2,1,0:T(4,128)S(1)}, u32[]{:S(2)}, u32[]{:S(2)}) collective-permute-start(f32[165,4,128]{2,1,0:T(4,128)S(1)} %get-tuple-element.57), channel_id=1, source_target_pairs={{0,2},{1,3},{2,0},{3,1},{4,6},{5,7},{6,4},{7,5},{8,10},{9,11},{10,... | collective-permute-start | bytes 1013768 | tf_op jit(solution)/shard_map/ppermute | solution.py:711
  6.4 0.0 collective-permute-start.3
  6.4 1.5 %collective-permute-start = (f32[20,32,128]{2,1,0:T(8,128)S(1)}, f32[20,32,128]{2,1,0:T(8,128)S(1)}, u32[]{:S(2)}, u32[]{:S(2)}) collective-permute-start(f32[20,32,128]{2,1,0:T(8,128)S(1)} %get-tuple-element.55), channel_id=1, source_target_pairs={{0,8},{1,9},{2,10},{3,11},{4,12},{5,13},{6,14},{7,15},{8,0},{9,1},... | collective-permute-start | bytes 983048 | tf_op jit(solution)/shard_map/ppermute | solution.py:711
  7.9 0.2 collective-permute-start.1
  8.2 6.2 %collective-permute-done.2.refs_0_ = f32[165,4,128]{2,1,0:T(4,128)S(1)} collective-permute-done((f32[165,4,128]{2,1,0:T(4,128)S(1)}, f32[165,4,128]{2,1,0:T(4,128)S(1)}, u32[]{:S(2)}, u32[]{:S(2)}) %collective-permute-start.2) | collective-permute-done | bytes 337952 | tf_op jit(solution)/shard_map/ppermute | solution.py:711
  14.4 0.0 collective-permute-done.3.refs_1_
  14.4 0.0 copy-done
  14.4 5.7 %inner_first.1 = (f32[2,40,40,128]{3,2,1,0:T(8,128)S(1)}, f32[2,40,40,128]{3,2,1,0:T(8,128)S(1)}, f32[32,40,128]{2,1,0:T(8,128)S(1)}, f32[5,40,128]{2,1,0:T(8,12...) custom-call(f32[2]{0:T(128)S(1)} %copy-done, ...), custom_call_target="tpu_custom_call", output_to_operand_aliasing={{0}: (3, {}), {1}: (4, {}), {2}: (5, {}), {3}: (6, {})} | custom-call | tf_op jit(solution)/shard_map/inner_first/pallas_call | solution.py:443
  20.0 1.7 %collective-permute-start.4 = (f32[20,8,128]{2,1,0:T(8,128)S(1)}, f32[20,8,128]{2,1,0:T(8,128)S(1)}, u32[]{:S(2)}, u32[]{:S(2)}) collective-permute-start(f32[20,8,128]{2,1,0:T(8,128)S(1)} %get-tuple-element.63), channel_id=1, source_target_pairs={{0,8},{1,9},{2,10},{3,11},{4,12},{5,13},{6,14},{7,15},{8,0},{9,1},... | collective-permute-start | bytes 245768 | tf_op jit(solution)/shard_map/ppermute | solution.py:711
  21.8 0.0 collective-permute-start.5
  21.8 5.0 %inner_second.1 = (f32[2,40,40,128]{3,2,1,0:T(8,128)S(1)}, f32[2,40,40,128]{3,2,1,0:T(8,128)S(1)}, f32[2,40,40,128]{3,2,1,0:T(8,128)S(1)}, f32[2,40,40,128]{3,2,...) custom-call(f32[2]{0:T(128)S(1)} %copy-done, ...), custom_call_target="tpu_custom_call", output_to_operand_aliasing={{0}: (5, {}), {1}: (6, {}), {2}: (7, {}), {3}: (8, {}), {4}... | custom-call | tf_op jit(solution)/shard_map/inner_second/pallas_call | solution.py:461
  26.7 0.0 collective-permute-done.xe
  26.7 0.0 collective-permute-done.1.xo
  26.8 0.0 collective-permute-done.4.ce
  26.8 0.0 collective-permute-done.5.co
  26.8 3.6 %edge_part.1 = (f32[2,40,40,128]{3,2,1,0:T(8,128)S(1)}, f32[2,40,40,128]{3,2,1,0:T(8,128)S(1)}, f32[2,40,40,128]{3,2,1,0:T(8,128)S(1)}, f32[2,40,40,128]{3,2,1,0...) custom-call(f32[2]{0:T(128)S(1)} %copy-done, ...), custom_call_target="tpu_custom_call", output_to_operand_aliasing={{0}: (5, {}), {1}: (6, {}), {2}: (7, {}), {3}: (8, {}), {4}... | custom-call | tf_op jit(solution)/shard_map/edge_part/pallas_call | solution.py:585
  30.4 14.9 %all_to_all.5.sums = f32[16,8,128]{2,1,0:T(8,128)S(1)} all-to-all(f32[16,8,128]{2,1,0:T(8,128)S(1)} %get-tuple-element.97), channel_id=1, replica_groups=mesh['gx'=4,'gy'=4,'af'=2] {'gx','gy'}, dimensions={0} | all-to-all | bytes 131072 | tf_op jit(solution)/shard_map/all_to_all | solution.py:727
  45.3 1.7 %gradient_part.1 = f32[32,32,128]{2,1,0:T(8,128)S(1)} custom-call(f32[2]{0:T(128)S(1)} %copy-done, f32[16,8,128]{2,1,0:T(8,128)S(1)} %all_to_all.5.sums, f32[2,40,40,128]{3,2,1,0:T(8,128)S(1)} %get-tuple-element.102.refs_0_, f32[2,40,40,128]{3,2,1,0:T(8,128)S(1)} %get-tuple-element.98.refs_0_.refs_1_, f32[2,40,40,128]{3,2,1,0:T(8,128)S(1)} %get-tuple-element.103.refs_2_, ...), custom_call_target="tpu_custom_call" | custom-call | tf_op jit(solution)/shard_map/gradient_part/pallas_call | solution.py:673
  47.0 0.1 collective-permute-start.6
  47.1 1.7 %wavefield.1 = f32[2,2,32,32,128]{4,3,2,1,0:T(8,128)} custom-call(f32[16,8,128]{2,1,0:T(8,128)S(1)} %all_to_all.5.sums, f32[2,40,40,128]{3,2,1,0:T(8,128)S(1)} %get-tuple-element.98.refs_0_.refs_1_, f32[2,40,40,128]{3,2,1,0:T(8,128)S(1)} %get-tuple-element.99.refs_1_.refs_3_, f32[2,40,40,128]{3,2,1,0:T(8,128)S(1)} %get-tuple-element.100.refs_2_.refs_6_, ...), custom_call_target="tpu_custom_call" | custom-call | tf_op jit(solution)/shard_map/wavefield/pallas_call | solution.py:681
  48.8 0.1 collective-permute-done.6
  49.0 0.9 %add.3 = f32[32,32,128]{2,1,0:T(8,128)} add(f32[32,32,128]{2,1,0:T(8,128)S(1)} %gradient_part.1, f32[32,32,128]{2,1,0:T(8,128)S(1)} %collective-permute-done.6) | non-fusion elementwise | flops 131072 | bytes 1572864 | tf_op jit(solution)/shard_map/add | solution.py:730
Async XLA Ops:
  0.6 13.7 %copy-start = (f32[2]{0:T(128)S(1)}, f32[2]{0:T(128)}, u32[]{:S(2)}) copy-start(f32[2]{0:T(128)} %freq_sq.7) | copy-start | bytes 28
  3.3 11.0 %collective-permute-start.2 = (f32[165,4,128]{2,1,0:T(4,128)S(1)}, f32[165,4,128]{2,1,0:T(4,128)S(1)}, u32[]{:S(2)}, u32[]{:S(2)}) collective-permute-start(f32[165,4,128]{2,1,0:T(4,128)S(1)} %get-tuple-element.57), channel_id=1, source_target_pairs={{0,2},{1,3},{2,0},{3,1},{4,6},{5,7},{6,4},{7,5},{8,10},{9,11},{10,... | collective-permute-start | bytes 1013768 | tf_op jit(solution)/shard_map/ppermute | solution.py:711
  6.4 7.9 %collective-permute-start.3 = (f32[165,4,128]{2,1,0:T(4,128)S(1)}, f32[165,4,128]{2,1,0:T(4,128)S(1)}, u32[]{:S(2)}, u32[]{:S(2)}) collective-permute-start(f32[165,4,128]{2,1,0:T(4,128)S(1)} %get-tuple-element.58), channel_id=1, source_target_pairs={{0,1},{1,0},{2,4},{3,5},{4,2},{5,3},{6,7},{7,6},{8,9},{9,8},{10,12... | collective-permute-start | bytes 1013768 | tf_op jit(solution)/shard_map/ppermute | solution.py:711
  6.4 20.3 %collective-permute-start = (f32[20,32,128]{2,1,0:T(8,128)S(1)}, f32[20,32,128]{2,1,0:T(8,128)S(1)}, u32[]{:S(2)}, u32[]{:S(2)}) collective-permute-start(f32[20,32,128]{2,1,0:T(8,128)S(1)} %get-tuple-element.55), channel_id=1, source_target_pairs={{0,8},{1,9},{2,10},{3,11},{4,12},{5,13},{6,14},{7,15},{8,0},{9,1},... | collective-permute-start | bytes 983048 | tf_op jit(solution)/shard_map/ppermute | solution.py:711
  7.9 18.8 %collective-permute-start.1 = (f32[20,32,128]{2,1,0:T(8,128)S(1)}, f32[20,32,128]{2,1,0:T(8,128)S(1)}, u32[]{:S(2)}, u32[]{:S(2)}) collective-permute-start(f32[20,32,128]{2,1,0:T(8,128)S(1)} %get-tuple-element.56), channel_id=1, source_target_pairs={{0,1},{1,0},{2,3},{3,2},{4,5},{5,4},{6,7},{7,6},{8,16},{9,17},{10,... | collective-permute-start | bytes 983048 | tf_op jit(solution)/shard_map/ppermute | solution.py:711
  20.0 6.7 %collective-permute-start.4 = (f32[20,8,128]{2,1,0:T(8,128)S(1)}, f32[20,8,128]{2,1,0:T(8,128)S(1)}, u32[]{:S(2)}, u32[]{:S(2)}) collective-permute-start(f32[20,8,128]{2,1,0:T(8,128)S(1)} %get-tuple-element.63), channel_id=1, source_target_pairs={{0,8},{1,9},{2,10},{3,11},{4,12},{5,13},{6,14},{7,15},{8,0},{9,1},... | collective-permute-start | bytes 245768 | tf_op jit(solution)/shard_map/ppermute | solution.py:711
  21.8 5.0 %collective-permute-start.5 = (f32[20,8,128]{2,1,0:T(8,128)S(1)}, f32[20,8,128]{2,1,0:T(8,128)S(1)}, u32[]{:S(2)}, u32[]{:S(2)}) collective-permute-start(f32[20,8,128]{2,1,0:T(8,128)S(1)} %get-tuple-element.64), channel_id=1, source_target_pairs={{0,1},{1,0},{2,3},{3,2},{4,5},{5,4},{6,7},{7,6},{8,16},{9,17},{10,... | collective-permute-start | bytes 245768 | tf_op jit(solution)/shard_map/ppermute | solution.py:711
  47.0 2.0 %collective-permute-start.6 = (f32[32,32,128]{2,1,0:T(8,128)S(1)}, f32[32,32,128]{2,1,0:T(8,128)S(1)}, u32[]{:S(2)}, u32[]{:S(2)}) collective-permute-start(f32[32,32,128]{2,1,0:T(8,128)S(1)} %gradient_part.1), channel_id=1, source_target_pairs={{0,1},{1,0},{2,3},{3,2},{4,5},{5,4},{6,7},{7,6},{8,9},{9,8},{10,11... | collective-permute-start | bytes 1572872 | tf_op jit(solution)/shard_map/ppermute | solution.py:730

commit v4 on v3

--- a/solution.py
+++ b/solution.py
@@ -161,114 +161,121 @@
 class Grid:
     def __init__(self, nx, ny, nz):
         self.nx, self.ny, self.nz = nx, ny, nz
-        self.xe, self.ye = nx + 2 * HALO, ny + 2 * HALO
-        self.tiles = self.ye // 8
+        self.xe = nx + 2 * HALO
+        self.tiles = ny // 8
+        self.own = range(self.tiles)
+        self.both = range(self.tiles + 1)
         lane = lax.broadcasted_iota(jnp.int32, (8, nz), 1)
         self.first = lane == 0
         self.last = lane == nz - 1
         self.depths = lane.astype(F32)
-        self.sub = lax.broadcasted_iota(jnp.int32, (8, nz), 0)
+        sub = lax.broadcasted_iota(jnp.int32, (8, nz), 0)
+        self.top = sub == 7
+        self.bottom = sub == 0
         has_left = lax.axis_index("gy") > 0
         has_right = lax.axis_index("gy") < lax.axis_size("gy") - 1
-        self.cut_left = jnp.where(
-            self.sub == 0, jnp.where(has_left, 1.0, 0.0), jnp.ones((8, nz), F32)
-        )
-        self.cut_tile = (ny - 1) % self.tiles
-        self.cut_right = jnp.where(
-            self.sub == (ny - 1) // self.tiles,
-            jnp.where(has_right, 1.0, 0.0),
-            jnp.ones((8, nz), F32),
-        )
-        self.groups = {}
-        for t in range(self.tiles):
-            owned = -((t - ny) // self.tiles)
-            self.groups.setdefault(owned, []).append(t)
-
-    def rows(self, ref, p, i):
-        return [
-            ref[p, i, pl.ds(t, 8, stride=self.tiles), :] for t in range(self.tiles)
-        ]
-
-    def put(self, ref, p, i, values):
-        for t in range(self.tiles):
-            ref[p, i, pl.ds(t, 8, stride=self.tiles), :] = values[t]
+        self.left = jnp.where(has_left, 1.0, 0.0)
+        self.right = jnp.where(has_right, 1.0, 0.0)
+
+    def tile(self, t):
+        if t < self.tiles:
+            return pl.ds(t, 8, stride=self.tiles)
+        return pl.ds(self.ny, 8)
+
+    def rows(self, ref, p, i, tiles):
+        return [ref[p, i, self.tile(t), :] for t in tiles]
+
+    def put(self, ref, p, i, values, tiles):
+        for t in tiles:
+            ref[p, i, self.tile(t), :] = values[t]
 
     def beside(self, mid):
+        left = jnp.where(self.first, 0.0, pltpu.roll(mid, 1, axis=1))
+        right = jnp.where(self.last, 0.0, pltpu.roll(mid, self.nz - 1, axis=1))
+        return left + right
+
+    def around(self, mid, below, above, tiles):
+        n = self.tiles
+        halo = mid[n] if len(mid) > n else None
+        first_up = pltpu.roll(mid[0], 7, axis=0)
+        last_down = pltpu.roll(mid[n - 1], 1, axis=0)
+        if halo is not None:
+            halo_up = pltpu.roll(halo, 7, axis=0)
+            halo_down = pltpu.roll(halo, 1, axis=0)
+        total = {}
+        for t in tiles:
+            if t == n:
+                up = jnp.where(self.top, first_up, halo_up)
+                down = jnp.where(self.bottom, last_down, halo_down)
+            else:
+                up = mid[t + 1] if t + 1 < n else None
+                down = mid[t - 1] if t else None
+                if up is None:
+                    edge = 0.0 if halo is None else halo_up * self.right
+                    up = jnp.where(self.top, edge, first_up)
+                if down is None:
+                    edge = 0.0 if halo is None else halo_down * self.left
+                    down = jnp.where(self.bottom, edge, last_down)
+            total[t] = ((below[t] + above[t]) + (up + down)) + self.beside(mid[t])
+        return total
+
+    def apply(self, src, i, lo, hi, sign, coef, tiles, wide=True, cut=None):
+        cr, ci = coef
+        mids, totals = [], []
+        for p in range(2):
+            mid = self.rows(src, p, i, self.both if wide else self.own)
+            below = {t: src[p, lo, self.tile(t), :] for t in tiles}
+            above = {t: src[p, hi, self.tile(t), :] for t in tiles}
+            if cut is not None and cut[0] < 0:
+                below = {t: v * cut[1] for t, v in below.items()}
+            if cut is not None and cut[0] > 0:
+                above = {t: v * cut[1] for t, v in above.items()}
+            mids.append(mid)
+            totals.append(self.around(mid, below, above, tiles))
+        out_re, out_im = {}, {}
+        for t in tiles:
+            re, im = mids[0][t], mids[1][t]
+            if sign > 0:
+                out_re[t] = cr[t] * re - ci[t] * im - totals[0][t]
+                out_im[t] = cr[t] * im + ci[t] * re - totals[1][t]
+            else:
+                out_re[t] = cr[t] * re + ci[t] * im - totals[0][t]
+                out_im[t] = cr[t] * im - ci[t] * re - totals[1][t]
+        return mids, out_re, out_im
+
+    def squares(self, re, im):
+        return {t: re[t] * re[t] + im[t] * im[t] for t in self.own}
+
+    def gather(self, values):
+        return functools.reduce(jnp.add, [values[t] for t in self.own])
+
+    def zero(self):
+        return jnp.zeros((8, self.nz), F32)
+
+    def prepare(self, i, tiles, freq_sq, w, many, cell, column):
+        fields = 2 * len(many)
+        weight = {}
+        for t in tiles:
+            depth = column(fields, t)
+            weight[t] = jnp.where(self.depths == depth, penalty, 0.0)
+            w[i, t] = weight[t]
         out = []
-        for t in range(self.tiles):
-            left = jnp.where(self.first, 0.0, pltpu.roll(mid[t], 1, axis=1))
-            right = jnp.where(self.last, 0.0, pltpu.roll(mid[t], self.nz - 1, axis=1))
-            out.append(left + right)
+        for f, field in enumerate(many):
+            for t in tiles:
+                scaled = freq_sq[f] * cell(t)
+                field.cr[i, t] = 6.0 - scaled
+                field.ci[i, t] = attenuation * scaled
+            out.append(
+                [
+                    {t: weight[t] * column(2 * f + p, t) for t in tiles}
+                    for p in range(2)
+                ]
+            )
         return out
 
-    def around(self, mid, below, above, beside):
-        total = []
-        n = self.tiles
-        for t in range(n):
-            up = mid[t + 1] if t + 1 < n else pltpu.roll(mid[0], 7, axis=0)
-            down = mid[t - 1] if t else pltpu.roll(mid[n - 1], 1, axis=0)
-            if t == 0:
-                down = down * self.cut_left
-            if t == self.cut_tile:
-                up = up * self.cut_right
-            total.append(((below[t] + above[t]) + (up + down)) + beside[t])
-        return total
-
-    def apply(self, src, i, lo, hi, sign, coef, mid_im, beside_im, cut=None):
-        cr, ci = coef
-        mid_re = self.rows(src, 0, i)
-        total = []
-        for p, mid, beside in (
-            (0, mid_re, self.beside(mid_re)),
-            (1, mid_im, beside_im),
-        ):
-            below, above = self.rows(src, p, lo), self.rows(src, p, hi)
-            if cut is not None and cut[0] < 0:
-                below = [b * cut[1] for b in below]
-            if cut is not None and cut[0] > 0:
-                above = [a * cut[1] for a in above]
-            total.append(self.around(mid, below, above, beside))
-        out_re, out_im = [], []
-        for t in range(self.tiles):
-            re, im = mid_re[t], mid_im[t]
-            if sign > 0:
-                out_re.append(cr[t] * re - ci[t] * im - total[0][t])
-                out_im.append(cr[t] * im + ci[t] * re - total[1][t])
-            else:
-                out_re.append(cr[t] * re + ci[t] * im - total[0][t])
-                out_im.append(cr[t] * im - ci[t] * re - total[1][t])
-        return out_re, out_im
-
-    def squares(self, re, im):
-        return [re[t] * re[t] + im[t] * im[t] for t in range(self.tiles)]
-
-    def gather(self, acc, values):
-        return tuple(
-            a + functools.reduce(jnp.add, [values[t] for t in ts])
-            for a, ts in zip(acc, self.groups.values())
-        )
-
-    def zero(self):
-        return tuple(jnp.zeros((8, self.nz), F32) for _ in self.groups)
-
-    def total(self, acc):
-        return functools.reduce(
-            jnp.add,
-            [jnp.where(self.sub < n, a, 0.0) for a, n in zip(acc, self.groups)],
-        )
-
-    def tile_list(self, ref, i):
-        return [ref[i, t] for t in range(self.tiles)]
-
-    def weigh(self, i, w, depth):
-        for t in range(self.tiles):
-            w[i, t] = jnp.where(self.depths == depth[t], penalty, 0.0)
-
-    def coefs(self, i, freq_sq, cells, cr, ci):
-        for t in range(self.tiles):
-            scaled = freq_sq * cells[t]
-            cr[i, t] = 6.0 - scaled
-            ci[i, t] = attenuation * scaled
+    def pick(self, ref, lead, t, lane):
+        at = jnp.full((8, self.nz), lane, jnp.int32)
+        return jnp.take_along_axis(ref[lead, self.tile(t), :], at, axis=1)
 
 
 class Field:
@@ -277,39 +284,119 @@
         self.s, self.v0, self.u0, self.v1, self.u1, self.cr, self.ci = refs
         self.w = w
 
-    def source_of(self, stage):
-        return (self.s, self.v0, self.u0, self.v1)[stage]
-
-    def target_of(self, stage):
-        return (self.v0, self.u0, self.v1, self.u1)[stage]
-
-    def step(self, stage, i, lo, hi, mid_im, beside_im, terms=None, cut=None, acc=None):
+    def coef(self, i, tiles):
+        return {t: self.cr[i, t] for t in tiles}, {t: self.ci[i, t] for t in tiles}
+
+    def finish(self, i, tiles, wide, lo=None, hi=None, cut=None):
         g = self.grid
-        tiles = range(g.tiles)
-        coef = (g.tile_list(self.cr, i), g.tile_list(self.ci, i))
-        sign = -1 if stage in (0, 2) else 1
-        re, im = g.apply(
-            self.source_of(stage), i, lo, hi, sign, coef, mid_im, beside_im, cut
-        )
-        weight = g.tile_list(self.w, i) if stage in (0, 2) else None
-        if stage == 0:
-            re = [re[t] + terms[0][t] for t in tiles]
-            im = [im[t] + terms[1][t] for t in tiles]
+        _, re, im = g.apply(self.s, i, lo, hi, -1, self.coef(i, tiles), tiles, wide, cut)
+        for p, value in enumerate((re, im)):
+            for t in tiles:
+                at = g.tile(t)
+                self.v0[p, i, at, :] = self.v0[p, i, at, :] + value[t]
+
+    def first_halo(self, i, terms):
+        g = self.grid
+        n = g.tiles
+        coef = self.coef(i, [n])
+        _, re, im = g.apply(self.s, i, i - 1, i + 1, -1, coef, [n])
+        for p, value in enumerate((re, im)):
+            self.v0[p, i, g.tile(n), :] = value[n] + terms[p][n]
+            halo = self.s[p, i, g.tile(n), :]
+            low = jnp.where(g.bottom, pltpu.roll(halo, 1, axis=0) * g.left, 0.0)
+            high = jnp.where(g.top, pltpu.roll(halo, 7, axis=0) * g.right, 0.0)
+            for t, change in ((0, low), (n - 1, high)):
+                at = g.tile(t)
+                self.v0[p, i, at, :] = self.v0[p, i, at, :] - change
+
+    def step(self, stage, i, lo, hi, cut=None, acc=None):
+        g = self.grid
+        src = (None, self.v0, self.u0, self.v1)[stage]
+        dst = (None, self.u0, self.v1, self.u1)[stage]
+        tiles = g.own if stage == 3 else g.both
+        sign = -1 if stage == 2 else 1
+        mids, re, im = g.apply(src, i, lo, hi, sign, self.coef(i, tiles), tiles, True, cut)
+        if stage != 3:
+            weight = {t: self.w[i, t] for t in tiles}
         if stage == 2:
-            old_re, old_im = g.rows(self.v0, 0, i), g.rows(self.v0, 1, i)
-            re = [re[t] + weight[t] * old_re[t] for t in tiles]
-            im = [im[t] + weight[t] * old_im[t] for t in tiles]
-        g.put(self.target_of(stage), 0, i, re)
-        g.put(self.target_of(stage), 1, i, im)
+            for p, out in enumerate((re, im)):
+                for t in tiles:
+                    out[t] = out[t] + weight[t] * self.v0[p, i, g.tile(t), :]
+        g.put(dst, 0, i, re, tiles)
+        g.put(dst, 1, i, im, tiles)
         if acc is None:
             return None
         acc = list(acc)
         squares = g.squares(re, im)
-        acc[stage] = g.gather(acc[stage], squares)
-        if stage in (0, 2):
-            weighted = [weight[t] * squares[t] for t in tiles]
-            acc[stage + 1] = g.gather(acc[stage + 1], weighted)
+        acc[stage] = acc[stage] + g.gather(squares)
+        if stage == 1:
+            squares = g.squares(*mids)
+            acc[0] = acc[0] + g.gather(squares)
+        if stage != 3:
+            at = 1 if stage == 1 else 3
+            weighted = {t: weight[t] * squares[t] for t in g.own}
+            acc[at] = acc[at] + g.gather(weighted)
         return tuple(acc)
+
+
+def early_kernel(freqs, nx, ny, freq_sq, *refs):
+    s, (cells, aux), refs = refs[:freqs], refs[freqs : freqs + 2], refs[freqs + 2 :]
+    w = refs[3 * freqs]
+    nz = cells.shape[2]
+    grid = Grid(nx, ny, nz)
+    many = [
+        Field(grid, (s[f], refs[3 * f], None, None, None, *refs[3 * f + 1 : 3 * f + 3]), w)
+        for f in range(freqs)
+    ]
+
+    def prepare(i):
+        return grid.prepare(
+            i,
+            grid.own,
+            freq_sq,
+            w,
+            many,
+            lambda t: cells[i, grid.tile(t), :],
+            lambda k, t: grid.pick(aux, k, t, i),
+        )
+
+    for i in (0, nx - 1):
+        terms = prepare(i)
+        for f in range(freqs):
+            for p in range(2):
+                grid.put(many[f].v0, p, i, terms[f][p], grid.own)
+
+    def row(i):
+        terms = prepare(i)
+        for f in range(freqs):
+            field = many[f]
+            _, re, im = grid.apply(
+                field.s, i, i - 1, i + 1, -1, field.coef(i, grid.own), grid.own, False
+            )
+            for p, value in enumerate((re, im)):
+                value = {t: value[t] + terms[f][p][t] for t in grid.own}
+                grid.put(field.v0, p, i, value, grid.own)
+
+    def pair(k, _):
+        row(2 * k + 1)
+        row(2 * k + 2)
+        return 0
+
+    lax.fori_loop(0, (nx - 2) // 2, pair, 0)
+
+
+def early(nx, ny, freq_sq, s, cells, aux):
+    freqs = len(s)
+    _, xe, _, nz = s[0].shape
+    field = pltpu.VMEM(s[0].shape, F32)
+    coef = pltpu.VMEM((xe, ny // 8 + 1, 8, nz), F32)
+    return pl.pallas_call(
+        functools.partial(early_kernel, freqs, nx, ny),
+        out_shape=(field, coef, coef) * freqs + (coef,),
+        in_specs=[SMEM] + [VMEM] * (freqs + 2),
+        compiler_params=params(8),
+        name="early",
+    )(freq_sq, *s, cells, aux)
 
 
 def corner_faces(freqs, nx, ny, s, cells, aux, ce, co, slab, sem):
@@ -339,16 +426,25 @@
 def inner_kernel(freqs, nx, ny, half, freq_sq, *refs):
     if half == 0:
         ye, yo = refs[:2]
-        refs = refs[2 + freqs + 2 :]
+        count = 4 * freqs + 3
+        refs = refs[2 + count :]
         s, (cells, aux), refs = refs[:freqs], refs[freqs : freqs + 2], refs[freqs + 2 :]
-        state, (w, moments, ce, co, slab, sem) = refs[: 6 * freqs], refs[6 * freqs :]
+        known, refs = refs[: 3 * freqs + 1], refs[3 * freqs + 1 :]
+        news, (moments, ce, co, slab, sem) = refs[: 3 * freqs], refs[3 * freqs :]
     else:
-        (cells, aux), s = refs[:2], refs[2 : 2 + freqs]
-        partial = refs[2 + freqs + 6 * freqs + 1]
-        refs = refs[2 + 7 * freqs + 2 :]
-        state, (w, moments) = refs[: 6 * freqs], refs[6 * freqs :]
-    nz = cells.shape[2]
+        s, known = refs[:freqs], refs[freqs : 4 * freqs + 1]
+        partial = refs[7 * freqs + 1]
+        refs = refs[7 * freqs + 2 :]
+        news, (moments,) = refs[: 3 * freqs], refs[3 * freqs :]
+    nz = s[0].shape[3]
     fields = 2 * freqs
+    w = known[3 * freqs]
+    grid = Grid(nx, ny, nz)
+    many = []
+    for f in range(freqs):
+        v0, cr, ci = known[3 * f : 3 * f + 3]
+        u0, v1, u1 = news[3 * f : 3 * f + 3]
+        many.append(Field(grid, (s[f], v0, u0, v1, u1, cr, ci), w))
     if half == 0:
         copies = Copies(sem.at[0])
         for yb, at in zip((ye, yo), halo_places(ny)):
@@ -362,84 +458,74 @@
                     yb.at[pl.ds(k * nx, nx)],
                     s[k // 2].at[k % 2, pl.ds(0, nx), rows, :],
                 )
-    grid = Grid(nx, ny, nz)
-    if half == 0:
         copies.wait()
         out = corner_faces(freqs, nx, ny, s, cells, aux, ce, co, slab, sem.at[1])
-    tiles = grid.tiles
-    many = [Field(grid, (s[f], *state[6 * f : 6 * f + 6]), w) for f in range(freqs)]
 
     def prepare(i):
-        def column(k):
-            pick = jnp.full((8, nz), i, jnp.int32)
-            return [
-                jnp.take_along_axis(
-                    aux[k, pl.ds(t, 8, stride=tiles), :], pick, axis=1
-                )
-                for t in range(tiles)
-            ]
-
-        rows = [cells[i, pl.ds(t, 8, stride=tiles), :] for t in range(tiles)]
-        grid.weigh(i, w, column(fields))
-        weight = grid.tile_list(w, i)
-        out = []
-        for f in range(freqs):
-            grid.coefs(i, freq_sq[f], rows, many[f].cr, many[f].ci)
-            terms = []
-            for p in range(2):
-                seen = column(2 * f + p)
-                terms.append([weight[t] * seen[t] for t in range(tiles)])
-            out.append(terms)
-        return out
+        return grid.prepare(
+            i,
+            [grid.tiles],
+            freq_sq,
+            w,
+            many,
+            lambda t: cells[i, grid.tile(t), :],
+            lambda k, t: grid.pick(aux, k, t, i),
+        )
 
     if half == 0:
         for i in (0, nx - 1):
             terms = prepare(i)
             for f in range(freqs):
                 for p in range(2):
-                    grid.put(many[f].v0, p, i, terms[f][p])
+                    grid.put(many[f].v0, p, i, terms[f][p], [grid.tiles])
 
     def step(j, acc, active):
         acc = list(acc)
         for k in reversed(active):
             i = j - 2 * k
-            terms = prepare(i) if k == 0 else [None] * freqs
+            if k == 0:
+                terms = prepare(i)
             for f in range(freqs):
-                mid = grid.rows(many[f].source_of(k), 1, i)
-                acc[f] = many[f].step(
-                    k, i, i - 1, i + 1, mid, grid.beside(mid), terms[f], acc=acc[f]
-                )
+                if k == 0:
+                    many[f].first_halo(i, terms[f])
+                else:
+                    acc[f] = many[f].step(k, i, i - 1, i + 1, acc=acc[f])
         return tuple(acc)
+
+    def heads(i, _):
+        terms = prepare(i)
+        for f in range(freqs):
+            many[f].first_halo(i, terms[f])
+        return 0
 
     spans = [(1 + 3 * k, nx - 1 + k) for k in range(4)]
     middle = nx // 2 + SHIFT
     edges = sorted({e for span in spans for e in span} | {middle})
     acc = tuple(tuple(grid.zero() for _ in range(4)) for _ in range(freqs))
+    if half == 0:
+        lax.fori_loop(1, nx - 1, heads, 0, unroll=3)
     for lo, hi in zip(edges[:-1], edges[1:]):
         if (lo < middle) != (half == 0):
             continue
-        active = [k for k, (a, b) in enumerate(spans) if a <= lo and hi <= b]
-        acc = lax.fori_loop(lo, hi, functools.partial(step, active=active), acc)
+        active = [k for k, (a, b) in enumerate(spans) if k and a <= lo and hi <= b]
+        if active:
+            acc = lax.fori_loop(lo, hi, functools.partial(step, active=active), acc)
     for f in range(freqs):
         for m in range(4):
-            value = grid.total(acc[f][m])
+            value = acc[f][m]
             moments[f, m] = value if half == 0 else value + partial[f, m]
     if half == 0:
         out.wait()
 
 
-def inner_part(nx, ny, freq_sq, ye, yo, s, cells, aux):
-    _, xe, ye_rows, nz = s[0].shape
+def inner_part(nx, ny, freq_sq, ye, yo, s, cells, aux, known):
     freqs = len(s)
+    nz = cells.shape[2]
     slabs = 2 * freqs * HALO + INNER + 1
     field = pltpu.VMEM(s[0].shape, F32)
-    coef = pltpu.VMEM((xe, ye_rows // 8, 8, nz), F32)
     corner = pltpu.VMEM((slabs, 2 * HALO, nz), F32)
-    kept = (*s, cells, aux)
-    news = ((field,) * 4 + (coef, coef)) * freqs + (
-        coef,
-        pltpu.VMEM((freqs, 4, 8, nz), F32),
-    )
+    kept = (*s, cells, aux, *known)
+    news = (field,) * (3 * freqs) + (pltpu.VMEM((freqs, 4, 8, nz), F32),)
     got = pl.pallas_call(
         functools.partial(inner_kernel, freqs, nx, ny, 0),
         out_shape=tuple(pltpu.VMEM(k.shape, F32) for k in kept)
@@ -454,22 +540,24 @@
         compiler_params=params(8),
         name="inner_first",
     )(freq_sq, ye, yo, *kept)
-    s, cells, aux = got[:freqs], got[freqs], got[freqs + 1]
-    news_got, (ce, co) = got[freqs + 2 : -2], got[-2:]
+    s, known = got[:freqs], got[freqs + 2 : len(kept)]
+    news_got, (ce, co) = got[len(kept) : -2], got[-2:]
 
     def rest():
+        first = 1 + freqs + len(known)
         again = pl.pallas_call(
             functools.partial(inner_kernel, freqs, nx, ny, 1),
             out_shape=news,
-            in_specs=[SMEM] + [VMEM] * (2 + freqs + len(news)),
-            input_output_aliases={3 + freqs + k: k for k in range(len(news))},
+            in_specs=[SMEM] + [VMEM] * (freqs + len(known) + len(news)),
+            input_output_aliases={first + k: k for k in range(len(news))},
             compiler_params=params(8),
             name="inner_second",
-        )(freq_sq, cells, aux, *s, *news_got)
+        )(freq_sq, *s, *known, *news_got)
         state = []
         for f in range(freqs):
-            state += [s[f], *again[6 * f : 6 * f + 6]]
-        return state + [again[-2]], again[-1]
+            v0, cr, ci = known[3 * f : 3 * f + 3]
+            state += [s[f], v0, *again[3 * f : 3 * f + 3], cr, ci]
+        return state + [known[-1]], again[-1]
 
     return ce, co, rest
 
@@ -508,34 +596,22 @@
         )
     grid = Grid(nx, ny, nz)
     copies.wait()
-    tiles = grid.tiles
     many = [Field(grid, state[7 * f : 7 * f + 7], w) for f in range(freqs)]
-
     for half in range(2):
         for layer in range(INNER):
             i = nx + layer if half == 0 else nx + HALO + 1 + layer
-
-            def column(k):
-                pick = jnp.full((8, nz), 8 * k + layer, jnp.int32)
-                return [
-                    jnp.take_along_axis(
-                        aux[half, pl.ds(t, 8, stride=tiles), :], pick, axis=1
-                    )
-                    for t in range(tiles)
-                ]
-
-            rows = [
-                cells[half, layer, pl.ds(t, 8, stride=tiles), :] for t in range(tiles)
-            ]
-            grid.weigh(i, w, column(fields))
-            weight = grid.tile_list(w, i)
+            terms = grid.prepare(
+                i,
+                grid.both,
+                freq_sq,
+                w,
+                many,
+                lambda t: cells[half, layer, grid.tile(t), :],
+                lambda k, t: grid.pick(aux, half, t, 8 * k + layer),
+            )
             for f in range(freqs):
-                grid.coefs(i, freq_sq[f], rows, many[f].cr, many[f].ci)
                 for p in range(2):
-                    seen = column(2 * f + p)
-                    grid.put(
-                        many[f].v0, p, i, [weight[t] * seen[t] for t in range(tiles)]
-                    )
+                    grid.put(many[f].v0, p, i, terms[f][p], grid.both)
 
     left = jnp.where(lax.axis_index("gx") > 0, 1.0, 0.0)
     right = jnp.where(lax.axis_index("gx") < lax.axis_size("gx") - 1, 1.0, 0.0)
@@ -543,15 +619,7 @@
     acc = [tuple(grid.zero() for _ in range(4)) for _ in range(freqs)]
     for stage in range(4):
         for k in range(HALO):
-            jobs = [
-                (x, f)
-                for x in (k - INNER + stage, nx - 1 - stage + k)
-                for f in range(freqs)
-            ]
-            mids = [many[f].source_of(stage) for _, f in jobs]
-            mids = [grid.rows(ref, 1, x % wrap) for ref, (x, _) in zip(mids, jobs)]
-            sums = [grid.beside(mid) for mid in mids]
-            for (x, f), mid, beside in zip(jobs, mids, sums):
+            for x in (k - INNER + stage, nx - 1 - stage + k):
                 i, lo, hi = x % wrap, (x - 1) % wrap, (x + 1) % wrap
                 own = 0 <= x < nx
                 cut = None
@@ -559,19 +627,20 @@
                     cut = (-1, left)
                 if x == nx - 1:
                     cut = (1, right)
-                terms = None
-                if stage == 0:
-                    terms = [grid.rows(many[f].v0, p, i) for p in range(2)]
-                got = many[f].step(
-                    stage, i, lo, hi, mid, beside, terms, cut, acc[f] if own else None
-                )
-                if own:
-                    acc[f] = got
+                for f in range(freqs):
+                    if stage == 0:
+                        many[f].finish(i, grid.both, True, lo, hi, cut)
+                        continue
+                    got = many[f].step(
+                        stage, i, lo, hi, cut, acc[f] if own else None
+                    )
+                    if own:
+                        acc[f] = got
 
     rows = []
     for f in range(freqs):
         for m in range(4):
-            both = grid.total(acc[f][m]) + moments[f, m]
+            both = acc[f][m] + moments[f, m]
             rows.append(jnp.sum(both, axis=0, keepdims=True))
     sums = jnp.sum(jnp.concatenate(rows, axis=0), axis=1, keepdims=True)
     sums = jnp.broadcast_to(sums, (4 * freqs, nz))
@@ -717,7 +786,8 @@
     *s, cells, aux, xe, xo, ye, yo = load(source, model, observed, receiver_depth)
     ye, yo = swap(ye, "gy", 0), swap(yo, "gy", 1)
     xe, xo = swap(xe, "gx", 0), swap(xo, "gx", 1)
-    ce, co, rest = inner_part(nx, ny, freq_sq, ye, yo, s, cells, aux)
+    known = early(nx, ny, freq_sq, s, cells, aux)
+    ce, co, rest = inner_part(nx, ny, freq_sq, ye, yo, s, cells, aux, known)
     ce, co = swap(ce, "gx", 0), swap(co, "gx", 1)
     state, moments = rest()
     peers = lax.axis_size("gx") * lax.axis_size("gy")

time: 50 us -> 48.3 us (0.966)
  waiting for transfers between devices: 6.37 us -> 4.03 us
  Pallas kernels: 20.3 us -> 21.6 us
  blocking collectives: 14.9 us -> 14.4 us
    pallas_call x0 -> x1, Pallas kernels: none -> 3.43 us  [early(): pl.pallas_call(functools.partial(early_kernel, freqs, nx, ny), out_shape=...]
    ppermute x6, waiting for transfers between devices: 6.22 us -> 3.88 us  [swap(): return lax.ppermute(cells, names, pairs)]
    pallas_call x1, Pallas kernels: 4.96 us -> 3.53 us  [rest(): pl.pallas_call(functools.partial(inner_kernel, freqs, nx, ny, 1), out_sha...]
    pallas_call x1, Pallas kernels: 5.67 us -> 4.96 us  [inner_part(): pl.pallas_call(functools.partial(inner_kernel, freqs, nx, ny, 0), out_sha...]
    all_to_all x1, blocking collectives: 14.9 us -> 14.4 us  [on_device(): sums = lax.all_to_all(part, ('gx', 'gy'), 0, 0)]
  transfers between devices with their start and end apart: 7 -> 7, of which waited for: 2 -> 3; matrix products, arithmetic and copies ran while one was open for 0% -> 0% of each run, Pallas kernels for 25% -> 28%
where the time goes in v4:
time: 48.3 us; the launch traced here: 48.2 us
  Pallas kernels  21.6 us (45%)
  blocking collectives  14.4 us (30%)
  starting transfers between devices  6.6 us (14%)
  waiting for transfers between devices  4.03 us (8%)
  other arithmetic  0.87 us (2%)
  between operations  0.72 us (1%)
    all_to_all x1, blocking collectives, on_device(): sums = lax.all_to_all(part, ('gx', 'gy'), 0, 0)  14.4 us
    ppermute x6, starting transfers between devices, swap(): return lax.ppermute(cells, names, pairs)  6.53 us
    pallas_call x1, Pallas kernels, inner_part(): pl.pallas_call(functools.partial(inner_kernel, freqs, nx, ny, 0), out_sha...  4.96 us
    ppermute x6, waiting for transfers between devices, swap(): return lax.ppermute(cells, names, pairs)  3.88 us
    pallas_call x1, Pallas kernels, rest(): pl.pallas_call(functools.partial(inner_kernel, freqs, nx, ny, 1), out_sha...  3.53 us
    pallas_call x1, Pallas kernels, edge_part(): pl.pallas_call(functools.partial(edge_kernel, peers, freqs, nx, ny), out_...  3.45 us
    pallas_call x1, Pallas kernels, early(): pl.pallas_call(functools.partial(early_kernel, freqs, nx, ny), out_shape=...  3.43 us
    pallas_call x1, Pallas kernels, load(): pl.pallas_call(load_kernel, out_shape=(pltpu.VMEM((2, nx + 2 * HALO, ny +...  2.69 us
  transfers between devices with their start and end apart: 7, of which 3 were waited for; matrix products, arithmetic and copies ran while one was open for 0% of the time, Pallas kernels for 28%

profile of v4, /device:TPU:0, one launch (start us, length us, event | category | flops | bytes accessed | tf_op | source)
XLA Modules:
  0.0 48.2 jit_solution(14990722829388173988)
XLA Ops:
  0.6 0.0 copy-start
  0.6 2.7 %load.1 = (f32[2,40,40,128]{3,2,1,0:T(8,128)S(1)}, f32[2,40,40,128]{3,2,1,0:T(8,128)S(1)}, f32[32,40,128]{2,1,0:T(8,128)S(1)}, f32[5,40,128]{2,1,0:T(8,128)S(1)}...) custom-call(f32[2,2,32,32,128]{4,3,2,1,0:T(8,128)} %source.1, ...), custom_call_target="tpu_custom_call" | custom-call | tf_op jit(solution)/shard_map/load/pallas_call | solution.py:130
  3.3 3.1 %collective-permute-start.2 = (f32[165,4,128]{2,1,0:T(4,128)S(1)}, f32[165,4,128]{2,1,0:T(4,128)S(1)}, u32[]{:S(2)}, u32[]{:S(2)}) collective-permute-start(f32[165,4,128]{2,1,0:T(4,128)S(1)} %get-tuple-element.55), channel_id=1, source_target_pairs={{0,2},{1,3},{2,0},{3,1},{4,6},{5,7},{6,4},{7,5},{8,10},{9,11},{10,... | collective-permute-start | bytes 1013768 | tf_op jit(solution)/shard_map/ppermute | solution.py:780
  6.4 0.0 collective-permute-start.3
  6.4 1.5 %collective-permute-start = (f32[20,32,128]{2,1,0:T(8,128)S(1)}, f32[20,32,128]{2,1,0:T(8,128)S(1)}, u32[]{:S(2)}, u32[]{:S(2)}) collective-permute-start(f32[20,32,128]{2,1,0:T(8,128)S(1)} %get-tuple-element.53), channel_id=1, source_target_pairs={{0,8},{1,9},{2,10},{3,11},{4,12},{5,13},{6,14},{7,15},{8,0},{9,1},... | collective-permute-start | bytes 983048 | tf_op jit(solution)/shard_map/ppermute | solution.py:780
  7.9 0.2 collective-permute-start.1
  8.2 0.0 copy-done
  8.2 3.4 %early.1 = (f32[2,40,40,128]{3,2,1,0:T(8,128)S(1)}, f32[40,5,8,128]{3,2,1,0:T(8,128)S(1)}, f32[40,5,8,128]{3,2,1,0:T(8,128)S(1)}, f32[2,40,40,128]{3,2,1,0:T(8,1...) custom-call(f32[2]{0:T(128)S(1)} %copy-done, ...), custom_call_target="tpu_custom_call" | custom-call | tf_op jit(solution)/shard_map/early/pallas_call | solution.py:393
  11.6 2.8 %collective-permute-done.2.refs_0_ = f32[165,4,128]{2,1,0:T(4,128)S(1)} collective-permute-done((f32[165,4,128]{2,1,0:T(4,128)S(1)}, f32[165,4,128]{2,1,0:T(4,128)S(1)}, u32[]{:S(2)}, u32[]{:S(2)}) %collective-permute-start.2) | collective-permute-done | bytes 337952 | tf_op jit(solution)/shard_map/ppermute | solution.py:780
  14.4 0.0 collective-permute-done.3.refs_1_
  14.4 5.0 %inner_first.1 = (f32[2,40,40,128]{3,2,1,0:T(8,128)S(1)}, f32[2,40,40,128]{3,2,1,0:T(8,128)S(1)}, f32[32,40,128]{2,1,0:T(8,128)S(1)}, f32[5,40,128]{2,1,0:T(8,12...) custom-call(f32[2]{0:T(128)S(1)} %copy-done, ...), custom_call_target="tpu_custom_call", output_to_operand_aliasing={{0}: (3, {}), {1}: (4, {}), {2}: (5, {}), {3}: (6, {}), {4}... | custom-call | tf_op jit(solution)/shard_map/inner_first/pallas_call | solution.py:529
  19.3 1.7 %collective-permute-start.4 = (f32[20,8,128]{2,1,0:T(8,128)S(1)}, f32[20,8,128]{2,1,0:T(8,128)S(1)}, u32[]{:S(2)}, u32[]{:S(2)}) collective-permute-start(f32[20,8,128]{2,1,0:T(8,128)S(1)} %get-tuple-element.68), channel_id=1, source_target_pairs={{0,8},{1,9},{2,10},{3,11},{4,12},{5,13},{6,14},{7,15},{8,0},{9,1},... | collective-permute-start | bytes 245768 | tf_op jit(solution)/shard_map/ppermute | solution.py:780
  21.1 0.0 collective-permute-start.5
  21.1 3.5 %inner_second.1 = (f32[2,40,40,128]{3,2,1,0:T(8,128)S(1)}, f32[2,40,40,128]{3,2,1,0:T(8,128)S(1)}, f32[2,40,40,128]{3,2,1,0:T(8,128)S(1)}, f32[2,40,40,128]{3,2,...) custom-call(f32[2]{0:T(128)S(1)} %copy-done, ...), custom_call_target="tpu_custom_call", output_to_operand_aliasing={{0}: (10, {}), {1}: (11, {}), {2}: (12, {}), {3}: (13, {}),... | custom-call | tf_op jit(solution)/shard_map/inner_second/pallas_call | solution.py:548
  24.6 0.0 collective-permute-done.xe
  24.6 0.0 collective-permute-done.1.xo
  24.6 1.1 %collective-permute-done.4.ce = f32[20,8,128]{2,1,0:T(8,128)S(1)} collective-permute-done((f32[20,8,128]{2,1,0:T(8,128)S(1)}, f32[20,8,128]{2,1,0:T(8,128)S(1)}, u32[]{:S(2)}, u32[]{:S(2)}) %collective-permute-start.4) | collective-permute-done | bytes 81952 | tf_op jit(solution)/shard_map/ppermute | solution.py:780
  25.7 0.0 collective-permute-done.5.co
  25.7 3.5 %edge_part.1 = (f32[2,40,40,128]{3,2,1,0:T(8,128)S(1)}, f32[2,40,40,128]{3,2,1,0:T(8,128)S(1)}, f32[2,40,40,128]{3,2,1,0:T(8,128)S(1)}, f32[2,40,40,128]{3,2,1,0...) custom-call(f32[2]{0:T(128)S(1)} %copy-done, ...), custom_call_target="tpu_custom_call", output_to_operand_aliasing={{0}: (5, {}), {1}: (6, {}), {2}: (7, {}), {3}: (8, {}), {4}... | custom-call | tf_op jit(solution)/shard_map/edge_part/pallas_call | solution.py:654
  29.2 14.4 %all_to_all.5.sums = f32[16,8,128]{2,1,0:T(8,128)S(1)} all-to-all(f32[16,8,128]{2,1,0:T(8,128)S(1)} %get-tuple-element.93), channel_id=1, replica_groups=mesh['gx'=4,'gy'=4,'af'=2] {'gx','gy'}, dimensions={0} | all-to-all | bytes 131072 | tf_op jit(solution)/shard_map/all_to_all | solution.py:797
  43.5 1.8 %gradient_part.1 = f32[32,32,128]{2,1,0:T(8,128)S(1)} custom-call(f32[2]{0:T(128)S(1)} %copy-done, f32[16,8,128]{2,1,0:T(8,128)S(1)} %all_to_all.5.sums, f32[2,40,40,128]{3,2,1,0:T(8,128)S(1)} %get-tuple-element.98.refs_0_, f32[2,40,40,128]{3,2,1,0:T(8,128)S(1)} %get-tuple-element.94.refs_0_.refs_1_, f32[2,40,40,128]{3,2,1,0:T(8,128)S(1)} %get-tuple-element.99.refs_2_, ...), custom_call_target="tpu_custom_call" | custom-call | tf_op jit(solution)/shard_map/gradient_part/pallas_call | solution.py:742
  45.3 0.1 collective-permute-start.6
  45.4 1.7 %wavefield.1 = f32[2,2,32,32,128]{4,3,2,1,0:T(8,128)} custom-call(f32[16,8,128]{2,1,0:T(8,128)S(1)} %all_to_all.5.sums, f32[2,40,40,128]{3,2,1,0:T(8,128)S(1)} %get-tuple-element.94.refs_0_.refs_1_, f32[2,40,40,128]{3,2,1,0:T(8,128)S(1)} %get-tuple-element.95.refs_1_.refs_3_, f32[2,40,40,128]{3,2,1,0:T(8,128)S(1)} %get-tuple-element.96.refs_2_.refs_6_, ...), custom_call_target="tpu_custom_call" | custom-call | tf_op jit(solution)/shard_map/wavefield/pallas_call | solution.py:750
  47.1 0.1 collective-permute-done.6
  47.3 0.9 %add.3 = f32[32,32,128]{2,1,0:T(8,128)} add(f32[32,32,128]{2,1,0:T(8,128)S(1)} %gradient_part.1, f32[32,32,128]{2,1,0:T(8,128)S(1)} %collective-permute-done.6) | non-fusion elementwise | flops 131072 | bytes 1572864 | tf_op jit(solution)/shard_map/add | solution.py:800
Async XLA Ops:
  0.6 7.5 %copy-start = (f32[2]{0:T(128)S(1)}, f32[2]{0:T(128)}, u32[]{:S(2)}) copy-start(f32[2]{0:T(128)} %freq_sq.9) | copy-start | bytes 28
  3.3 11.0 %collective-permute-start.2 = (f32[165,4,128]{2,1,0:T(4,128)S(1)}, f32[165,4,128]{2,1,0:T(4,128)S(1)}, u32[]{:S(2)}, u32[]{:S(2)}) collective-permute-start(f32[165,4,128]{2,1,0:T(4,128)S(1)} %get-tuple-element.55), channel_id=1, source_target_pairs={{0,2},{1,3},{2,0},{3,1},{4,6},{5,7},{6,4},{7,5},{8,10},{9,11},{10,... | collective-permute-start | bytes 1013768 | tf_op jit(solution)/shard_map/ppermute | solution.py:780
  6.4 7.9 %collective-permute-start.3 = (f32[165,4,128]{2,1,0:T(4,128)S(1)}, f32[165,4,128]{2,1,0:T(4,128)S(1)}, u32[]{:S(2)}, u32[]{:S(2)}) collective-permute-start(f32[165,4,128]{2,1,0:T(4,128)S(1)} %get-tuple-element.56), channel_id=1, source_target_pairs={{0,1},{1,0},{2,4},{3,5},{4,2},{5,3},{6,7},{7,6},{8,9},{9,8},{10,12... | collective-permute-start | bytes 1013768 | tf_op jit(solution)/shard_map/ppermute | solution.py:780
  6.4 18.2 %collective-permute-start = (f32[20,32,128]{2,1,0:T(8,128)S(1)}, f32[20,32,128]{2,1,0:T(8,128)S(1)}, u32[]{:S(2)}, u32[]{:S(2)}) collective-permute-start(f32[20,32,128]{2,1,0:T(8,128)S(1)} %get-tuple-element.53), channel_id=1, source_target_pairs={{0,8},{1,9},{2,10},{3,11},{4,12},{5,13},{6,14},{7,15},{8,0},{9,1},... | collective-permute-start | bytes 983048 | tf_op jit(solution)/shard_map/ppermute | solution.py:780
  7.9 16.7 %collective-permute-start.1 = (f32[20,32,128]{2,1,0:T(8,128)S(1)}, f32[20,32,128]{2,1,0:T(8,128)S(1)}, u32[]{:S(2)}, u32[]{:S(2)}) collective-permute-start(f32[20,32,128]{2,1,0:T(8,128)S(1)} %get-tuple-element.54), channel_id=1, source_target_pairs={{0,1},{1,0},{2,3},{3,2},{4,5},{5,4},{6,7},{7,6},{8,16},{9,17},{10,... | collective-permute-start | bytes 983048 | tf_op jit(solution)/shard_map/ppermute | solution.py:780
  19.3 6.4 %collective-permute-start.4 = (f32[20,8,128]{2,1,0:T(8,128)S(1)}, f32[20,8,128]{2,1,0:T(8,128)S(1)}, u32[]{:S(2)}, u32[]{:S(2)}) collective-permute-start(f32[20,8,128]{2,1,0:T(8,128)S(1)} %get-tuple-element.68), channel_id=1, source_target_pairs={{0,8},{1,9},{2,10},{3,11},{4,12},{5,13},{6,14},{7,15},{8,0},{9,1},... | collective-permute-start | bytes 245768 | tf_op jit(solution)/shard_map/ppermute | solution.py:780
  21.1 4.7 %collective-permute-start.5 = (f32[20,8,128]{2,1,0:T(8,128)S(1)}, f32[20,8,128]{2,1,0:T(8,128)S(1)}, u32[]{:S(2)}, u32[]{:S(2)}) collective-permute-start(f32[20,8,128]{2,1,0:T(8,128)S(1)} %get-tuple-element.69), channel_id=1, source_target_pairs={{0,1},{1,0},{2,3},{3,2},{4,5},{5,4},{6,7},{7,6},{8,16},{9,17},{10,... | collective-permute-start | bytes 245768 | tf_op jit(solution)/shard_map/ppermute | solution.py:780
  45.3 2.0 %collective-permute-start.6 = (f32[32,32,128]{2,1,0:T(8,128)S(1)}, f32[32,32,128]{2,1,0:T(8,128)S(1)}, u32[]{:S(2)}, u32[]{:S(2)}) collective-permute-start(f32[32,32,128]{2,1,0:T(8,128)S(1)} %gradient_part.1), channel_id=1, source_target_pairs={{0,1},{1,0},{2,3},{3,2},{4,5},{5,4},{6,7},{7,6},{8,9},{9,8},{10,11... | collective-permute-start | bytes 1572872 | tf_op jit(solution)/shard_map/ppermute | solution.py:800

commit v5 on v4

--- a/solution.py
+++ b/solution.py
@@ -90,35 +90,36 @@
         copies.add(
             slab.at[pl.ds(side, 1)], xb.at[pl.ds(fields * HALO + INNER, 1)]
         )
-    places = []
-    for side, yb in enumerate((ye, yo)):
-        last = even_y if side == 0 else jnp.logical_not(even_y)
-        at = pl.multiple_of(jnp.where(last, ny - HALO, 0), HALO)
-        places.append((yb, at))
-        copies.add(
-            table.at[:, pl.ds(at, HALO), :],
-            yb.at[pl.ds((fields + 1) * nx, fields + 1)],
-        )
+    swapped = jnp.broadcast_to(even_y, (HALO, nz))
+
+    def y_faces(block, at):
+        def row(x, _):
+            head, tail = block[x, 0:HALO, :], block[x, ny - HALO : ny, :]
+            ye[at + x] = jnp.where(swapped, tail, head)
+            yo[at + x] = jnp.where(swapped, head, tail)
+            return 0
+
+        lax.fori_loop(0, nx, row, 0, unroll=8)
+
+    def x_face(xb, to, block, at, layers):
+        for layer in range(layers):
+            for y in range(0, ny, 8):
+                xb[to + layer, y : y + 8, :] = block[at + layer, y : y + 8, :]
+
+    for k in range(fields + 1):
+        head, tail = table[k, 0:HALO, :], table[k, ny - HALO : ny, :]
+        ye[(fields + 1) * nx + k] = jnp.where(swapped, tail, head)
+        yo[(fields + 1) * nx + k] = jnp.where(swapped, head, tail)
     large.all[0].wait()
-    for yb, at in places:
-        copies.add(cells.at[:, pl.ds(at, HALO), :], yb.at[pl.ds(fields * nx, nx)])
+    y_faces(cells, fields * nx)
     for xb, skip, _ in faces:
-        copies.add(
-            cells.at[pl.ds(skip, INNER), pl.ds(0, ny), :],
-            xb.at[pl.ds(fields * HALO, INNER)],
-        )
+        x_face(xb, fields * HALO, cells, skip, INNER)
     for k in range(fields):
         large.all[1 + k].wait()
         block = s[k // 2].at[k % 2]
-        for yb, at in places:
-            copies.add(
-                block.at[pl.ds(0, nx), pl.ds(at, HALO), :], yb.at[pl.ds(k * nx, nx)]
-            )
+        y_faces(block, k * nx)
         for xb, _, at in faces:
-            copies.add(
-                block.at[pl.ds(at, HALO), pl.ds(0, ny), :],
-                xb.at[pl.ds(k * HALO, HALO)],
-            )
+            x_face(xb, k * HALO, block, at, HALO)
     copies.wait()
 
 
@@ -151,13 +152,6 @@
     )(source, model, observed, depth)
 
 
-def halo_places(ny):
-    even_y = parity("gy")
-    at_e = pl.multiple_of(jnp.where(even_y, ny, ny + HALO), HALO)
-    at_o = pl.multiple_of(jnp.where(even_y, ny + HALO, ny), HALO)
-    return at_e, at_o
-
-
 class Grid:
     def __init__(self, nx, ny, nz):
         self.nx, self.ny, self.nz = nx, ny, nz
@@ -176,6 +170,7 @@
         has_right = lax.axis_index("gy") < lax.axis_size("gy") - 1
         self.left = jnp.where(has_left, 1.0, 0.0)
         self.right = jnp.where(has_right, 1.0, 0.0)
+        self.inside = jnp.where(sub < HALO, self.right, self.left)
 
     def tile(self, t):
         if t < self.tiles:
@@ -211,10 +206,10 @@
                 up = mid[t + 1] if t + 1 < n else None
                 down = mid[t - 1] if t else None
                 if up is None:
-                    edge = 0.0 if halo is None else halo_up * self.right
+                    edge = 0.0 if halo is None else halo_up
                     up = jnp.where(self.top, edge, first_up)
                 if down is None:
-                    edge = 0.0 if halo is None else halo_down * self.left
+                    edge = 0.0 if halo is None else halo_down
                     down = jnp.where(self.bottom, edge, last_down)
             total[t] = ((below[t] + above[t]) + (up + down)) + self.beside(mid[t])
         return total
@@ -293,7 +288,8 @@
         for p, value in enumerate((re, im)):
             for t in tiles:
                 at = g.tile(t)
-                self.v0[p, i, at, :] = self.v0[p, i, at, :] + value[t]
+                total = self.v0[p, i, at, :] + value[t]
+                self.v0[p, i, at, :] = total * g.inside if t == g.tiles else total
 
     def first_halo(self, i, terms):
         g = self.grid
@@ -301,10 +297,10 @@
         coef = self.coef(i, [n])
         _, re, im = g.apply(self.s, i, i - 1, i + 1, -1, coef, [n])
         for p, value in enumerate((re, im)):
-            self.v0[p, i, g.tile(n), :] = value[n] + terms[p][n]
+            self.v0[p, i, g.tile(n), :] = (value[n] + terms[p][n]) * g.inside
             halo = self.s[p, i, g.tile(n), :]
-            low = jnp.where(g.bottom, pltpu.roll(halo, 1, axis=0) * g.left, 0.0)
-            high = jnp.where(g.top, pltpu.roll(halo, 7, axis=0) * g.right, 0.0)
+            low = jnp.where(g.bottom, pltpu.roll(halo, 1, axis=0), 0.0)
+            high = jnp.where(g.top, pltpu.roll(halo, 7, axis=0), 0.0)
             for t, change in ((0, low), (n - 1, high)):
                 at = g.tile(t)
                 self.v0[p, i, at, :] = self.v0[p, i, at, :] - change
@@ -322,6 +318,9 @@
             for p, out in enumerate((re, im)):
                 for t in tiles:
                     out[t] = out[t] + weight[t] * self.v0[p, i, g.tile(t), :]
+        if stage != 3:
+            re[g.tiles] = re[g.tiles] * g.inside
+            im[g.tiles] = im[g.tiles] * g.inside
         g.put(dst, 0, i, re, tiles)
         g.put(dst, 1, i, im, tiles)
         if acc is None:
@@ -446,20 +445,24 @@
         u0, v1, u1 = news[3 * f : 3 * f + 3]
         many.append(Field(grid, (s[f], v0, u0, v1, u1, cr, ci), w))
     if half == 0:
-        copies = Copies(sem.at[0])
-        for yb, at in zip((ye, yo), halo_places(ny)):
-            rows = pl.ds(at, HALO)
-            copies.add(
-                yb.at[pl.ds((fields + 1) * nx, fields + 1)], aux.at[:, rows, :]
-            )
-            copies.add(yb.at[pl.ds(fields * nx, nx)], cells.at[:, rows, :])
+        swapped = jnp.broadcast_to(parity("gy"), (HALO, nz))
+
+        def halo(at):
+            even, odd = ye[at], yo[at]
+            high = jnp.where(swapped, even, odd) * grid.right
+            low = jnp.where(swapped, odd, even) * grid.left
+            return jnp.concatenate([high, low], axis=0)
+
+        def merge(x, _):
+            cells[x, ny:, :] = halo(fields * nx + x)
             for k in range(fields):
-                copies.add(
-                    yb.at[pl.ds(k * nx, nx)],
-                    s[k // 2].at[k % 2, pl.ds(0, nx), rows, :],
-                )
-        copies.wait()
-        out = corner_faces(freqs, nx, ny, s, cells, aux, ce, co, slab, sem.at[1])
+                s[k // 2][k % 2, x, ny:, :] = halo(k * nx + x)
+            return 0
+
+        lax.fori_loop(0, nx, merge, 0, unroll=4)
+        for k in range(fields + 1):
+            aux[k, ny:, :] = halo((fields + 1) * nx + k)
+        out = corner_faces(freqs, nx, ny, s, cells, aux, ce, co, slab, sem)
 
     def prepare(i):
         return grid.prepare(
@@ -531,11 +534,11 @@
         out_shape=tuple(pltpu.VMEM(k.shape, F32) for k in kept)
         + news
         + (corner, corner),
-        in_specs=[SMEM, ANY, ANY] + [VMEM] * len(kept),
+        in_specs=[SMEM, VMEM, VMEM] + [VMEM] * len(kept),
         input_output_aliases={3 + k: k for k in range(len(kept))},
         scratch_shapes=[
             pltpu.VMEM((2, 2 * HALO, nz), F32),
-            pltpu.SemaphoreType.DMA((2, 16)),
+            pltpu.SemaphoreType.DMA((16,)),
         ],
         compiler_params=params(8),
         name="inner_first",
@@ -565,11 +568,10 @@
 def edge_kernel(peers, freqs, nx, ny, freq_sq, xe, xo, ce, co, *refs):
     count = 7 * freqs + 1
     moments, refs = refs[count], refs[count + 1 :]
-    state, (part, cells, aux, sem) = refs[:count], refs[count:]
+    state, (part, cells, aux) = refs[:count], refs[count:]
     fields = 2 * freqs
     nz = state[0].shape[3]
     w = state[-1]
-    copies = Copies(sem)
     even_x = parity("gx")
     pieces = (
         (xe, 0, 0, ny),
@@ -581,21 +583,17 @@
         above = even_x if side == 0 else jnp.logical_not(even_x)
         slot = jnp.where(above, nx, nx + HALO)
         half = jnp.where(above, 0, 1)
-        rows = pl.ds(at, size)
-        for k in range(fields):
-            copies.add(
-                block.at[pl.ds(k * HALO, HALO)],
-                state[7 * (k // 2)].at[k % 2, pl.ds(slot, HALO), rows, :],
-            )
-        copies.add(
-            block.at[pl.ds(fields * HALO, INNER)], cells.at[half, :, rows, :]
-        )
-        copies.add(
-            block.at[pl.ds(fields * HALO + INNER, 1)],
-            aux.at[pl.ds(half, 1), rows, :],
-        )
+        for y in range(0, size, 8):
+            here, there = pl.ds(y, 8), pl.ds(at + y, 8)
+            for k in range(fields):
+                for layer in range(HALO):
+                    state[7 * (k // 2)][k % 2, slot + layer, there, :] = block[
+                        k * HALO + layer, here, :
+                    ]
+            for layer in range(INNER):
+                cells[half, layer, there, :] = block[fields * HALO + layer, here, :]
+            aux[half, there, :] = block[fields * HALO + INNER, here, :]
     grid = Grid(nx, ny, nz)
-    copies.wait()
     many = [Field(grid, state[7 * f : 7 * f + 7], w) for f in range(freqs)]
     for half in range(2):
         for layer in range(INNER):
@@ -654,12 +652,11 @@
     return pl.pallas_call(
         functools.partial(edge_kernel, peers, freqs, nx, ny),
         out_shape=outs + (jax.ShapeDtypeStruct((peers, 4 * freqs, nz), F32),),
-        in_specs=[SMEM] + [ANY] * 4 + [VMEM] * (len(state) + 1),
+        in_specs=[SMEM] + [VMEM] * (5 + len(state)),
         input_output_aliases={5 + k: k for k in range(len(state))},
         scratch_shapes=[
             pltpu.VMEM((2, INNER, ny + 2 * HALO, nz), F32),
             pltpu.VMEM((2, ny + 2 * HALO, nz), F32),
-            pltpu.SemaphoreType.DMA((64,)),
         ],
         compiler_params=params(8),
         name="edge_part",
@@ -708,7 +705,7 @@
             out[x, at, :] = total
         return 0
 
-    lax.fori_loop(0, nx, row, 0)
+    lax.fori_loop(0, nx, row, 0, unroll=2)
 
 
 def wave_kernel(freqs, nx, ny, sums, *refs):
@@ -727,7 +724,7 @@
                     block[k, x, at, :] = a * v0[p, x, at, :] + b * v1[p, x, at, :]
                 return 0
 
-            lax.fori_loop(0, nx, row, 0)
+            lax.fori_loop(0, nx, row, 0, unroll=8)
             copies.add(block.at[k], out.at[f, p])
     copies.wait()
 

time: 48.3 us -> 47.2 us (0.977)
  Pallas kernels: 21.6 us -> 20 us
    pallas_call x1, Pallas kernels: 3.45 us -> 2.48 us  [edge_part(): pl.pallas_call(functools.partial(edge_kernel, peers, freqs, nx, ny), out_...]
where the time goes in v5:
time: 47.2 us; the launch traced here: 47 us
  Pallas kernels  20 us (42%)
  blocking collectives  14.3 us (30%)
  starting transfers between devices  6.6 us (14%)
  waiting for transfers between devices  4.48 us (9%)
  other arithmetic  0.87 us (2%)
  between operations  0.71 us (2%)
    all_to_all x1, blocking collectives, on_device(): sums = lax.all_to_all(part, ('gx', 'gy'), 0, 0)  14.3 us
    ppermute x6, starting transfers between devices, swap(): return lax.ppermute(cells, names, pairs)  6.53 us
    pallas_call x1, Pallas kernels, inner_part(): pl.pallas_call(functools.partial(inner_kernel, freqs, nx, ny, 0), out_sha...  4.85 us
    ppermute x6, waiting for transfers between devices, swap(): return lax.ppermute(cells, names, pairs)  4.05 us
    pallas_call x1, Pallas kernels, rest(): pl.pallas_call(functools.partial(inner_kernel, freqs, nx, ny, 1), out_sha...  3.47 us
    pallas_call x1, Pallas kernels, early(): pl.pallas_call(functools.partial(early_kernel, freqs, nx, ny), out_shape=...  3.43 us
    pallas_call x1, Pallas kernels, load(): pl.pallas_call(load_kernel, out_shape=(pltpu.VMEM((2, nx + 2 * HALO, ny +...  2.64 us
    pallas_call x1, Pallas kernels, edge_part(): pl.pallas_call(functools.partial(edge_kernel, peers, freqs, nx, ny), out_...  2.48 us
  transfers between devices with their start and end apart: 7, of which 3 were waited for; matrix products, arithmetic and copies ran while one was open for 0% of the time, Pallas kernels for 28%

profile of v5, /device:TPU:0, one launch (start us, length us, event | category | flops | bytes accessed | tf_op | source)
XLA Modules:
  0.0 47.0 jit_solution(13197053404848894457)
XLA Ops:
  0.6 0.0 copy-start
  0.6 2.6 %load.1 = (f32[2,40,40,128]{3,2,1,0:T(8,128)S(1)}, f32[2,40,40,128]{3,2,1,0:T(8,128)S(1)}, f32[32,40,128]{2,1,0:T(8,128)S(1)}, f32[5,40,128]{2,1,0:T(8,128)S(1)}...) custom-call(f32[2,2,32,32,128]{4,3,2,1,0:T(8,128)} %source.1, ...), custom_call_target="tpu_custom_call" | custom-call | tf_op jit(solution)/shard_map/load/pallas_call | solution.py:131
  3.3 3.1 %collective-permute-start.2 = (f32[165,4,128]{2,1,0:T(4,128)S(1)}, f32[165,4,128]{2,1,0:T(4,128)S(1)}, u32[]{:S(2)}, u32[]{:S(2)}) collective-permute-start(f32[165,4,128]{2,1,0:T(4,128)S(1)} %get-tuple-element.55), channel_id=1, source_target_pairs={{0,2},{1,3},{2,0},{3,1},{4,6},{5,7},{6,4},{7,5},{8,10},{9,11},{10,... | collective-permute-start | bytes 1013768 | tf_op jit(solution)/shard_map/ppermute | solution.py:777
  6.4 0.0 collective-permute-start.3
  6.4 1.5 %collective-permute-start = (f32[20,32,128]{2,1,0:T(8,128)S(1)}, f32[20,32,128]{2,1,0:T(8,128)S(1)}, u32[]{:S(2)}, u32[]{:S(2)}) collective-permute-start(f32[20,32,128]{2,1,0:T(8,128)S(1)} %get-tuple-element.53), channel_id=1, source_target_pairs={{0,8},{1,9},{2,10},{3,11},{4,12},{5,13},{6,14},{7,15},{8,0},{9,1},... | collective-permute-start | bytes 983048 | tf_op jit(solution)/shard_map/ppermute | solution.py:777
  7.9 0.2 collective-permute-start.1
  8.1 0.0 copy-done
  8.1 3.4 %early.1 = (f32[2,40,40,128]{3,2,1,0:T(8,128)S(1)}, f32[40,5,8,128]{3,2,1,0:T(8,128)S(1)}, f32[40,5,8,128]{3,2,1,0:T(8,128)S(1)}, f32[2,40,40,128]{3,2,1,0:T(8,1...) custom-call(f32[2]{0:T(128)S(1)} %copy-done, ...), custom_call_target="tpu_custom_call" | custom-call | tf_op jit(solution)/shard_map/early/pallas_call | solution.py:392
  11.5 2.8 %collective-permute-done.2.refs_0_ = f32[165,4,128]{2,1,0:T(4,128)S(1)} collective-permute-done((f32[165,4,128]{2,1,0:T(4,128)S(1)}, f32[165,4,128]{2,1,0:T(4,128)S(1)}, u32[]{:S(2)}, u32[]{:S(2)}) %collective-permute-start.2) | collective-permute-done | bytes 337952 | tf_op jit(solution)/shard_map/ppermute | solution.py:777
  14.3 0.0 collective-permute-done.3.refs_1_
  14.3 4.8 %inner_first.1 = (f32[2,40,40,128]{3,2,1,0:T(8,128)S(1)}, f32[2,40,40,128]{3,2,1,0:T(8,128)S(1)}, f32[32,40,128]{2,1,0:T(8,128)S(1)}, f32[5,40,128]{2,1,0:T(8,12...) custom-call(f32[2]{0:T(128)S(1)} %copy-done, ...), custom_call_target="tpu_custom_call", output_to_operand_aliasing={{0}: (3, {}), {1}: (4, {}), {2}: (5, {}), {3}: (6, {}), {4}... | custom-call | tf_op jit(solution)/shard_map/inner_first/pallas_call | solution.py:532
  19.2 1.7 %collective-permute-start.4 = (f32[20,8,128]{2,1,0:T(8,128)S(1)}, f32[20,8,128]{2,1,0:T(8,128)S(1)}, u32[]{:S(2)}, u32[]{:S(2)}) collective-permute-start(f32[20,8,128]{2,1,0:T(8,128)S(1)} %get-tuple-element.68), channel_id=1, source_target_pairs={{0,8},{1,9},{2,10},{3,11},{4,12},{5,13},{6,14},{7,15},{8,0},{9,1},... | collective-permute-start | bytes 245768 | tf_op jit(solution)/shard_map/ppermute | solution.py:777
  20.9 0.0 collective-permute-start.5
  20.9 3.5 %inner_second.1 = (f32[2,40,40,128]{3,2,1,0:T(8,128)S(1)}, f32[2,40,40,128]{3,2,1,0:T(8,128)S(1)}, f32[2,40,40,128]{3,2,1,0:T(8,128)S(1)}, f32[2,40,40,128]{3,2,...) custom-call(f32[2]{0:T(128)S(1)} %copy-done, ...), custom_call_target="tpu_custom_call", output_to_operand_aliasing={{0}: (10, {}), {1}: (11, {}), {2}: (12, {}), {3}: (13, {}),... | custom-call | tf_op jit(solution)/shard_map/inner_second/pallas_call | solution.py:551
  24.4 0.0 collective-permute-done.xe
  24.4 0.0 collective-permute-done.1.xo
  24.4 1.3 %collective-permute-done.4.ce = f32[20,8,128]{2,1,0:T(8,128)S(1)} collective-permute-done((f32[20,8,128]{2,1,0:T(8,128)S(1)}, f32[20,8,128]{2,1,0:T(8,128)S(1)}, u32[]{:S(2)}, u32[]{:S(2)}) %collective-permute-start.4) | collective-permute-done | bytes 81952 | tf_op jit(solution)/shard_map/ppermute | solution.py:777
  25.7 0.0 collective-permute-done.5.co
  25.7 2.5 %edge_part.1 = (f32[2,40,40,128]{3,2,1,0:T(8,128)S(1)}, f32[2,40,40,128]{3,2,1,0:T(8,128)S(1)}, f32[2,40,40,128]{3,2,1,0:T(8,128)S(1)}, f32[2,40,40,128]{3,2,1,0...) custom-call(f32[2]{0:T(128)S(1)} %copy-done, ...), custom_call_target="tpu_custom_call", output_to_operand_aliasing={{0}: (5, {}), {1}: (6, {}), {2}: (7, {}), {3}: (8, {}), {4}... | custom-call | tf_op jit(solution)/shard_map/edge_part/pallas_call | solution.py:652
  28.1 14.3 %all_to_all.5.sums = f32[16,8,128]{2,1,0:T(8,128)S(1)} all-to-all(f32[16,8,128]{2,1,0:T(8,128)S(1)} %get-tuple-element.93), channel_id=1, replica_groups=mesh['gx'=4,'gy'=4,'af'=2] {'gx','gy'}, dimensions={0} | all-to-all | bytes 131072 | tf_op jit(solution)/shard_map/all_to_all | solution.py:794
  42.5 1.7 %gradient_part.1 = f32[32,32,128]{2,1,0:T(8,128)S(1)} custom-call(f32[2]{0:T(128)S(1)} %copy-done, f32[16,8,128]{2,1,0:T(8,128)S(1)} %all_to_all.5.sums, f32[2,40,40,128]{3,2,1,0:T(8,128)S(1)} %get-tuple-element.98.refs_0_, f32[2,40,40,128]{3,2,1,0:T(8,128)S(1)} %get-tuple-element.94.refs_0_.refs_1_, f32[2,40,40,128]{3,2,1,0:T(8,128)S(1)} %get-tuple-element.99.refs_2_, ...), custom_call_target="tpu_custom_call" | custom-call | tf_op jit(solution)/shard_map/gradient_part/pallas_call | solution.py:739
  44.1 0.1 collective-permute-start.6
  44.2 1.5 %wavefield.1 = f32[2,2,32,32,128]{4,3,2,1,0:T(8,128)} custom-call(f32[16,8,128]{2,1,0:T(8,128)S(1)} %all_to_all.5.sums, f32[2,40,40,128]{3,2,1,0:T(8,128)S(1)} %get-tuple-element.94.refs_0_.refs_1_, f32[2,40,40,128]{3,2,1,0:T(8,128)S(1)} %get-tuple-element.95.refs_1_.refs_3_, f32[2,40,40,128]{3,2,1,0:T(8,128)S(1)} %get-tuple-element.96.refs_2_.refs_6_, ...), custom_call_target="tpu_custom_call" | custom-call | tf_op jit(solution)/shard_map/wavefield/pallas_call | solution.py:747
  45.7 0.4 collective-permute-done.6
  46.1 0.9 %add.3 = f32[32,32,128]{2,1,0:T(8,128)} add(f32[32,32,128]{2,1,0:T(8,128)S(1)} %gradient_part.1, f32[32,32,128]{2,1,0:T(8,128)S(1)} %collective-permute-done.6) | non-fusion elementwise | flops 131072 | bytes 1572864 | tf_op jit(solution)/shard_map/add | solution.py:797
Async XLA Ops:
  0.6 7.5 %copy-start = (f32[2]{0:T(128)S(1)}, f32[2]{0:T(128)}, u32[]{:S(2)}) copy-start(f32[2]{0:T(128)} %freq_sq.9) | copy-start | bytes 28
  3.3 11.0 %collective-permute-start.2 = (f32[165,4,128]{2,1,0:T(4,128)S(1)}, f32[165,4,128]{2,1,0:T(4,128)S(1)}, u32[]{:S(2)}, u32[]{:S(2)}) collective-permute-start(f32[165,4,128]{2,1,0:T(4,128)S(1)} %get-tuple-element.55), channel_id=1, source_target_pairs={{0,2},{1,3},{2,0},{3,1},{4,6},{5,7},{6,4},{7,5},{8,10},{9,11},{10,... | collective-permute-start | bytes 1013768 | tf_op jit(solution)/shard_map/ppermute | solution.py:777
  6.4 7.9 %collective-permute-start.3 = (f32[165,4,128]{2,1,0:T(4,128)S(1)}, f32[165,4,128]{2,1,0:T(4,128)S(1)}, u32[]{:S(2)}, u32[]{:S(2)}) collective-permute-start(f32[165,4,128]{2,1,0:T(4,128)S(1)} %get-tuple-element.56), channel_id=1, source_target_pairs={{0,1},{1,0},{2,4},{3,5},{4,2},{5,3},{6,7},{7,6},{8,9},{9,8},{10,12... | collective-permute-start | bytes 1013768 | tf_op jit(solution)/shard_map/ppermute | solution.py:777
  6.4 18.0 %collective-permute-start = (f32[20,32,128]{2,1,0:T(8,128)S(1)}, f32[20,32,128]{2,1,0:T(8,128)S(1)}, u32[]{:S(2)}, u32[]{:S(2)}) collective-permute-start(f32[20,32,128]{2,1,0:T(8,128)S(1)} %get-tuple-element.53), channel_id=1, source_target_pairs={{0,8},{1,9},{2,10},{3,11},{4,12},{5,13},{6,14},{7,15},{8,0},{9,1},... | collective-permute-start | bytes 983048 | tf_op jit(solution)/shard_map/ppermute | solution.py:777
  7.9 16.5 %collective-permute-start.1 = (f32[20,32,128]{2,1,0:T(8,128)S(1)}, f32[20,32,128]{2,1,0:T(8,128)S(1)}, u32[]{:S(2)}, u32[]{:S(2)}) collective-permute-start(f32[20,32,128]{2,1,0:T(8,128)S(1)} %get-tuple-element.54), channel_id=1, source_target_pairs={{0,1},{1,0},{2,3},{3,2},{4,5},{5,4},{6,7},{7,6},{8,16},{9,17},{10,... | collective-permute-start | bytes 983048 | tf_op jit(solution)/shard_map/ppermute | solution.py:777
  19.2 6.5 %collective-permute-start.4 = (f32[20,8,128]{2,1,0:T(8,128)S(1)}, f32[20,8,128]{2,1,0:T(8,128)S(1)}, u32[]{:S(2)}, u32[]{:S(2)}) collective-permute-start(f32[20,8,128]{2,1,0:T(8,128)S(1)} %get-tuple-element.68), channel_id=1, source_target_pairs={{0,8},{1,9},{2,10},{3,11},{4,12},{5,13},{6,14},{7,15},{8,0},{9,1},... | collective-permute-start | bytes 245768 | tf_op jit(solution)/shard_map/ppermute | solution.py:777
  20.9 4.8 %collective-permute-start.5 = (f32[20,8,128]{2,1,0:T(8,128)S(1)}, f32[20,8,128]{2,1,0:T(8,128)S(1)}, u32[]{:S(2)}, u32[]{:S(2)}) collective-permute-start(f32[20,8,128]{2,1,0:T(8,128)S(1)} %get-tuple-element.69), channel_id=1, source_target_pairs={{0,1},{1,0},{2,3},{3,2},{4,5},{5,4},{6,7},{7,6},{8,16},{9,17},{10,... | collective-permute-start | bytes 245768 | tf_op jit(solution)/shard_map/ppermute | solution.py:777
  44.1 2.0 %collective-permute-start.6 = (f32[32,32,128]{2,1,0:T(8,128)S(1)}, f32[32,32,128]{2,1,0:T(8,128)S(1)}, u32[]{:S(2)}, u32[]{:S(2)}) collective-permute-start(f32[32,32,128]{2,1,0:T(8,128)S(1)} %gradient_part.1), channel_id=1, source_target_pairs={{0,1},{1,0},{2,3},{3,2},{4,5},{5,4},{6,7},{7,6},{8,9},{9,8},{10,11... | collective-permute-start | bytes 1572872 | tf_op jit(solution)/shard_map/ppermute | solution.py:797

commit v6 on v5

--- a/solution.py
+++ b/solution.py
@@ -55,16 +55,27 @@
     lane = lax.broadcasted_iota(jnp.int32, (rows, nz), 1)
     lanes = jnp.zeros((rows, nz), F32)
     for k in range(fields + 1):
-        inside = (lane >= 8 * k) & (lane < 8 * k + INNER)
-        shift = lax.rem(8 * k + nz - skip, nz)
+        inside = (lane >= INNER * k) & (lane < INNER * k + INNER)
+        shift = lax.rem(INNER * k + nz - skip, nz)
         lanes = jnp.where(inside, pltpu.roll(table[k], shift, axis=1), lanes)
     return lanes
+
+
+def fold(slab, nz):
+    rows, width = slab.shape[0] // 8, nz // 8
+    lane = lax.broadcasted_iota(jnp.int32, (rows, nz), 1)
+    out = jnp.zeros((rows, nz), F32)
+    for g in range(8):
+        piece = slab[g * rows : (g + 1) * rows, :]
+        inside = (lane >= g * width) & (lane < (g + 1) * width)
+        out = jnp.where(inside, pltpu.roll(piece, g * width, axis=1), out)
+    return out
 
 
 def load_kernel(source, model, observed, depth, *refs):
     freqs, _, nx, ny, nz = source.shape
     fields = 2 * freqs
-    s, (cells, aux, xe, xo, ye, yo, seen, sunk, table, slab, sem) = refs[:freqs], refs[freqs:]
+    s, (cells, aux, xe, xo, ye, yo, seen, sunk, table, sem) = refs[:freqs], refs[freqs:]
     small = Copies(sem.at[0])
     small.add(observed, seen)
     small.add(depth, sunk)
@@ -86,10 +97,8 @@
         last = even_x if side == 0 else jnp.logical_not(even_x)
         skip = jnp.where(last, nx - INNER, 0)
         faces.append((xb, skip, jnp.where(last, nx - HALO, 0)))
-        slab[side] = lane_slab(table, fields, skip, ny, nz)
-        copies.add(
-            slab.at[pl.ds(side, 1)], xb.at[pl.ds(fields * HALO + INNER, 1)]
-        )
+        at = (fields * HALO + INNER) * ny
+        xb[at : at + ny // 8, :] = fold(lane_slab(table, fields, skip, ny, nz), nz)
     swapped = jnp.broadcast_to(even_y, (HALO, nz))
 
     def y_faces(block, at):
@@ -104,7 +113,8 @@
     def x_face(xb, to, block, at, layers):
         for layer in range(layers):
             for y in range(0, ny, 8):
-                xb[to + layer, y : y + 8, :] = block[at + layer, y : y + 8, :]
+                row = (to + layer) * ny + y
+                xb[row : row + 8, :] = block[at + layer, y : y + 8, :]
 
     for k in range(fields + 1):
         head, tail = table[k, 0:HALO, :], table[k, ny - HALO : ny, :]
@@ -126,7 +136,7 @@
 def load(source, model, observed, depth):
     freqs, _, nx, ny, nz = source.shape
     fields = 2 * freqs
-    xs = pltpu.VMEM((fields * HALO + INNER + 1, ny, nz), F32)
+    xs = pltpu.VMEM(((fields * HALO + INNER) * ny + 8, nz), F32)
     ys = pltpu.VMEM(((fields + 1) * nx + fields + 1, HALO, nz), F32)
     return pl.pallas_call(
         load_kernel,
@@ -144,7 +154,6 @@
             pltpu.VMEM(observed.shape, F32),
             pltpu.VMEM(depth.shape, jnp.int32),
             pltpu.VMEM((fields + 1, ny, nz), F32),
-            pltpu.VMEM((2, ny, nz), F32),
             pltpu.SemaphoreType.DMA((3, 32)),
         ],
         compiler_params=params(LOAD_MIB),
@@ -340,8 +349,10 @@
 
 def early_kernel(freqs, nx, ny, freq_sq, *refs):
     s, (cells, aux), refs = refs[:freqs], refs[freqs : freqs + 2], refs[freqs + 2 :]
-    w = refs[3 * freqs]
+    w, splat = refs[3 * freqs :]
     nz = cells.shape[2]
+    for f in range(freqs):
+        splat[f] = jnp.full((8, nz), freq_sq[f], F32)
     grid = Grid(nx, ny, nz)
     many = [
         Field(grid, (s[f], refs[3 * f], None, None, None, *refs[3 * f + 1 : 3 * f + 3]), w)
@@ -391,35 +402,27 @@
     coef = pltpu.VMEM((xe, ny // 8 + 1, 8, nz), F32)
     return pl.pallas_call(
         functools.partial(early_kernel, freqs, nx, ny),
-        out_shape=(field, coef, coef) * freqs + (coef,),
+        out_shape=(field, coef, coef) * freqs
+        + (coef, pltpu.VMEM((freqs, 8, nz), F32)),
         in_specs=[SMEM] + [VMEM] * (freqs + 2),
         compiler_params=params(8),
         name="early",
     )(freq_sq, *s, cells, aux)
 
 
-def corner_faces(freqs, nx, ny, s, cells, aux, ce, co, slab, sem):
+def corner_faces(freqs, nx, ny, s, cells, aux, ce, co):
     fields = 2 * freqs
     nz = cells.shape[2]
     even_x = parity("gx")
-    out = Copies(sem)
-    rows = pl.ds(ny, 2 * HALO)
+    near = [aux[k, ny:, :] for k in range(fields + 1)]
     for side, cb in enumerate((ce, co)):
         last = even_x if side == 0 else jnp.logical_not(even_x)
-        skip = jnp.where(last, nx - INNER, 0)
-        at = jnp.where(last, nx - HALO, 0)
-        for k in range(fields):
-            out.add(
-                s[k // 2].at[k % 2, pl.ds(at, HALO), rows, :],
-                cb.at[pl.ds(k * HALO, HALO)],
-            )
-        out.add(cells.at[pl.ds(skip, INNER), rows, :], cb.at[pl.ds(fields * HALO, INNER)])
-        near = [aux[k, ny:, :] for k in range(fields + 1)]
-        slab[side] = lane_slab(near, fields, skip, 2 * HALO, nz)
-        out.add(
-            slab.at[pl.ds(side, 1)], cb.at[pl.ds(fields * HALO + INNER, 1)]
-        )
-    return out
+        at = jnp.where(last, nx - INNER, 0)
+        for layer in range(INNER):
+            for k in range(fields):
+                cb[k * INNER + layer] = s[k // 2][k % 2, at + layer, ny:, :]
+            cb[fields * INNER + layer] = cells[at + layer, ny:, :]
+        cb[(fields + 1) * INNER] = lane_slab(near, fields, at, 2 * HALO, nz)
 
 
 def inner_kernel(freqs, nx, ny, half, freq_sq, *refs):
@@ -429,7 +432,7 @@
         refs = refs[2 + count :]
         s, (cells, aux), refs = refs[:freqs], refs[freqs : freqs + 2], refs[freqs + 2 :]
         known, refs = refs[: 3 * freqs + 1], refs[3 * freqs + 1 :]
-        news, (moments, ce, co, slab, sem) = refs[: 3 * freqs], refs[3 * freqs :]
+        news, (moments, ce, co) = refs[: 3 * freqs], refs[3 * freqs :]
     else:
         s, known = refs[:freqs], refs[freqs : 4 * freqs + 1]
         partial = refs[7 * freqs + 1]
@@ -462,7 +465,7 @@
         lax.fori_loop(0, nx, merge, 0, unroll=4)
         for k in range(fields + 1):
             aux[k, ny:, :] = halo((fields + 1) * nx + k)
-        out = corner_faces(freqs, nx, ny, s, cells, aux, ce, co, slab, sem)
+        corner_faces(freqs, nx, ny, s, cells, aux, ce, co)
 
     def prepare(i):
         return grid.prepare(
@@ -517,14 +520,12 @@
         for m in range(4):
             value = acc[f][m]
             moments[f, m] = value if half == 0 else value + partial[f, m]
-    if half == 0:
-        out.wait()
 
 
 def inner_part(nx, ny, freq_sq, ye, yo, s, cells, aux, known):
     freqs = len(s)
     nz = cells.shape[2]
-    slabs = 2 * freqs * HALO + INNER + 1
+    slabs = (2 * freqs + 1) * INNER + 1
     field = pltpu.VMEM(s[0].shape, F32)
     corner = pltpu.VMEM((slabs, 2 * HALO, nz), F32)
     kept = (*s, cells, aux, *known)
@@ -534,12 +535,8 @@
         out_shape=tuple(pltpu.VMEM(k.shape, F32) for k in kept)
         + news
         + (corner, corner),
-        in_specs=[SMEM, VMEM, VMEM] + [VMEM] * len(kept),
+        in_specs=[VMEM] * (3 + len(kept)),
         input_output_aliases={3 + k: k for k in range(len(kept))},
-        scratch_shapes=[
-            pltpu.VMEM((2, 2 * HALO, nz), F32),
-            pltpu.SemaphoreType.DMA((16,)),
-        ],
         compiler_params=params(8),
         name="inner_first",
     )(freq_sq, ye, yo, *kept)
@@ -547,15 +544,15 @@
     news_got, (ce, co) = got[len(kept) : -2], got[-2:]
 
     def rest():
-        first = 1 + freqs + len(known)
+        first = freqs + len(known)
         again = pl.pallas_call(
-            functools.partial(inner_kernel, freqs, nx, ny, 1),
+            functools.partial(inner_kernel, freqs, nx, ny, 1, None),
             out_shape=news,
-            in_specs=[SMEM] + [VMEM] * (freqs + len(known) + len(news)),
+            in_specs=[VMEM] * (freqs + len(known) + len(news)),
             input_output_aliases={first + k: k for k in range(len(news))},
             compiler_params=params(8),
             name="inner_second",
-        )(freq_sq, *s, *known, *news_got)
+        )(*s, *known, *news_got)
         state = []
         for f in range(freqs):
             v0, cr, ci = known[3 * f : 3 * f + 3]
@@ -573,26 +570,34 @@
     nz = state[0].shape[3]
     w = state[-1]
     even_x = parity("gx")
-    pieces = (
-        (xe, 0, 0, ny),
-        (xo, 1, 0, ny),
-        (ce, 0, ny, 2 * HALO),
-        (co, 1, ny, 2 * HALO),
-    )
-    for block, side, at, size in pieces:
+    group = nz // 8
+    for side, (xb, cb) in enumerate(((xe, ce), (xo, co))):
         above = even_x if side == 0 else jnp.logical_not(even_x)
         slot = jnp.where(above, nx, nx + HALO)
+        near = jnp.where(above, nx, nx + HALO + 1)
         half = jnp.where(above, 0, 1)
-        for y in range(0, size, 8):
-            here, there = pl.ds(y, 8), pl.ds(at + y, 8)
+        for layer in range(HALO):
             for k in range(fields):
-                for layer in range(HALO):
-                    state[7 * (k // 2)][k % 2, slot + layer, there, :] = block[
-                        k * HALO + layer, here, :
-                    ]
-            for layer in range(INNER):
-                cells[half, layer, there, :] = block[fields * HALO + layer, here, :]
-            aux[half, there, :] = block[fields * HALO + INNER, here, :]
+                block = state[7 * (k // 2)]
+                for y in range(0, ny, 8):
+                    row = (k * HALO + layer) * ny + y
+                    block[k % 2, slot + layer, y : y + 8, :] = xb[row : row + 8, :]
+                if layer < INNER:
+                    block[k % 2, near + layer, ny:, :] = cb[k * INNER + layer]
+            if layer < INNER:
+                for y in range(0, ny, 8):
+                    row = (fields * HALO + layer) * ny + y
+                    cells[half, layer, y : y + 8, :] = xb[row : row + 8, :]
+                cells[half, layer, ny:, :] = cb[fields * INNER + layer]
+        at = (fields * HALO + INNER) * ny
+        folded = xb[at : at + ny // 8, :]
+        for g in range(8):
+            rows = pl.ds(g * (ny // 8), ny // 8)
+            aux[half, rows, :] = pltpu.roll(folded, (nz - g * group) % nz, axis=1)
+        aux[half, ny:, :] = cb[(fields + 1) * INNER]
+    for k in range(fields):
+        for i in (nx + HALO - 1, nx + HALO):
+            state[7 * (k // 2)][k % 2, i, ny:, :] = jnp.zeros((2 * HALO, nz), F32)
     grid = Grid(nx, ny, nz)
     many = [Field(grid, state[7 * f : 7 * f + 7], w) for f in range(freqs)]
     for half in range(2):
@@ -605,7 +610,7 @@
                 w,
                 many,
                 lambda t: cells[half, layer, grid.tile(t), :],
-                lambda k, t: grid.pick(aux, half, t, 8 * k + layer),
+                lambda k, t: grid.pick(aux, half, t, INNER * k + layer),
             )
             for f in range(freqs):
                 for p in range(2):
@@ -652,7 +657,7 @@
     return pl.pallas_call(
         functools.partial(edge_kernel, peers, freqs, nx, ny),
         out_shape=outs + (jax.ShapeDtypeStruct((peers, 4 * freqs, nz), F32),),
-        in_specs=[SMEM] + [VMEM] * (5 + len(state)),
+        in_specs=[VMEM] * (6 + len(state)),
         input_output_aliases={5 + k: k for k in range(len(state))},
         scratch_shapes=[
             pltpu.VMEM((2, INNER, ny + 2 * HALO, nz), F32),
@@ -684,6 +689,7 @@
 def gradient_kernel(freqs, nx, ny, freq_sq, sums, *refs):
     out = refs[-1]
     weights = steps(sums, freqs)
+    scale = [-freq_sq[f] for f in range(freqs)]
 
     def row(x, _):
         for y in range(0, ny, 8):
@@ -700,7 +706,7 @@
                 miss_im = miss_im - s[1, x, at, :]
                 left = (wave_re + attenuation * wave_im) * miss_re
                 right = (wave_im - attenuation * wave_re) * miss_im
-                term = -freq_sq[f] * (left + right)
+                term = scale[f] * (left + right)
                 total = term if total is None else total + term
             out[x, at, :] = total
         return 0
@@ -739,7 +745,7 @@
     gradient = pl.pallas_call(
         functools.partial(gradient_kernel, freqs, nx, ny),
         out_shape=jax.ShapeDtypeStruct((nx, ny, nz), F32),
-        in_specs=[SMEM] + [VMEM] * (1 + len(fields)),
+        in_specs=[VMEM] * (2 + len(fields)),
         out_specs=VMEM,
         compiler_params=params(8),
         name="gradient_part",
@@ -783,16 +789,16 @@
     *s, cells, aux, xe, xo, ye, yo = load(source, model, observed, receiver_depth)
     ye, yo = swap(ye, "gy", 0), swap(yo, "gy", 1)
     xe, xo = swap(xe, "gx", 0), swap(xo, "gx", 1)
-    known = early(nx, ny, freq_sq, s, cells, aux)
-    ce, co, rest = inner_part(nx, ny, freq_sq, ye, yo, s, cells, aux, known)
+    *known, splat = early(nx, ny, freq_sq, s, cells, aux)
+    ce, co, rest = inner_part(nx, ny, splat, ye, yo, s, cells, aux, known)
     ce, co = swap(ce, "gx", 0), swap(co, "gx", 1)
     state, moments = rest()
     peers = lax.axis_size("gx") * lax.axis_size("gy")
     *state, part = edge_part(
-        peers, freqs, nx, ny, freq_sq, xe, xo, ce, co, state, moments
+        peers, freqs, nx, ny, splat, xe, xo, ce, co, state, moments
     )
     sums = lax.all_to_all(part, ("gx", "gy"), 0, 0)
-    gradient, wave = results(freqs, nx, ny, freq_sq, sums, state)
+    gradient, wave = results(freqs, nx, ny, splat, sums, state)
     if lax.axis_size("af") == 2:
         gradient = gradient + lax.ppermute(gradient, "af", [(0, 1), (1, 0)])
     else:

time: 47.2 us -> 45 us (0.953)
  Pallas kernels: 20 us -> 17.6 us
  waiting for transfers between devices: 4.48 us -> 5.02 us
    pallas_call x1, Pallas kernels: 4.85 us -> 3.95 us  [inner_part(): pl.pallas_call(functools.partial(inner_kernel, freqs, nx, ny, 0), out_sha...]
    ppermute x6, waiting for transfers between devices: 4.05 us -> 4.59 us  [swap(): return lax.ppermute(cells, names, pairs)]
    pallas_call x1, Pallas kernels: 1.66 us -> 1.12 us  [results(): pl.pallas_call(functools.partial(gradient_kernel, freqs, nx, ny), out_sha...]
    pallas_call x1, Pallas kernels: 3.47 us -> 2.95 us  [rest(): pl.pallas_call(functools.partial(inner_kernel, freqs, nx, ny, 1, None), o...]
  transfers between devices with their start and end apart: 7 -> 7, of which waited for: 3 -> 3; matrix products, arithmetic and copies ran while one was open for 0% -> 0% of each run, Pallas kernels for 28% -> 26%
where the time goes in v6:
time: 45 us; the launch traced here: 44.8 us
  Pallas kernels  17.6 us (39%)
  blocking collectives  14 us (31%)
  starting transfers between devices  6.6 us (15%)
  waiting for transfers between devices  5.02 us (11%)
  other arithmetic  0.87 us (2%)
  between operations  0.71 us (2%)
    all_to_all x1, blocking collectives, on_device(): sums = lax.all_to_all(part, ('gx', 'gy'), 0, 0)  14 us
    ppermute x6, starting transfers between devices, swap(): return lax.ppermute(cells, names, pairs)  6.53 us
    ppermute x6, waiting for transfers between devices, swap(): return lax.ppermute(cells, names, pairs)  4.59 us
    pallas_call x1, Pallas kernels, inner_part(): pl.pallas_call(functools.partial(inner_kernel, freqs, nx, ny, 0), out_sha...  3.95 us
    pallas_call x1, Pallas kernels, early(): pl.pallas_call(functools.partial(early_kernel, freqs, nx, ny), out_shape=...  3.43 us
    pallas_call x1, Pallas kernels, rest(): pl.pallas_call(functools.partial(inner_kernel, freqs, nx, ny, 1, None), o...  2.95 us
    pallas_call x1, Pallas kernels, load(): pl.pallas_call(load_kernel, out_shape=(pltpu.VMEM((2, nx + 2 * HALO, ny +...  2.63 us
    pallas_call x1, Pallas kernels, edge_part(): pl.pallas_call(functools.partial(edge_kernel, peers, freqs, nx, ny), out_...  2.01 us
  transfers between devices with their start and end apart: 7, of which 3 were waited for; matrix products, arithmetic and copies ran while one was open for 0% of the time, Pallas kernels for 26%

profile of v6, /device:TPU:0, one launch (start us, length us, event | category | flops | bytes accessed | tf_op | source)
XLA Modules:
  0.0 44.8 jit_solution(294935409277628546)
XLA Ops:
  0.6 0.0 copy-start
  0.6 2.6 %load.1 = (f32[2,40,40,128]{3,2,1,0:T(8,128)S(1)}, f32[2,40,40,128]{3,2,1,0:T(8,128)S(1)}, f32[32,40,128]{2,1,0:T(8,128)S(1)}, f32[5,40,128]{2,1,0:T(8,128)S(1)}...) custom-call(f32[2,2,32,32,128]{4,3,2,1,0:T(8,128)} %source.1, ...), custom_call_target="tpu_custom_call" | custom-call | tf_op jit(solution)/shard_map/load/pallas_call | solution.py:141
  3.3 3.1 %collective-permute-start.2 = (f32[165,4,128]{2,1,0:T(4,128)S(1)}, f32[165,4,128]{2,1,0:T(4,128)S(1)}, u32[]{:S(2)}, u32[]{:S(2)}) collective-permute-start(f32[165,4,128]{2,1,0:T(4,128)S(1)} %get-tuple-element.61), channel_id=1, source_target_pairs={{0,2},{1,3},{2,0},{3,1},{4,6},{5,7},{6,4},{7,5},{8,10},{9,11},{10,... | collective-permute-start | bytes 1013768 | tf_op jit(solution)/shard_map/ppermute | solution.py:783
  6.4 0.0 collective-permute-start.3
  6.4 1.5 %collective-permute-start = (f32[616,128]{1,0:T(8,128)S(1)}, f32[616,128]{1,0:T(8,128)S(1)}, u32[]{:S(2)}, u32[]{:S(2)}) collective-permute-start(f32[616,128]{1,0:T(8,128)S(1)} %get-tuple-element.59), channel_id=1, source_target_pairs={{0,8},{1,9},{2,10},{3,11},{4,12},{5,13},{6,14},{7,15},{8,0},{9,1},... | collective-permute-start | bytes 946184 | tf_op jit(solution)/shard_map/ppermute | solution.py:783
  7.9 0.2 collective-permute-start.1
  8.1 0.0 copy-done
  8.1 3.4 %early.1 = (f32[2,40,40,128]{3,2,1,0:T(8,128)S(1)}, f32[40,5,8,128]{3,2,1,0:T(8,128)S(1)}, f32[40,5,8,128]{3,2,1,0:T(8,128)S(1)}, f32[2,40,40,128]{3,2,1,0:T(8,1...) custom-call(f32[2]{0:T(128)S(1)} %copy-done, ...), custom_call_target="tpu_custom_call" | custom-call | tf_op jit(solution)/shard_map/early/pallas_call | solution.py:403
  11.5 2.8 %collective-permute-done.2.refs_0_ = f32[165,4,128]{2,1,0:T(4,128)S(1)} collective-permute-done((f32[165,4,128]{2,1,0:T(4,128)S(1)}, f32[165,4,128]{2,1,0:T(4,128)S(1)}, u32[]{:S(2)}, u32[]{:S(2)}) %collective-permute-start.2) | collective-permute-done | bytes 337952 | tf_op jit(solution)/shard_map/ppermute | solution.py:783
  14.3 0.0 collective-permute-done.3.refs_1_
  14.3 4.0 %inner_first.1 = (f32[2,40,40,128]{3,2,1,0:T(8,128)S(1)}, f32[2,40,40,128]{3,2,1,0:T(8,128)S(1)}, f32[32,40,128]{2,1,0:T(8,128)S(1)}, f32[5,40,128]{2,1,0:T(8,12...) custom-call(f32[2,8,128]{2,1,0:T(8,128)S(1)} %get-tuple-element.58.f, ...), custom_call_target="tpu_custom_call", output_to_operand_aliasing={{0}: (3, {}), {1}: (4, {}), {2}: (5, {}), {3}: (6, {}), {4}... | custom-call | tf_op jit(solution)/shard_map/inner_first/pallas_call | solution.py:533
  18.3 1.7 %collective-permute-start.4 = (f32[16,8,128]{2,1,0:T(8,128)S(1)}, f32[16,8,128]{2,1,0:T(8,128)S(1)}, u32[]{:S(2)}, u32[]{:S(2)}) collective-permute-start(f32[16,8,128]{2,1,0:T(8,128)S(1)} %get-tuple-element.70), channel_id=1, source_target_pairs={{0,8},{1,9},{2,10},{3,11},{4,12},{5,13},{6,14},{7,15},{8,0},{9,1},... | collective-permute-start | bytes 196616 | tf_op jit(solution)/shard_map/ppermute | solution.py:783
  20.0 0.0 collective-permute-start.5
  20.0 2.9 %inner_second.1 = (f32[2,40,40,128]{3,2,1,0:T(8,128)S(1)}, f32[2,40,40,128]{3,2,1,0:T(8,128)S(1)}, f32[2,40,40,128]{3,2,1,0:T(8,128)S(1)}, f32[2,40,40,128]{3,2,...) custom-call(f32[2,40,40,128]{3,2,1,0:T(8,128)S(1)} %get-tuple-elemen, ...), custom_call_target="tpu_custom_call", output_to_operand_aliasing={{0}: (9, {}), {1}: (10, {}), {2}: (11, {}), {3}: (12, {}), ... | custom-call | tf_op jit(solution)/shard_map/inner_second/pallas_call | solution.py:548
  22.9 0.0 collective-permute-done.xe
  23.0 0.0 collective-permute-done.1.xo
  23.0 1.8 %collective-permute-done.4.ce = f32[16,8,128]{2,1,0:T(8,128)S(1)} collective-permute-done((f32[16,8,128]{2,1,0:T(8,128)S(1)}, f32[16,8,128]{2,1,0:T(8,128)S(1)}, u32[]{:S(2)}, u32[]{:S(2)}) %collective-permute-start.4) | collective-permute-done | bytes 65568 | tf_op jit(solution)/shard_map/ppermute | solution.py:783
  24.8 0.0 collective-permute-done.5.co
  24.8 2.0 %edge_part.1 = (f32[2,40,40,128]{3,2,1,0:T(8,128)S(1)}, f32[2,40,40,128]{3,2,1,0:T(8,128)S(1)}, f32[2,40,40,128]{3,2,1,0:T(8,128)S(1)}, f32[2,40,40,128]{3,2,1,0...) custom-call(f32[2,8,128]{2,1,0:T(8,128)S(1)} %get-tuple-element.58.f, ...), custom_call_target="tpu_custom_call", output_to_operand_aliasing={{0}: (5, {}), {1}: (6, {}), {2}: (7, {}), {3}: (8, {}), {4}... | custom-call | tf_op jit(solution)/shard_map/edge_part/pallas_call | solution.py:657
  26.8 14.0 %all_to_all.5.sums = f32[16,8,128]{2,1,0:T(8,128)S(1)} all-to-all(f32[16,8,128]{2,1,0:T(8,128)S(1)} %get-tuple-element.95), channel_id=1, replica_groups=mesh['gx'=4,'gy'=4,'af'=2] {'gx','gy'}, dimensions={0} | all-to-all | bytes 131072 | tf_op jit(solution)/shard_map/all_to_all | solution.py:800
  40.8 1.1 %gradient_part.1 = f32[32,32,128]{2,1,0:T(8,128)S(1)} custom-call(f32[2,8,128]{2,1,0:T(8,128)S(1)} %get-tuple-element.58.freq_sq, f32[16,8,128]{2,1,0:T(8,128)S(1)} %all_to_all.5.sums, f32[2,40,40,128]{3,2,1,0:T(8,128)S(1)} %get-tuple-element.100.refs_0_, f32[2,40,40,128]{3,2,1,0:T(8,128)S(1)} %get-tuple-element.96.refs_0_.refs_1_, ...), custom_call_target="tpu_custom_call" | custom-call | tf_op jit(solution)/shard_map/gradient_part/pallas_call | solution.py:745
  41.9 0.1 collective-permute-start.6
  42.0 1.5 %wavefield.1 = f32[2,2,32,32,128]{4,3,2,1,0:T(8,128)} custom-call(f32[16,8,128]{2,1,0:T(8,128)S(1)} %all_to_all.5.sums, f32[2,40,40,128]{3,2,1,0:T(8,128)S(1)} %get-tuple-element.96.refs_0_.refs_1_, f32[2,40,40,128]{3,2,1,0:T(8,128)S(1)} %get-tuple-element.97.refs_1_.refs_3_, f32[2,40,40,128]{3,2,1,0:T(8,128)S(1)} %get-tuple-element.98.refs_2_.refs_6_, ...), custom_call_target="tpu_custom_call" | custom-call | tf_op jit(solution)/shard_map/wavefield/pallas_call | solution.py:753
  43.5 0.4 collective-permute-done.6
  43.9 0.9 %add.3 = f32[32,32,128]{2,1,0:T(8,128)} add(f32[32,32,128]{2,1,0:T(8,128)S(1)} %gradient_part.1, f32[32,32,128]{2,1,0:T(8,128)S(1)} %collective-permute-done.6) | non-fusion elementwise | flops 131072 | bytes 1572864 | tf_op jit(solution)/shard_map/add | solution.py:803
Async XLA Ops:
  0.6 7.5 %copy-start = (f32[2]{0:T(128)S(1)}, f32[2]{0:T(128)}, u32[]{:S(2)}) copy-start(f32[2]{0:T(128)} %freq_sq.1) | copy-start | bytes 28
  3.3 11.0 %collective-permute-start.2 = (f32[165,4,128]{2,1,0:T(4,128)S(1)}, f32[165,4,128]{2,1,0:T(4,128)S(1)}, u32[]{:S(2)}, u32[]{:S(2)}) collective-permute-start(f32[165,4,128]{2,1,0:T(4,128)S(1)} %get-tuple-element.61), channel_id=1, source_target_pairs={{0,2},{1,3},{2,0},{3,1},{4,6},{5,7},{6,4},{7,5},{8,10},{9,11},{10,... | collective-permute-start | bytes 1013768 | tf_op jit(solution)/shard_map/ppermute | solution.py:783
  6.4 7.9 %collective-permute-start.3 = (f32[165,4,128]{2,1,0:T(4,128)S(1)}, f32[165,4,128]{2,1,0:T(4,128)S(1)}, u32[]{:S(2)}, u32[]{:S(2)}) collective-permute-start(f32[165,4,128]{2,1,0:T(4,128)S(1)} %get-tuple-element.62), channel_id=1, source_target_pairs={{0,1},{1,0},{2,4},{3,5},{4,2},{5,3},{6,7},{7,6},{8,9},{9,8},{10,12... | collective-permute-start | bytes 1013768 | tf_op jit(solution)/shard_map/ppermute | solution.py:783
  6.4 16.6 %collective-permute-start = (f32[616,128]{1,0:T(8,128)S(1)}, f32[616,128]{1,0:T(8,128)S(1)}, u32[]{:S(2)}, u32[]{:S(2)}) collective-permute-start(f32[616,128]{1,0:T(8,128)S(1)} %get-tuple-element.59), channel_id=1, source_target_pairs={{0,8},{1,9},{2,10},{3,11},{4,12},{5,13},{6,14},{7,15},{8,0},{9,1},... | collective-permute-start | bytes 946184 | tf_op jit(solution)/shard_map/ppermute | solution.py:783
  7.9 15.1 %collective-permute-start.1 = (f32[616,128]{1,0:T(8,128)S(1)}, f32[616,128]{1,0:T(8,128)S(1)}, u32[]{:S(2)}, u32[]{:S(2)}) collective-permute-start(f32[616,128]{1,0:T(8,128)S(1)} %get-tuple-element.60), channel_id=1, source_target_pairs={{0,1},{1,0},{2,3},{3,2},{4,5},{5,4},{6,7},{7,6},{8,16},{9,17},{10,... | collective-permute-start | bytes 946184 | tf_op jit(solution)/shard_map/ppermute | solution.py:783
  18.3 6.5 %collective-permute-start.4 = (f32[16,8,128]{2,1,0:T(8,128)S(1)}, f32[16,8,128]{2,1,0:T(8,128)S(1)}, u32[]{:S(2)}, u32[]{:S(2)}) collective-permute-start(f32[16,8,128]{2,1,0:T(8,128)S(1)} %get-tuple-element.70), channel_id=1, source_target_pairs={{0,8},{1,9},{2,10},{3,11},{4,12},{5,13},{6,14},{7,15},{8,0},{9,1},... | collective-permute-start | bytes 196616 | tf_op jit(solution)/shard_map/ppermute | solution.py:783
  20.0 4.8 %collective-permute-start.5 = (f32[16,8,128]{2,1,0:T(8,128)S(1)}, f32[16,8,128]{2,1,0:T(8,128)S(1)}, u32[]{:S(2)}, u32[]{:S(2)}) collective-permute-start(f32[16,8,128]{2,1,0:T(8,128)S(1)} %get-tuple-element.71), channel_id=1, source_target_pairs={{0,1},{1,0},{2,3},{3,2},{4,5},{5,4},{6,7},{7,6},{8,16},{9,17},{10,... | collective-permute-start | bytes 196616 | tf_op jit(solution)/shard_map/ppermute | solution.py:783
  41.9 2.0 %collective-permute-start.6 = (f32[32,32,128]{2,1,0:T(8,128)S(1)}, f32[32,32,128]{2,1,0:T(8,128)S(1)}, u32[]{:S(2)}, u32[]{:S(2)}) collective-permute-start(f32[32,32,128]{2,1,0:T(8,128)S(1)} %gradient_part.1), channel_id=1, source_target_pairs={{0,1},{1,0},{2,3},{3,2},{4,5},{5,4},{6,7},{7,6},{8,9},{9,8},{10,11... | collective-permute-start | bytes 1572872 | tf_op jit(solution)/shard_map/ppermute | solution.py:803

commit v7 on v6

--- a/solution.py
+++ b/solution.py
@@ -413,16 +413,57 @@
 def corner_faces(freqs, nx, ny, s, cells, aux, ce, co):
     fields = 2 * freqs
     nz = cells.shape[2]
+    sub = lax.broadcasted_iota(jnp.int32, (2 * HALO, nz), 0)
     even_x = parity("gx")
     near = [aux[k, ny:, :] for k in range(fields + 1)]
     for side, cb in enumerate((ce, co)):
         last = even_x if side == 0 else jnp.logical_not(even_x)
-        at = jnp.where(last, nx - INNER, 0)
-        for layer in range(INNER):
-            for k in range(fields):
-                cb[k * INNER + layer] = s[k // 2][k % 2, at + layer, ny:, :]
-            cb[fields * INNER + layer] = cells[at + layer, ny:, :]
-        cb[(fields + 1) * INNER] = lane_slab(near, fields, at, 2 * HALO, nz)
+        at = [jnp.where(last, nx - d, d - 1) for d in range(1, HALO)]
+        for k in range(fields):
+            one, two, three = (s[k // 2][k % 2, x, ny:, :] for x in at)
+            one = jnp.where(sub == 3, pltpu.roll(three, 3, axis=0), one)
+            cb[k] = jnp.where(sub == 4, pltpu.roll(three, 5, axis=0), one)
+            if k % 2 == 0:
+                kept = two
+                continue
+            two = jnp.where(
+                sub < 4, pltpu.roll(two, 2, axis=0), pltpu.roll(two, 6, axis=0)
+            )
+            outer = (sub < 2) | (sub > 5)
+            cb[fields + k // 2] = jnp.where(outer, kept, two)
+        one, two = cells[at[0], ny:, :], cells[at[1], ny:, :]
+        one = jnp.where(sub == 2, pltpu.roll(two, 2, axis=0), one)
+        cb[fields + freqs] = jnp.where(sub == 5, pltpu.roll(two, 6, axis=0), one)
+        skip = jnp.where(last, nx - INNER, 0)
+        cb[fields + freqs + 1] = lane_slab(near, fields, skip, 2 * HALO, nz)
+
+
+def place_corners(freqs, nx, ny, cb, s, cells, aux, above):
+    fields = 2 * freqs
+    nz = cb.shape[2]
+    sub = lax.broadcasted_iota(jnp.int32, (2 * HALO, nz), 0)
+    slot = [jnp.where(above, nx + d - 1, nx + 2 * HALO - d) for d in range(1, HALO)]
+    layer = [jnp.where(above, d - 1, INNER - d) for d in range(1, HALO)]
+    for k in range(fields):
+        field, p = s[k // 2], k % 2
+        one = cb[k]
+        field[p, slot[0], ny:, :] = one
+        field[p, slot[2], ny:, :] = jnp.where(
+            sub == 0, pltpu.roll(one, 5, axis=0), pltpu.roll(one, 3, axis=0)
+        )
+        two = cb[fields + k // 2]
+        if p:
+            two = jnp.where(
+                sub < 4, pltpu.roll(two, 6, axis=0), pltpu.roll(two, 2, axis=0)
+            )
+        field[p, slot[1], ny:, :] = two
+    one = cb[fields + freqs]
+    cells[layer[0], ny:, :] = one
+    cells[layer[1], ny:, :] = jnp.where(
+        sub == 0, pltpu.roll(one, 6, axis=0), pltpu.roll(one, 2, axis=0)
+    )
+    cells[layer[2], ny:, :] = jnp.zeros((2 * HALO, nz), F32)
+    aux[ny:, :] = cb[fields + freqs + 1]
 
 
 def inner_kernel(freqs, nx, ny, half, freq_sq, *refs):
@@ -525,7 +566,7 @@
 def inner_part(nx, ny, freq_sq, ye, yo, s, cells, aux, known):
     freqs = len(s)
     nz = cells.shape[2]
-    slabs = (2 * freqs + 1) * INNER + 1
+    slabs = 3 * freqs + 2
     field = pltpu.VMEM(s[0].shape, F32)
     corner = pltpu.VMEM((slabs, 2 * HALO, nz), F32)
     kept = (*s, cells, aux, *known)
@@ -574,7 +615,6 @@
     for side, (xb, cb) in enumerate(((xe, ce), (xo, co))):
         above = even_x if side == 0 else jnp.logical_not(even_x)
         slot = jnp.where(above, nx, nx + HALO)
-        near = jnp.where(above, nx, nx + HALO + 1)
         half = jnp.where(above, 0, 1)
         for layer in range(HALO):
             for k in range(fields):
@@ -582,19 +622,18 @@
                 for y in range(0, ny, 8):
                     row = (k * HALO + layer) * ny + y
                     block[k % 2, slot + layer, y : y + 8, :] = xb[row : row + 8, :]
-                if layer < INNER:
-                    block[k % 2, near + layer, ny:, :] = cb[k * INNER + layer]
             if layer < INNER:
                 for y in range(0, ny, 8):
                     row = (fields * HALO + layer) * ny + y
                     cells[half, layer, y : y + 8, :] = xb[row : row + 8, :]
-                cells[half, layer, ny:, :] = cb[fields * INNER + layer]
         at = (fields * HALO + INNER) * ny
         folded = xb[at : at + ny // 8, :]
         for g in range(8):
             rows = pl.ds(g * (ny // 8), ny // 8)
             aux[half, rows, :] = pltpu.roll(folded, (nz - g * group) % nz, axis=1)
-        aux[half, ny:, :] = cb[(fields + 1) * INNER]
+        place_corners(
+            freqs, nx, ny, cb, state[: 7 * freqs : 7], cells.at[half], aux.at[half], above
+        )
     for k in range(fields):
         for i in (nx + HALO - 1, nx + HALO):
             state[7 * (k // 2)][k % 2, i, ny:, :] = jnp.zeros((2 * HALO, nz), F32)
@@ -765,6 +804,37 @@
     return gradient, wave
 
 
+def add_kernel(one, two, out, block, sem):
+    nx, ny, _ = one.shape
+    copies = Copies(sem)
+    parts = sem.shape[0]
+    step = nx // parts
+    for part in range(parts):
+
+        def row(x, _):
+            for y in range(0, ny, 8):
+                at = pl.ds(y, 8)
+                block[x, at, :] = one[x, at, :] + two[x, at, :]
+            return 0
+
+        lax.fori_loop(part * step, (part + 1) * step, row, 0, unroll=4)
+        span = pl.ds(part * step, step)
+        copies.add(block.at[span], out.at[span])
+    copies.wait()
+
+
+def add(one, two):
+    return pl.pallas_call(
+        add_kernel,
+        out_shape=jax.ShapeDtypeStruct(one.shape, F32),
+        in_specs=[VMEM] * 2,
+        out_specs=HBM,
+        scratch_shapes=[pltpu.VMEM(one.shape, F32), pltpu.SemaphoreType.DMA((2,))],
+        compiler_params=params(4),
+        name="add",
+    )(one, two)
+
+
 def swap(cells, axis, odd):
     names = ("gx", "gy", "af")
     sizes = [lax.axis_size(name) for name in names]
@@ -800,7 +870,7 @@
     sums = lax.all_to_all(part, ("gx", "gy"), 0, 0)
     gradient, wave = results(freqs, nx, ny, splat, sums, state)
     if lax.axis_size("af") == 2:
-        gradient = gradient + lax.ppermute(gradient, "af", [(0, 1), (1, 0)])
+        gradient = add(gradient, lax.ppermute(gradient, "af", [(0, 1), (1, 0)]))
     else:
         gradient = lax.psum(gradient, "af")
     return wave, gradient

time: 45 us -> 44.4 us (0.987)
  other arithmetic: 0.87 us -> 0 us
  Pallas kernels: 17.6 us -> 18.4 us
  waiting for transfers between devices: 5.02 us -> 4.28 us
    add x1 -> x0, other arithmetic: 0.87 us -> none  [on_device(): gradient = gradient + lax.ppermute(gradient, 'af', [(0, 1), (1, 0)])]
    pallas_call x0 -> x1, Pallas kernels: none -> 0.84 us  [add(): pl.pallas_call(add_kernel, out_shape=jax.ShapeDtypeStruct(one.shape, F32)...]
    ppermute x6, waiting for transfers between devices: 4.59 us -> 3.85 us  [swap(): return lax.ppermute(cells, names, pairs)]
  transfers between devices with their start and end apart: 7 -> 7, of which waited for: 3 -> 3; matrix products, arithmetic and copies ran while one was open for 0% -> 0% of each run, Pallas kernels for 26% -> 27%
where the time goes in v7:
time: 44.4 us; the launch traced here: 44.2 us
  Pallas kernels  18.4 us (41%)
  blocking collectives  14.2 us (32%)
  starting transfers between devices  6.6 us (15%)
  waiting for transfers between devices  4.28 us (10%)
  between operations  0.71 us (2%)
    all_to_all x1, blocking collectives, on_device(): sums = lax.all_to_all(part, ('gx', 'gy'), 0, 0)  14.2 us
    ppermute x6, starting transfers between devices, swap(): return lax.ppermute(cells, names, pairs)  6.53 us
    pallas_call x1, Pallas kernels, inner_part(): pl.pallas_call(functools.partial(inner_kernel, freqs, nx, ny, 0), out_sha...  3.96 us
    ppermute x6, waiting for transfers between devices, swap(): return lax.ppermute(cells, names, pairs)  3.85 us
    pallas_call x1, Pallas kernels, early(): pl.pallas_call(functools.partial(early_kernel, freqs, nx, ny), out_shape=...  3.43 us
    pallas_call x1, Pallas kernels, rest(): pl.pallas_call(functools.partial(inner_kernel, freqs, nx, ny, 1, None), o...  2.95 us
    pallas_call x1, Pallas kernels, load(): pl.pallas_call(load_kernel, out_shape=(pltpu.VMEM((2, nx + 2 * HALO, ny +...  2.63 us
    pallas_call x1, Pallas kernels, edge_part(): pl.pallas_call(functools.partial(edge_kernel, peers, freqs, nx, ny), out_...  2 us
  transfers between devices with their start and end apart: 7, of which 3 were waited for; matrix products, arithmetic and copies ran while one was open for 0% of the time, Pallas kernels for 27%

profile of v7, /device:TPU:0, one launch (start us, length us, event | category | flops | bytes accessed | tf_op | source)
XLA Modules:
  0.0 44.2 jit_solution(10564442568875027717)
XLA Ops:
  0.6 0.0 copy-start
  0.6 2.6 %load.1 = (f32[2,40,40,128]{3,2,1,0:T(8,128)S(1)}, f32[2,40,40,128]{3,2,1,0:T(8,128)S(1)}, f32[32,40,128]{2,1,0:T(8,128)S(1)}, f32[5,40,128]{2,1,0:T(8,128)S(1)}...) custom-call(f32[2,2,32,32,128]{4,3,2,1,0:T(8,128)} %source.1, ...), custom_call_target="tpu_custom_call" | custom-call | tf_op jit(solution)/shard_map/load/pallas_call | solution.py:141
  3.3 3.1 %collective-permute-start.2 = (f32[165,4,128]{2,1,0:T(4,128)S(1)}, f32[165,4,128]{2,1,0:T(4,128)S(1)}, u32[]{:S(2)}, u32[]{:S(2)}) collective-permute-start(f32[165,4,128]{2,1,0:T(4,128)S(1)} %get-tuple-element.61), channel_id=1, source_target_pairs={{0,2},{1,3},{2,0},{3,1},{4,6},{5,7},{6,4},{7,5},{8,10},{9,11},{10,... | collective-permute-start | bytes 1013768 | tf_op jit(solution)/shard_map/ppermute | solution.py:853
  6.4 0.0 collective-permute-start.3
  6.4 1.5 %collective-permute-start = (f32[616,128]{1,0:T(8,128)S(1)}, f32[616,128]{1,0:T(8,128)S(1)}, u32[]{:S(2)}, u32[]{:S(2)}) collective-permute-start(f32[616,128]{1,0:T(8,128)S(1)} %get-tuple-element.59), channel_id=1, source_target_pairs={{0,8},{1,9},{2,10},{3,11},{4,12},{5,13},{6,14},{7,15},{8,0},{9,1},... | collective-permute-start | bytes 946184 | tf_op jit(solution)/shard_map/ppermute | solution.py:853
  7.9 0.2 collective-permute-start.1
  8.1 0.0 copy-done
  8.1 3.4 %early.1 = (f32[2,40,40,128]{3,2,1,0:T(8,128)S(1)}, f32[40,5,8,128]{3,2,1,0:T(8,128)S(1)}, f32[40,5,8,128]{3,2,1,0:T(8,128)S(1)}, f32[2,40,40,128]{3,2,1,0:T(8,1...) custom-call(f32[2]{0:T(128)S(1)} %copy-done, ...), custom_call_target="tpu_custom_call" | custom-call | tf_op jit(solution)/shard_map/early/pallas_call | solution.py:403
  11.5 2.8 %collective-permute-done.2.refs_0_ = f32[165,4,128]{2,1,0:T(4,128)S(1)} collective-permute-done((f32[165,4,128]{2,1,0:T(4,128)S(1)}, f32[165,4,128]{2,1,0:T(4,128)S(1)}, u32[]{:S(2)}, u32[]{:S(2)}) %collective-permute-start.2) | collective-permute-done | bytes 337952 | tf_op jit(solution)/shard_map/ppermute | solution.py:853
  14.3 0.0 collective-permute-done.3.refs_1_
  14.3 4.0 %inner_first.1 = (f32[2,40,40,128]{3,2,1,0:T(8,128)S(1)}, f32[2,40,40,128]{3,2,1,0:T(8,128)S(1)}, f32[32,40,128]{2,1,0:T(8,128)S(1)}, f32[5,40,128]{2,1,0:T(8,12...) custom-call(f32[2,8,128]{2,1,0:T(8,128)S(1)} %get-tuple-element.58.f, ...), custom_call_target="tpu_custom_call", output_to_operand_aliasing={{0}: (3, {}), {1}: (4, {}), {2}: (5, {}), {3}: (6, {}), {4}... | custom-call | tf_op jit(solution)/shard_map/inner_first/pallas_call | solution.py:574
  18.3 1.7 %collective-permute-start.4 = (f32[8,8,128]{2,1,0:T(8,128)S(1)}, f32[8,8,128]{2,1,0:T(8,128)S(1)}, u32[]{:S(2)}, u32[]{:S(2)}) collective-permute-start(f32[8,8,128]{2,1,0:T(8,128)S(1)} %get-tuple-element.70), channel_id=1, source_target_pairs={{0,8},{1,9},{2,10},{3,11},{4,12},{5,13},{6,14},{7,15},{8,0},{9,1},... | collective-permute-start | bytes 98312 | tf_op jit(solution)/shard_map/ppermute | solution.py:853
  20.0 0.0 collective-permute-start.5
  20.0 2.9 %inner_second.1 = (f32[2,40,40,128]{3,2,1,0:T(8,128)S(1)}, f32[2,40,40,128]{3,2,1,0:T(8,128)S(1)}, f32[2,40,40,128]{3,2,1,0:T(8,128)S(1)}, f32[2,40,40,128]{3,2,...) custom-call(f32[2,40,40,128]{3,2,1,0:T(8,128)S(1)} %get-tuple-elemen, ...), custom_call_target="tpu_custom_call", output_to_operand_aliasing={{0}: (9, {}), {1}: (10, {}), {2}: (11, {}), {3}: (12, {}), ... | custom-call | tf_op jit(solution)/shard_map/inner_second/pallas_call | solution.py:589
  22.9 0.0 collective-permute-done.xe
  23.0 0.0 collective-permute-done.1.xo
  23.0 1.1 %collective-permute-done.4.ce = f32[8,8,128]{2,1,0:T(8,128)S(1)} collective-permute-done((f32[8,8,128]{2,1,0:T(8,128)S(1)}, f32[8,8,128]{2,1,0:T(8,128)S(1)}, u32[]{:S(2)}, u32[]{:S(2)}) %collective-permute-start.4) | collective-permute-done | bytes 32800 | tf_op jit(solution)/shard_map/ppermute | solution.py:853
  24.0 0.0 collective-permute-done.5.co
  24.0 2.0 %edge_part.1 = (f32[2,40,40,128]{3,2,1,0:T(8,128)S(1)}, f32[2,40,40,128]{3,2,1,0:T(8,128)S(1)}, f32[2,40,40,128]{3,2,1,0:T(8,128)S(1)}, f32[2,40,40,128]{3,2,1,0...) custom-call(f32[2,8,128]{2,1,0:T(8,128)S(1)} %get-tuple-element.58.f, ...), custom_call_target="tpu_custom_call", output_to_operand_aliasing={{0}: (5, {}), {1}: (6, {}), {2}: (7, {}), {3}: (8, {}), {4}... | custom-call | tf_op jit(solution)/shard_map/edge_part/pallas_call | solution.py:696
  26.1 14.2 %all_to_all.5.sums = f32[16,8,128]{2,1,0:T(8,128)S(1)} all-to-all(f32[16,8,128]{2,1,0:T(8,128)S(1)} %get-tuple-element.95), channel_id=1, replica_groups=mesh['gx'=4,'gy'=4,'af'=2] {'gx','gy'}, dimensions={0} | all-to-all | bytes 131072 | tf_op jit(solution)/shard_map/all_to_all | solution.py:870
  40.3 1.1 %gradient_part.1.one = f32[32,32,128]{2,1,0:T(8,128)S(1)} custom-call(f32[2,8,128]{2,1,0:T(8,128)S(1)} %get-tuple-element.58.freq_sq, f32[16,8,128]{2,1,0:T(8,128)S(1)} %all_to_all.5.sums, f32[2,40,40,128]{3,2,1,0:T(8,128)S(1)} %get-tuple-element.100.refs_0_, f32[2,40,40,128]{3,2,1,0:T(8,128)S(1)} %get-tuple-element.96.refs_0_.refs_1_, ...), custom_call_target="tpu_custom_call" | custom-call | tf_op jit(solution)/shard_map/gradient_part/pallas_call | solution.py:784
  41.4 0.1 collective-permute-start.6
  41.5 1.5 %wavefield.1 = f32[2,2,32,32,128]{4,3,2,1,0:T(8,128)} custom-call(f32[16,8,128]{2,1,0:T(8,128)S(1)} %all_to_all.5.sums, f32[2,40,40,128]{3,2,1,0:T(8,128)S(1)} %get-tuple-element.96.refs_0_.refs_1_, f32[2,40,40,128]{3,2,1,0:T(8,128)S(1)} %get-tuple-element.97.refs_1_.refs_3_, f32[2,40,40,128]{3,2,1,0:T(8,128)S(1)} %get-tuple-element.98.refs_2_.refs_6_, ...), custom_call_target="tpu_custom_call" | custom-call | tf_op jit(solution)/shard_map/wavefield/pallas_call | solution.py:792
  42.9 0.4 collective-permute-done.6.two
  43.4 0.8 %add.1 = f32[32,32,128]{2,1,0:T(8,128)} custom-call(f32[32,32,128]{2,1,0:T(8,128)S(1)} %gradient_part.1.one, f32[32,32,128]{2,1,0:T(8,128)S(1)} %collective-permute-done.6.two), custom_call_target="tpu_custom_call" | custom-call | tf_op jit(solution)/shard_map/add/pallas_call | solution.py:827
Async XLA Ops:
  0.6 7.5 %copy-start = (f32[2]{0:T(128)S(1)}, f32[2]{0:T(128)}, u32[]{:S(2)}) copy-start(f32[2]{0:T(128)} %freq_sq.1) | copy-start | bytes 28
  3.3 11.0 %collective-permute-start.2 = (f32[165,4,128]{2,1,0:T(4,128)S(1)}, f32[165,4,128]{2,1,0:T(4,128)S(1)}, u32[]{:S(2)}, u32[]{:S(2)}) collective-permute-start(f32[165,4,128]{2,1,0:T(4,128)S(1)} %get-tuple-element.61), channel_id=1, source_target_pairs={{0,2},{1,3},{2,0},{3,1},{4,6},{5,7},{6,4},{7,5},{8,10},{9,11},{10,... | collective-permute-start | bytes 1013768 | tf_op jit(solution)/shard_map/ppermute | solution.py:853
  6.4 7.9 %collective-permute-start.3 = (f32[165,4,128]{2,1,0:T(4,128)S(1)}, f32[165,4,128]{2,1,0:T(4,128)S(1)}, u32[]{:S(2)}, u32[]{:S(2)}) collective-permute-start(f32[165,4,128]{2,1,0:T(4,128)S(1)} %get-tuple-element.62), channel_id=1, source_target_pairs={{0,1},{1,0},{2,4},{3,5},{4,2},{5,3},{6,7},{7,6},{8,9},{9,8},{10,12... | collective-permute-start | bytes 1013768 | tf_op jit(solution)/shard_map/ppermute | solution.py:853
  6.4 16.6 %collective-permute-start = (f32[616,128]{1,0:T(8,128)S(1)}, f32[616,128]{1,0:T(8,128)S(1)}, u32[]{:S(2)}, u32[]{:S(2)}) collective-permute-start(f32[616,128]{1,0:T(8,128)S(1)} %get-tuple-element.59), channel_id=1, source_target_pairs={{0,8},{1,9},{2,10},{3,11},{4,12},{5,13},{6,14},{7,15},{8,0},{9,1},... | collective-permute-start | bytes 946184 | tf_op jit(solution)/shard_map/ppermute | solution.py:853
  7.9 15.1 %collective-permute-start.1 = (f32[616,128]{1,0:T(8,128)S(1)}, f32[616,128]{1,0:T(8,128)S(1)}, u32[]{:S(2)}, u32[]{:S(2)}) collective-permute-start(f32[616,128]{1,0:T(8,128)S(1)} %get-tuple-element.60), channel_id=1, source_target_pairs={{0,1},{1,0},{2,3},{3,2},{4,5},{5,4},{6,7},{7,6},{8,16},{9,17},{10,... | collective-permute-start | bytes 946184 | tf_op jit(solution)/shard_map/ppermute | solution.py:853
  18.3 5.8 %collective-permute-start.4 = (f32[8,8,128]{2,1,0:T(8,128)S(1)}, f32[8,8,128]{2,1,0:T(8,128)S(1)}, u32[]{:S(2)}, u32[]{:S(2)}) collective-permute-start(f32[8,8,128]{2,1,0:T(8,128)S(1)} %get-tuple-element.70), channel_id=1, source_target_pairs={{0,8},{1,9},{2,10},{3,11},{4,12},{5,13},{6,14},{7,15},{8,0},{9,1},... | collective-permute-start | bytes 98312 | tf_op jit(solution)/shard_map/ppermute | solution.py:853
  20.0 4.1 %collective-permute-start.5 = (f32[8,8,128]{2,1,0:T(8,128)S(1)}, f32[8,8,128]{2,1,0:T(8,128)S(1)}, u32[]{:S(2)}, u32[]{:S(2)}) collective-permute-start(f32[8,8,128]{2,1,0:T(8,128)S(1)} %get-tuple-element.71), channel_id=1, source_target_pairs={{0,1},{1,0},{2,3},{3,2},{4,5},{5,4},{6,7},{7,6},{8,16},{9,17},{10,... | collective-permute-start | bytes 98312 | tf_op jit(solution)/shard_map/ppermute | solution.py:853
  41.4 2.0 %collective-permute-start.6 = (f32[32,32,128]{2,1,0:T(8,128)S(1)}, f32[32,32,128]{2,1,0:T(8,128)S(1)}, u32[]{:S(2)}, u32[]{:S(2)}) collective-permute-start(f32[32,32,128]{2,1,0:T(8,128)S(1)} %gradient_part.1.one), channel_id=1, source_target_pairs={{0,1},{1,0},{2,3},{3,2},{4,5},{5,4},{6,7},{7,6},{8,9},{9,8},{10,11... | collective-permute-start | bytes 1572872 | tf_op jit(solution)/shard_map/ppermute | solution.py:873

commit v8 on v7

--- a/solution.py
+++ b/solution.py
@@ -20,7 +20,7 @@
 SMEM = pl.BlockSpec(memory_space=pltpu.SMEM)
 MIB = 1 << 20
 LOAD_MIB = 55
-SHIFT = 2
+SHIFT = -4
 
 
 def params(mib):
@@ -116,12 +116,35 @@
                 row = (to + layer) * ny + y
                 xb[row : row + 8, :] = block[at + layer, y : y + 8, :]
 
-    for k in range(fields + 1):
-        head, tail = table[k, 0:HALO, :], table[k, ny - HALO : ny, :]
-        ye[(fields + 1) * nx + k] = jnp.where(swapped, tail, head)
-        yo[(fields + 1) * nx + k] = jnp.where(swapped, head, tail)
+    lane = lax.broadcasted_iota(jnp.int32, (HALO, nz), 1)
+    at = fields * nx + nx // 4 * 3
+    for slab in range(-(-(fields + 1) // (nz // nx))):
+        pair = [jnp.zeros((HALO, nz), F32)] * 2
+        for g in range(nz // nx):
+            k = slab * (nz // nx) + g
+            if k > fields:
+                continue
+            inside = (lane >= g * nx) & (lane < (g + 1) * nx)
+            for end, rows in enumerate((table[k, 0:HALO, :], table[k, ny - HALO : ny, :])):
+                moved = pltpu.roll(rows, g * nx, axis=1)
+                pair[end] = jnp.where(inside, moved, pair[end])
+        ye[at + slab] = jnp.where(swapped, pair[1], pair[0])
+        yo[at + slab] = jnp.where(swapped, pair[0], pair[1])
     large.all[0].wait()
-    y_faces(cells, fields * nx)
+    sub = lax.broadcasted_iota(jnp.int32, (8, nz), 0)
+
+    def model_rows(g, _):
+        heads = [cells[4 * g + j, 0:8, :] for j in range(4)]
+        tails = [cells[4 * g + j, ny - 8 : ny, :] for j in range(4)]
+        for j in range(3):
+            head = jnp.where(sub == 3, pltpu.roll(heads[3], 3 - j, axis=0), heads[j])
+            tail = jnp.where(sub == 4, pltpu.roll(tails[3], 7 - j, axis=0), tails[j])
+            head, tail = head[0:HALO, :], tail[8 - HALO : 8, :]
+            ye[fields * nx + 3 * g + j] = jnp.where(swapped, tail, head)
+            yo[fields * nx + 3 * g + j] = jnp.where(swapped, head, tail)
+        return 0
+
+    lax.fori_loop(0, nx // 4, model_rows, 0, unroll=2)
     for xb, skip, _ in faces:
         x_face(xb, fields * HALO, cells, skip, INNER)
     for k in range(fields):
@@ -137,7 +160,8 @@
     freqs, _, nx, ny, nz = source.shape
     fields = 2 * freqs
     xs = pltpu.VMEM(((fields * HALO + INNER) * ny + 8, nz), F32)
-    ys = pltpu.VMEM(((fields + 1) * nx + fields + 1, HALO, nz), F32)
+    slabs = fields * nx + nx // 4 * 3 + -(-(fields + 1) // (nz // nx))
+    ys = pltpu.VMEM((slabs, HALO, nz), F32)
     return pl.pallas_call(
         load_kernel,
         out_shape=(pltpu.VMEM((2, nx + 2 * HALO, ny + 2 * HALO, nz), F32),) * freqs
@@ -497,15 +521,29 @@
             low = jnp.where(swapped, odd, even) * grid.left
             return jnp.concatenate([high, low], axis=0)
 
+        sub = lax.broadcasted_iota(jnp.int32, (8, nz), 0)
+
+        def model_rows(g, _):
+            tiles = [halo(fields * nx + 3 * g + j) for j in range(3)]
+            last = tiles[0]
+            for j in range(3):
+                cells[4 * g + j, ny:, :] = tiles[j]
+                last = jnp.where(sub == j, pltpu.roll(tiles[j], 5 + j, axis=0), last)
+                last = jnp.where(sub == 5 + j, pltpu.roll(tiles[j], 1 + j, axis=0), last)
+            cells[4 * g + 3, ny:, :] = last
+            return 0
+
         def merge(x, _):
-            cells[x, ny:, :] = halo(fields * nx + x)
             for k in range(fields):
                 s[k // 2][k % 2, x, ny:, :] = halo(k * nx + x)
             return 0
 
+        lax.fori_loop(0, nx // 4, model_rows, 0, unroll=2)
         lax.fori_loop(0, nx, merge, 0, unroll=4)
         for k in range(fields + 1):
-            aux[k, ny:, :] = halo((fields + 1) * nx + k)
+            slab, g = divmod(k, nz // nx)
+            tile = halo(fields * nx + nx // 4 * 3 + slab)
+            aux[k, ny:, :] = pltpu.roll(tile, (nz - g * nx) % nz, axis=1) if g else tile
         corner_faces(freqs, nx, ny, s, cells, aux, ce, co)
 
     def prepare(i):

time: 44.4 us -> 43.6 us (0.982)
  blocking collectives: 14.2 us -> 13.5 us
    pallas_call x1, Pallas kernels: 2.95 us -> 4.16 us  [rest(): pl.pallas_call(functools.partial(inner_kernel, freqs, nx, ny, 1, None), o...]
    pallas_call x1, Pallas kernels: 3.96 us -> 2.81 us  [inner_part(): pl.pallas_call(functools.partial(inner_kernel, freqs, nx, ny, 0), out_sha...]
    all_to_all x1, blocking collectives: 14.2 us -> 13.5 us  [on_device(): sums = lax.all_to_all(part, ('gx', 'gy'), 0, 0)]
where the time goes in v8:
time: 43.6 us; the launch traced here: 43.5 us
  Pallas kernels  18.5 us (42%)
  blocking collectives  13.5 us (31%)
  starting transfers between devices  6.6 us (15%)
  waiting for transfers between devices  4.21 us (10%)
  between operations  0.71 us (2%)
    all_to_all x1, blocking collectives, on_device(): sums = lax.all_to_all(part, ('gx', 'gy'), 0, 0)  13.5 us
    ppermute x6, starting transfers between devices, swap(): return lax.ppermute(cells, names, pairs)  6.53 us
    pallas_call x1, Pallas kernels, rest(): pl.pallas_call(functools.partial(inner_kernel, freqs, nx, ny, 1, None), o...  4.16 us
    ppermute x6, waiting for transfers between devices, swap(): return lax.ppermute(cells, names, pairs)  3.79 us
    pallas_call x1, Pallas kernels, early(): pl.pallas_call(functools.partial(early_kernel, freqs, nx, ny), out_shape=...  3.43 us
    pallas_call x1, Pallas kernels, inner_part(): pl.pallas_call(functools.partial(inner_kernel, freqs, nx, ny, 0), out_sha...  2.81 us
    pallas_call x1, Pallas kernels, load(): pl.pallas_call(load_kernel, out_shape=(pltpu.VMEM((2, nx + 2 * HALO, ny +...  2.63 us
    pallas_call x1, Pallas kernels, edge_part(): pl.pallas_call(functools.partial(edge_kernel, peers, freqs, nx, ny), out_...  2 us
  transfers between devices with their start and end apart: 7, of which 3 were waited for; matrix products, arithmetic and copies ran while one was open for 0% of the time, Pallas kernels for 27%

profile of v8, /device:TPU:0, one launch (start us, length us, event | category | flops | bytes accessed | tf_op | source)
XLA Modules:
  0.0 43.5 jit_solution(6231431016309484763)
XLA Ops:
  0.6 0.0 copy-start
  0.6 2.6 %load.1 = (f32[2,40,40,128]{3,2,1,0:T(8,128)S(1)}, f32[2,40,40,128]{3,2,1,0:T(8,128)S(1)}, f32[32,40,128]{2,1,0:T(8,128)S(1)}, f32[5,40,128]{2,1,0:T(8,128)S(1)}...) custom-call(f32[2,2,32,32,128]{4,3,2,1,0:T(8,128)} %source.1, ...), custom_call_target="tpu_custom_call" | custom-call | tf_op jit(solution)/shard_map/load/pallas_call | solution.py:165
  3.3 3.1 %collective-permute-start.2 = (f32[154,4,128]{2,1,0:T(4,128)S(1)}, f32[154,4,128]{2,1,0:T(4,128)S(1)}, u32[]{:S(2)}, u32[]{:S(2)}) collective-permute-start(f32[154,4,128]{2,1,0:T(4,128)S(1)} %get-tuple-element.61), channel_id=1, source_target_pairs={{0,2},{1,3},{2,0},{3,1},{4,6},{5,7},{6,4},{7,5},{8,10},{9,11},{10,... | collective-permute-start | bytes 946184 | tf_op jit(solution)/shard_map/ppermute | solution.py:891
  6.4 0.0 collective-permute-start.3
  6.4 1.5 %collective-permute-start = (f32[616,128]{1,0:T(8,128)S(1)}, f32[616,128]{1,0:T(8,128)S(1)}, u32[]{:S(2)}, u32[]{:S(2)}) collective-permute-start(f32[616,128]{1,0:T(8,128)S(1)} %get-tuple-element.59), channel_id=1, source_target_pairs={{0,8},{1,9},{2,10},{3,11},{4,12},{5,13},{6,14},{7,15},{8,0},{9,1},... | collective-permute-start | bytes 946184 | tf_op jit(solution)/shard_map/ppermute | solution.py:891
  7.9 0.2 collective-permute-start.1
  8.1 0.0 copy-done
  8.1 3.4 %early.1 = (f32[2,40,40,128]{3,2,1,0:T(8,128)S(1)}, f32[40,5,8,128]{3,2,1,0:T(8,128)S(1)}, f32[40,5,8,128]{3,2,1,0:T(8,128)S(1)}, f32[2,40,40,128]{3,2,1,0:T(8,1...) custom-call(f32[2]{0:T(128)S(1)} %copy-done, ...), custom_call_target="tpu_custom_call" | custom-call | tf_op jit(solution)/shard_map/early/pallas_call | solution.py:427
  11.5 2.3 %collective-permute-done.2.refs_0_ = f32[154,4,128]{2,1,0:T(4,128)S(1)} collective-permute-done((f32[154,4,128]{2,1,0:T(4,128)S(1)}, f32[154,4,128]{2,1,0:T(4,128)S(1)}, u32[]{:S(2)}, u32[]{:S(2)}) %collective-permute-start.2) | collective-permute-done | bytes 315424 | tf_op jit(solution)/shard_map/ppermute | solution.py:891
  13.8 0.0 collective-permute-done.3.refs_1_
  13.8 2.8 %inner_first.1 = (f32[2,40,40,128]{3,2,1,0:T(8,128)S(1)}, f32[2,40,40,128]{3,2,1,0:T(8,128)S(1)}, f32[32,40,128]{2,1,0:T(8,128)S(1)}, f32[5,40,128]{2,1,0:T(8,12...) custom-call(f32[2,8,128]{2,1,0:T(8,128)S(1)} %get-tuple-element.58.f, ...), custom_call_target="tpu_custom_call", output_to_operand_aliasing={{0}: (3, {}), {1}: (4, {}), {2}: (5, {}), {3}: (6, {}), {4}... | custom-call | tf_op jit(solution)/shard_map/inner_first/pallas_call | solution.py:612
  16.6 1.7 %collective-permute-start.4 = (f32[8,8,128]{2,1,0:T(8,128)S(1)}, f32[8,8,128]{2,1,0:T(8,128)S(1)}, u32[]{:S(2)}, u32[]{:S(2)}) collective-permute-start(f32[8,8,128]{2,1,0:T(8,128)S(1)} %get-tuple-element.70), channel_id=1, source_target_pairs={{0,8},{1,9},{2,10},{3,11},{4,12},{5,13},{6,14},{7,15},{8,0},{9,1},... | collective-permute-start | bytes 98312 | tf_op jit(solution)/shard_map/ppermute | solution.py:891
  18.4 0.0 collective-permute-start.5
  18.4 4.2 %inner_second.1 = (f32[2,40,40,128]{3,2,1,0:T(8,128)S(1)}, f32[2,40,40,128]{3,2,1,0:T(8,128)S(1)}, f32[2,40,40,128]{3,2,1,0:T(8,128)S(1)}, f32[2,40,40,128]{3,2,...) custom-call(f32[2,40,40,128]{3,2,1,0:T(8,128)S(1)} %get-tuple-elemen, ...), custom_call_target="tpu_custom_call", output_to_operand_aliasing={{0}: (9, {}), {1}: (10, {}), {2}: (11, {}), {3}: (12, {}), ... | custom-call | tf_op jit(solution)/shard_map/inner_second/pallas_call | solution.py:627
  22.5 0.0 collective-permute-done.xe
  22.5 0.0 collective-permute-done.1.xo
  22.6 1.5 %collective-permute-done.4.ce = f32[8,8,128]{2,1,0:T(8,128)S(1)} collective-permute-done((f32[8,8,128]{2,1,0:T(8,128)S(1)}, f32[8,8,128]{2,1,0:T(8,128)S(1)}, u32[]{:S(2)}, u32[]{:S(2)}) %collective-permute-start.4) | collective-permute-done | bytes 32800 | tf_op jit(solution)/shard_map/ppermute | solution.py:891
  24.0 0.0 collective-permute-done.5.co
  24.0 2.0 %edge_part.1 = (f32[2,40,40,128]{3,2,1,0:T(8,128)S(1)}, f32[2,40,40,128]{3,2,1,0:T(8,128)S(1)}, f32[2,40,40,128]{3,2,1,0:T(8,128)S(1)}, f32[2,40,40,128]{3,2,1,0...) custom-call(f32[2,8,128]{2,1,0:T(8,128)S(1)} %get-tuple-element.58.f, ...), custom_call_target="tpu_custom_call", output_to_operand_aliasing={{0}: (5, {}), {1}: (6, {}), {2}: (7, {}), {3}: (8, {}), {4}... | custom-call | tf_op jit(solution)/shard_map/edge_part/pallas_call | solution.py:734
  26.1 13.5 %all_to_all.5.sums = f32[16,8,128]{2,1,0:T(8,128)S(1)} all-to-all(f32[16,8,128]{2,1,0:T(8,128)S(1)} %get-tuple-element.95), channel_id=1, replica_groups=mesh['gx'=4,'gy'=4,'af'=2] {'gx','gy'}, dimensions={0} | all-to-all | bytes 131072 | tf_op jit(solution)/shard_map/all_to_all | solution.py:908
  39.5 1.1 %gradient_part.1.one = f32[32,32,128]{2,1,0:T(8,128)S(1)} custom-call(f32[2,8,128]{2,1,0:T(8,128)S(1)} %get-tuple-element.58.freq_sq, f32[16,8,128]{2,1,0:T(8,128)S(1)} %all_to_all.5.sums, f32[2,40,40,128]{3,2,1,0:T(8,128)S(1)} %get-tuple-element.100.refs_0_, f32[2,40,40,128]{3,2,1,0:T(8,128)S(1)} %get-tuple-element.96.refs_0_.refs_1_, ...), custom_call_target="tpu_custom_call" | custom-call | tf_op jit(solution)/shard_map/gradient_part/pallas_call | solution.py:822
  40.6 0.1 collective-permute-start.6
  40.7 1.5 %wavefield.1 = f32[2,2,32,32,128]{4,3,2,1,0:T(8,128)} custom-call(f32[16,8,128]{2,1,0:T(8,128)S(1)} %all_to_all.5.sums, f32[2,40,40,128]{3,2,1,0:T(8,128)S(1)} %get-tuple-element.96.refs_0_.refs_1_, f32[2,40,40,128]{3,2,1,0:T(8,128)S(1)} %get-tuple-element.97.refs_1_.refs_3_, f32[2,40,40,128]{3,2,1,0:T(8,128)S(1)} %get-tuple-element.98.refs_2_.refs_6_, ...), custom_call_target="tpu_custom_call" | custom-call | tf_op jit(solution)/shard_map/wavefield/pallas_call | solution.py:830
  42.2 0.4 collective-permute-done.6.two
  42.6 0.8 %add.1 = f32[32,32,128]{2,1,0:T(8,128)} custom-call(f32[32,32,128]{2,1,0:T(8,128)S(1)} %gradient_part.1.one, f32[32,32,128]{2,1,0:T(8,128)S(1)} %collective-permute-done.6.two), custom_call_target="tpu_custom_call" | custom-call | tf_op jit(solution)/shard_map/add/pallas_call | solution.py:865
Async XLA Ops:
  0.6 7.5 %copy-start = (f32[2]{0:T(128)S(1)}, f32[2]{0:T(128)}, u32[]{:S(2)}) copy-start(f32[2]{0:T(128)} %freq_sq.1) | copy-start | bytes 28
  3.3 10.5 %collective-permute-start.2 = (f32[154,4,128]{2,1,0:T(4,128)S(1)}, f32[154,4,128]{2,1,0:T(4,128)S(1)}, u32[]{:S(2)}, u32[]{:S(2)}) collective-permute-start(f32[154,4,128]{2,1,0:T(4,128)S(1)} %get-tuple-element.61), channel_id=1, source_target_pairs={{0,2},{1,3},{2,0},{3,1},{4,6},{5,7},{6,4},{7,5},{8,10},{9,11},{10,... | collective-permute-start | bytes 946184 | tf_op jit(solution)/shard_map/ppermute | solution.py:891
  6.4 7.4 %collective-permute-start.3 = (f32[154,4,128]{2,1,0:T(4,128)S(1)}, f32[154,4,128]{2,1,0:T(4,128)S(1)}, u32[]{:S(2)}, u32[]{:S(2)}) collective-permute-start(f32[154,4,128]{2,1,0:T(4,128)S(1)} %get-tuple-element.62), channel_id=1, source_target_pairs={{0,1},{1,0},{2,4},{3,5},{4,2},{5,3},{6,7},{7,6},{8,9},{9,8},{10,12... | collective-permute-start | bytes 946184 | tf_op jit(solution)/shard_map/ppermute | solution.py:891
  6.4 16.2 %collective-permute-start = (f32[616,128]{1,0:T(8,128)S(1)}, f32[616,128]{1,0:T(8,128)S(1)}, u32[]{:S(2)}, u32[]{:S(2)}) collective-permute-start(f32[616,128]{1,0:T(8,128)S(1)} %get-tuple-element.59), channel_id=1, source_target_pairs={{0,8},{1,9},{2,10},{3,11},{4,12},{5,13},{6,14},{7,15},{8,0},{9,1},... | collective-permute-start | bytes 946184 | tf_op jit(solution)/shard_map/ppermute | solution.py:891
  7.9 14.7 %collective-permute-start.1 = (f32[616,128]{1,0:T(8,128)S(1)}, f32[616,128]{1,0:T(8,128)S(1)}, u32[]{:S(2)}, u32[]{:S(2)}) collective-permute-start(f32[616,128]{1,0:T(8,128)S(1)} %get-tuple-element.60), channel_id=1, source_target_pairs={{0,1},{1,0},{2,3},{3,2},{4,5},{5,4},{6,7},{7,6},{8,16},{9,17},{10,... | collective-permute-start | bytes 946184 | tf_op jit(solution)/shard_map/ppermute | solution.py:891
  16.6 7.4 %collective-permute-start.4 = (f32[8,8,128]{2,1,0:T(8,128)S(1)}, f32[8,8,128]{2,1,0:T(8,128)S(1)}, u32[]{:S(2)}, u32[]{:S(2)}) collective-permute-start(f32[8,8,128]{2,1,0:T(8,128)S(1)} %get-tuple-element.70), channel_id=1, source_target_pairs={{0,8},{1,9},{2,10},{3,11},{4,12},{5,13},{6,14},{7,15},{8,0},{9,1},... | collective-permute-start | bytes 98312 | tf_op jit(solution)/shard_map/ppermute | solution.py:891
  18.4 5.7 %collective-permute-start.5 = (f32[8,8,128]{2,1,0:T(8,128)S(1)}, f32[8,8,128]{2,1,0:T(8,128)S(1)}, u32[]{:S(2)}, u32[]{:S(2)}) collective-permute-start(f32[8,8,128]{2,1,0:T(8,128)S(1)} %get-tuple-element.71), channel_id=1, source_target_pairs={{0,1},{1,0},{2,3},{3,2},{4,5},{5,4},{6,7},{7,6},{8,16},{9,17},{10,... | collective-permute-start | bytes 98312 | tf_op jit(solution)/shard_map/ppermute | solution.py:891
  40.6 2.0 %collective-permute-start.6 = (f32[32,32,128]{2,1,0:T(8,128)S(1)}, f32[32,32,128]{2,1,0:T(8,128)S(1)}, u32[]{:S(2)}, u32[]{:S(2)}) collective-permute-start(f32[32,32,128]{2,1,0:T(8,128)S(1)} %gradient_part.1.one), channel_id=1, source_target_pairs={{0,1},{1,0},{2,3},{3,2},{4,5},{5,4},{6,7},{7,6},{8,9},{9,8},{10,11... | collective-permute-start | bytes 1572872 | tf_op jit(solution)/shard_map/ppermute | solution.py:911

commit v9 on v8

--- a/solution.py
+++ b/solution.py
@@ -301,9 +301,9 @@
             )
         return out
 
-    def pick(self, ref, lead, t, lane):
+    def pick(self, ref, t, lane):
         at = jnp.full((8, self.nz), lane, jnp.int32)
-        return jnp.take_along_axis(ref[lead, self.tile(t), :], at, axis=1)
+        return jnp.take_along_axis(ref[self.tile(t), :], at, axis=1)
 
 
 class Field:
@@ -391,7 +391,7 @@
             w,
             many,
             lambda t: cells[i, grid.tile(t), :],
-            lambda k, t: grid.pick(aux, k, t, i),
+            lambda k, t: grid.pick(aux.at[k], t, i),
         )
 
     for i in (0, nx - 1):
@@ -554,7 +554,7 @@
             w,
             many,
             lambda t: cells[i, grid.tile(t), :],
-            lambda k, t: grid.pick(aux, k, t, i),
+            lambda k, t: grid.pick(aux.at[k], t, i),
         )
 
     if half == 0:
@@ -594,7 +594,13 @@
             continue
         active = [k for k, (a, b) in enumerate(spans) if k and a <= lo and hi <= b]
         if active:
-            acc = lax.fori_loop(lo, hi, functools.partial(step, active=active), acc)
+            acc = lax.fori_loop(
+                lo,
+                hi,
+                functools.partial(step, active=active),
+                acc,
+                unroll=3 if hi - lo > 4 else hi - lo,
+            )
     for f in range(freqs):
         for m in range(4):
             value = acc[f][m]
@@ -641,82 +647,81 @@
     return ce, co, rest
 
 
-def edge_kernel(peers, freqs, nx, ny, freq_sq, xe, xo, ce, co, *refs):
+def edge_kernel(side, peers, freqs, nx, ny, freq_sq, xb, cb, *refs):
     count = 7 * freqs + 1
     moments, refs = refs[count], refs[count + 1 :]
-    state, (part, cells, aux) = refs[:count], refs[count:]
+    state, (out, cells, aux) = refs[:count], refs[count:]
     fields = 2 * freqs
     nz = state[0].shape[3]
     w = state[-1]
-    even_x = parity("gx")
+    above = parity("gx") if side == 0 else jnp.logical_not(parity("gx"))
     group = nz // 8
-    for side, (xb, cb) in enumerate(((xe, ce), (xo, co))):
-        above = even_x if side == 0 else jnp.logical_not(even_x)
-        slot = jnp.where(above, nx, nx + HALO)
-        half = jnp.where(above, 0, 1)
-        for layer in range(HALO):
-            for k in range(fields):
-                block = state[7 * (k // 2)]
-                for y in range(0, ny, 8):
-                    row = (k * HALO + layer) * ny + y
-                    block[k % 2, slot + layer, y : y + 8, :] = xb[row : row + 8, :]
-            if layer < INNER:
-                for y in range(0, ny, 8):
-                    row = (fields * HALO + layer) * ny + y
-                    cells[half, layer, y : y + 8, :] = xb[row : row + 8, :]
-        at = (fields * HALO + INNER) * ny
-        folded = xb[at : at + ny // 8, :]
-        for g in range(8):
-            rows = pl.ds(g * (ny // 8), ny // 8)
-            aux[half, rows, :] = pltpu.roll(folded, (nz - g * group) % nz, axis=1)
-        place_corners(
-            freqs, nx, ny, cb, state[: 7 * freqs : 7], cells.at[half], aux.at[half], above
+    wrap = nx + 2 * HALO
+
+    def row_at(distance):
+        return jnp.where(above, (nx - 1 + distance) % wrap, -distance % wrap)
+
+    slot = jnp.where(above, nx, nx + HALO)
+    for layer in range(HALO):
+        for k in range(fields):
+            block = state[7 * (k // 2)]
+            for y in range(0, ny, 8):
+                row = (k * HALO + layer) * ny + y
+                block[k % 2, slot + layer, y : y + 8, :] = xb[row : row + 8, :]
+        if layer < INNER:
+            for y in range(0, ny, 8):
+                row = (fields * HALO + layer) * ny + y
+                cells[layer, y : y + 8, :] = xb[row : row + 8, :]
+    at = (fields * HALO + INNER) * ny
+    folded = xb[at : at + ny // 8, :]
+    for g in range(8):
+        rows = pl.ds(g * (ny // 8), ny // 8)
+        aux[rows, :] = pltpu.roll(folded, (nz - g * group) % nz, axis=1)
+    place_corners(freqs, nx, ny, cb, state[: 7 * freqs : 7], cells, aux, above)
+    for k in range(fields):
+        state[7 * (k // 2)][k % 2, row_at(HALO), ny:, :] = jnp.zeros(
+            (2 * HALO, nz), F32
         )
-    for k in range(fields):
-        for i in (nx + HALO - 1, nx + HALO):
-            state[7 * (k // 2)][k % 2, i, ny:, :] = jnp.zeros((2 * HALO, nz), F32)
     grid = Grid(nx, ny, nz)
     many = [Field(grid, state[7 * f : 7 * f + 7], w) for f in range(freqs)]
-    for half in range(2):
-        for layer in range(INNER):
-            i = nx + layer if half == 0 else nx + HALO + 1 + layer
-            terms = grid.prepare(
-                i,
-                grid.both,
-                freq_sq,
-                w,
-                many,
-                lambda t: cells[half, layer, grid.tile(t), :],
-                lambda k, t: grid.pick(aux, half, t, INNER * k + layer),
-            )
-            for f in range(freqs):
-                for p in range(2):
-                    grid.put(many[f].v0, p, i, terms[f][p], grid.both)
-
-    left = jnp.where(lax.axis_index("gx") > 0, 1.0, 0.0)
-    right = jnp.where(lax.axis_index("gx") < lax.axis_size("gx") - 1, 1.0, 0.0)
-    wrap = grid.xe
+    for layer in range(INNER):
+        i = jnp.where(above, nx + layer, nx + HALO + 1 + layer)
+        terms = grid.prepare(
+            i,
+            grid.both,
+            freq_sq,
+            w,
+            many,
+            lambda t: cells[layer, grid.tile(t), :],
+            lambda k, t: grid.pick(aux, t, INNER * k + layer),
+        )
+        for f in range(freqs):
+            for p in range(2):
+                grid.put(many[f].v0, p, i, terms[f][p], grid.both)
+
+    place = lax.axis_index("gx")
+    more = jnp.where(above, place < lax.axis_size("gx") - 1, place > 0)
+    cut = (-1, jnp.where(more, 1.0, 0.0))
     acc = [tuple(grid.zero() for _ in range(4)) for _ in range(freqs)]
     for stage in range(4):
         for k in range(HALO):
-            for x in (k - INNER + stage, nx - 1 - stage + k):
-                i, lo, hi = x % wrap, (x - 1) % wrap, (x + 1) % wrap
-                own = 0 <= x < nx
-                cut = None
-                if x == 0:
-                    cut = (-1, left)
-                if x == nx - 1:
-                    cut = (1, right)
-                for f in range(freqs):
-                    if stage == 0:
-                        many[f].finish(i, grid.both, True, lo, hi, cut)
-                        continue
-                    got = many[f].step(
-                        stage, i, lo, hi, cut, acc[f] if own else None
-                    )
-                    if own:
-                        acc[f] = got
-
+            distance = INNER - stage - k
+            i, lo, hi = (row_at(distance + d) for d in (0, 1, -1))
+            own = distance <= 0
+            ends = cut if distance == 0 else None
+            for f in range(freqs):
+                if stage == 0:
+                    many[f].finish(i, grid.both, True, lo, hi, ends)
+                    continue
+                got = many[f].step(stage, i, lo, hi, ends, acc[f] if own else None)
+                if own:
+                    acc[f] = got
+
+    if side == 0:
+        for f in range(freqs):
+            for m in range(4):
+                out[f, m] = acc[f][m] + moments[f, m]
+        return
     rows = []
     for f in range(freqs):
         for m in range(4):
@@ -725,24 +730,29 @@
     sums = jnp.sum(jnp.concatenate(rows, axis=0), axis=1, keepdims=True)
     sums = jnp.broadcast_to(sums, (4 * freqs, nz))
     for peer in range(peers):
-        part[peer] = sums
-
-
-def edge_part(peers, freqs, nx, ny, freq_sq, xe, xo, ce, co, state, moments):
+        out[peer] = sums
+
+
+def edge_part(side, peers, freqs, nx, ny, freq_sq, xb, cb, state, moments):
     nz = state[0].shape[3]
     outs = tuple(pltpu.VMEM(k.shape, F32) for k in state)
-    return pl.pallas_call(
-        functools.partial(edge_kernel, peers, freqs, nx, ny),
-        out_shape=outs + (jax.ShapeDtypeStruct((peers, 4 * freqs, nz), F32),),
-        in_specs=[VMEM] * (6 + len(state)),
-        input_output_aliases={5 + k: k for k in range(len(state))},
+    if side == 0:
+        last = pltpu.VMEM(moments.shape, F32)
+    else:
+        last = jax.ShapeDtypeStruct((peers, 4 * freqs, nz), F32)
+    *state, out = pl.pallas_call(
+        functools.partial(edge_kernel, side, peers, freqs, nx, ny),
+        out_shape=outs + (last,),
+        in_specs=[VMEM] * (4 + len(state)),
+        input_output_aliases={3 + k: k for k in range(len(state))},
         scratch_shapes=[
-            pltpu.VMEM((2, INNER, ny + 2 * HALO, nz), F32),
-            pltpu.VMEM((2, ny + 2 * HALO, nz), F32),
+            pltpu.VMEM((INNER, ny + 2 * HALO, nz), F32),
+            pltpu.VMEM((ny + 2 * HALO, nz), F32),
         ],
         compiler_params=params(8),
-        name="edge_part",
-    )(freq_sq, xe, xo, ce, co, *state, moments)
+        name="edge_odd" if side else "edge_even",
+    )(freq_sq, xb, cb, *state, moments)
+    return state, out
 
 
 def steps(sums, freqs):
@@ -902,9 +912,10 @@
     ce, co = swap(ce, "gx", 0), swap(co, "gx", 1)
     state, moments = rest()
     peers = lax.axis_size("gx") * lax.axis_size("gy")
-    *state, part = edge_part(
-        peers, freqs, nx, ny, splat, xe, xo, ce, co, state, moments
+    state, moments = edge_part(
+        0, peers, freqs, nx, ny, splat, xe, ce, state, moments
     )
+    state, part = edge_part(1, peers, freqs, nx, ny, splat, xo, co, state, moments)
     sums = lax.all_to_all(part, ("gx", "gy"), 0, 0)
     gradient, wave = results(freqs, nx, ny, splat, sums, state)
     if lax.axis_size("af") == 2:

time: 43.6 us -> 43.5 us (level)
  waiting for transfers between devices: 4.21 us -> 5.31 us
  Pallas kernels: 18.5 us -> 17.7 us
  blocking collectives: 13.5 us -> 13 us
    ppermute x6, waiting for transfers between devices: 3.79 us -> 4.89 us  [swap(): return lax.ppermute(cells, names, pairs)]
    pallas_call x1, Pallas kernels: 4.16 us -> 3.46 us  [rest(): pl.pallas_call(functools.partial(inner_kernel, freqs, nx, ny, 1, None), o...]
    all_to_all x1, blocking collectives: 13.5 us -> 13 us  [on_device(): sums = lax.all_to_all(part, ('gx', 'gy'), 0, 0)]
    pallas_call x1 -> x2, Pallas kernels: 2 us -> 2.32 us  [edge_part(): pl.pallas_call(functools.partial(edge_kernel, side, peers, freqs, nx, ny)...]
where the time goes in v9:
time: 43.5 us; the launch traced here: 43.3 us
  Pallas kernels  17.7 us (41%)
  blocking collectives  13 us (30%)
  starting transfers between devices  6.6 us (15%)
  waiting for transfers between devices  5.31 us (12%)
  between operations  0.72 us (2%)
    all_to_all x1, blocking collectives, on_device(): sums = lax.all_to_all(part, ('gx', 'gy'), 0, 0)  13 us
    ppermute x6, starting transfers between devices, swap(): return lax.ppermute(cells, names, pairs)  6.53 us
    ppermute x6, waiting for transfers between devices, swap(): return lax.ppermute(cells, names, pairs)  4.89 us
    pallas_call x1, Pallas kernels, rest(): pl.pallas_call(functools.partial(inner_kernel, freqs, nx, ny, 1, None), o...  3.46 us
    pallas_call x1, Pallas kernels, early(): pl.pallas_call(functools.partial(early_kernel, freqs, nx, ny), out_shape=...  3.43 us
    pallas_call x1, Pallas kernels, load(): pl.pallas_call(load_kernel, out_shape=(pltpu.VMEM((2, nx + 2 * HALO, ny +...  2.63 us
    pallas_call x1, Pallas kernels, inner_part(): pl.pallas_call(functools.partial(inner_kernel, freqs, nx, ny, 0), out_sha...  2.42 us
    pallas_call x2, Pallas kernels, edge_part(): pl.pallas_call(functools.partial(edge_kernel, side, peers, freqs, nx, ny)...  2.32 us
  transfers between devices with their start and end apart: 7, of which 3 were waited for; matrix products, arithmetic and copies ran while one was open for 0% of the time, Pallas kernels for 27%

profile of v9, /device:TPU:0, one launch (start us, length us, event | category | flops | bytes accessed | tf_op | source)
XLA Modules:
  0.0 43.3 jit_solution(3387633243578063537)
XLA Ops:
  0.6 0.0 copy-start
  0.6 2.6 %load.1 = (f32[2,40,40,128]{3,2,1,0:T(8,128)S(1)}, f32[2,40,40,128]{3,2,1,0:T(8,128)S(1)}, f32[32,40,128]{2,1,0:T(8,128)S(1)}, f32[5,40,128]{2,1,0:T(8,128)S(1)}...) custom-call(f32[2,2,32,32,128]{4,3,2,1,0:T(8,128)} %source.1, ...), custom_call_target="tpu_custom_call" | custom-call | tf_op jit(solution)/shard_map/load/pallas_call | solution.py:165
  3.3 3.1 %collective-permute-start.1 = (f32[154,4,128]{2,1,0:T(4,128)S(1)}, f32[154,4,128]{2,1,0:T(4,128)S(1)}, u32[]{:S(2)}, u32[]{:S(2)}) collective-permute-start(f32[154,4,128]{2,1,0:T(4,128)S(1)} %get-tuple-element.76), channel_id=1, source_target_pairs={{0,2},{1,3},{2,0},{3,1},{4,6},{5,7},{6,4},{7,5},{8,10},{9,11},{10,... | collective-permute-start | bytes 946184 | tf_op jit(solution)/shard_map/ppermute | solution.py:901
  6.4 0.0 collective-permute-start.2
  6.4 1.5 %collective-permute-start.4 = (f32[616,128]{1,0:T(8,128)S(1)}, f32[616,128]{1,0:T(8,128)S(1)}, u32[]{:S(2)}, u32[]{:S(2)}) collective-permute-start(f32[616,128]{1,0:T(8,128)S(1)} %get-tuple-element.86), channel_id=1, source_target_pairs={{0,8},{1,9},{2,10},{3,11},{4,12},{5,13},{6,14},{7,15},{8,0},{9,1},... | collective-permute-start | bytes 946184 | tf_op jit(solution)/shard_map/ppermute | solution.py:901
  7.9 0.2 collective-permute-start
  8.1 0.0 copy-done
  8.1 3.4 %early.1 = (f32[2,40,40,128]{3,2,1,0:T(8,128)S(1)}, f32[40,5,8,128]{3,2,1,0:T(8,128)S(1)}, f32[40,5,8,128]{3,2,1,0:T(8,128)S(1)}, f32[2,40,40,128]{3,2,1,0:T(8,1...) custom-call(f32[2]{0:T(128)S(1)} %copy-done, ...), custom_call_target="tpu_custom_call" | custom-call | tf_op jit(solution)/shard_map/early/pallas_call | solution.py:427
  11.5 2.3 %collective-permute-done.1.refs_0_ = f32[154,4,128]{2,1,0:T(4,128)S(1)} collective-permute-done((f32[154,4,128]{2,1,0:T(4,128)S(1)}, f32[154,4,128]{2,1,0:T(4,128)S(1)}, u32[]{:S(2)}, u32[]{:S(2)}) %collective-permute-start.1) | collective-permute-done | bytes 315424 | tf_op jit(solution)/shard_map/ppermute | solution.py:901
  13.8 0.0 collective-permute-done.2.refs_1_
  13.8 2.4 %inner_first.1 = (f32[2,40,40,128]{3,2,1,0:T(8,128)S(1)}, f32[2,40,40,128]{3,2,1,0:T(8,128)S(1)}, f32[32,40,128]{2,1,0:T(8,128)S(1)}, f32[5,40,128]{2,1,0:T(8,12...) custom-call(f32[2,8,128]{2,1,0:T(8,128)S(1)} %get-tuple-element.74.f, ...), custom_call_target="tpu_custom_call", output_to_operand_aliasing={{0}: (3, {}), {1}: (4, {}), {2}: (5, {}), {3}: (6, {}), {4}... | custom-call | tf_op jit(solution)/shard_map/inner_first/pallas_call | solution.py:618
  16.3 1.7 %collective-permute-start.5 = (f32[8,8,128]{2,1,0:T(8,128)S(1)}, f32[8,8,128]{2,1,0:T(8,128)S(1)}, u32[]{:S(2)}, u32[]{:S(2)}) collective-permute-start(f32[8,8,128]{2,1,0:T(8,128)S(1)} %get-tuple-element.87), channel_id=1, source_target_pairs={{0,8},{1,9},{2,10},{3,11},{4,12},{5,13},{6,14},{7,15},{8,0},{9,1},... | collective-permute-start | bytes 98312 | tf_op jit(solution)/shard_map/ppermute | solution.py:901
  18.0 0.0 collective-permute-start.3
  18.0 3.5 %inner_second.1 = (f32[2,40,40,128]{3,2,1,0:T(8,128)S(1)}, f32[2,40,40,128]{3,2,1,0:T(8,128)S(1)}, f32[2,40,40,128]{3,2,1,0:T(8,128)S(1)}, f32[2,40,40,128]{3,2,...) custom-call(f32[2,40,40,128]{3,2,1,0:T(8,128)S(1)} %get-tuple-elemen, ...), custom_call_target="tpu_custom_call", output_to_operand_aliasing={{0}: (9, {}), {1}: (10, {}), {2}: (11, {}), {3}: (12, {}), ... | custom-call | tf_op jit(solution)/shard_map/inner_second/pallas_call | solution.py:633
  21.4 0.0 collective-permute-done.4.xb
  21.4 2.6 %collective-permute-done.5.cb = f32[8,8,128]{2,1,0:T(8,128)S(1)} collective-permute-done((f32[8,8,128]{2,1,0:T(8,128)S(1)}, f32[8,8,128]{2,1,0:T(8,128)S(1)}, u32[]{:S(2)}, u32[]{:S(2)}) %collective-permute-start.5) | collective-permute-done | bytes 32800 | tf_op jit(solution)/shard_map/ppermute | solution.py:901
  24.0 1.1 %edge_even.1 = (f32[2,40,40,128]{3,2,1,0:T(8,128)S(1)}, f32[2,40,40,128]{3,2,1,0:T(8,128)S(1)}, f32[2,40,40,128]{3,2,1,0:T(8,128)S(1)}, f32[2,40,40,128]{3,2,1,0...) custom-call(f32[2,8,128]{2,1,0:T(8,128)S(1)} %get-tuple-element.74.f, ...), custom_call_target="tpu_custom_call", output_to_operand_aliasing={{0}: (3, {}), {1}: (4, {}), {2}: (5, {}), {3}: (6, {}), {4}... | custom-call | tf_op jit(solution)/shard_map/edge_even/pallas_call | solution.py:743
  25.2 0.0 collective-permute-done.xb
  25.2 0.0 collective-permute-done.3.cb
  25.2 1.2 %edge_odd.1 = (f32[2,40,40,128]{3,2,1,0:T(8,128)S(1)}, f32[2,40,40,128]{3,2,1,0:T(8,128)S(1)}, f32[2,40,40,128]{3,2,1,0:T(8,128)S(1)}, f32[2,40,40,128]{3,2,1,0:...) custom-call(f32[2,8,128]{2,1,0:T(8,128)S(1)} %get-tuple-element.74.f, ...), custom_call_target="tpu_custom_call", output_to_operand_aliasing={{0}: (3, {}), {1}: (4, {}), {2}: (5, {}), {3}: (6, {}), {4}... | custom-call | tf_op jit(solution)/shard_map/edge_odd/pallas_call | solution.py:743
  26.4 13.0 %all_to_all.5.sums = f32[16,8,128]{2,1,0:T(8,128)S(1)} all-to-all(f32[16,8,128]{2,1,0:T(8,128)S(1)} %get-tuple-element.127), channel_id=1, replica_groups=mesh['gx'=4,'gy'=4,'af'=2] {'gx','gy'}, dimensions={0} | all-to-all | bytes 131072 | tf_op jit(solution)/shard_map/all_to_all | solution.py:919
  39.4 1.1 %gradient_part.1.one = f32[32,32,128]{2,1,0:T(8,128)S(1)} custom-call(f32[2,8,128]{2,1,0:T(8,128)S(1)} %get-tuple-element.74.freq_sq, f32[16,8,128]{2,1,0:T(8,128)S(1)} %all_to_all.5.sums, f32[2,40,40,128]{3,2,1,0:T(8,128)S(1)} %get-tuple-element.132.refs_0_, f32[2,40,40,128]{3,2,1,0:T(8,128)S(1)} %get-tuple-element.128.refs_0_.refs_1_, ...), custom_call_target="tpu_custom_call" | custom-call | tf_op jit(solution)/shard_map/gradient_part/pallas_call | solution.py:832
  40.5 0.1 collective-permute-start.6
  40.6 1.5 %wavefield.1 = f32[2,2,32,32,128]{4,3,2,1,0:T(8,128)} custom-call(f32[16,8,128]{2,1,0:T(8,128)S(1)} %all_to_all.5.sums, f32[2,40,40,128]{3,2,1,0:T(8,128)S(1)} %get-tuple-element.128.refs_0_.refs_1_, f32[2,40,40,128]{3,2,1,0:T(8,128)S(1)} %get-tuple-element.129.refs_1_.refs_3_, f32[2,40,40,128]{3,2,1,0:T(8,128)S(1)} %get-tuple-element.130.refs_2_.refs_6_, ...), custom_call_target="tpu_custom_call" | custom-call | tf_op jit(solution)/shard_map/wavefield/pallas_call | solution.py:840
  42.0 0.4 collective-permute-done.6.two
  42.5 0.8 %add.1 = f32[32,32,128]{2,1,0:T(8,128)} custom-call(f32[32,32,128]{2,1,0:T(8,128)S(1)} %gradient_part.1.one, f32[32,32,128]{2,1,0:T(8,128)S(1)} %collective-permute-done.6.two), custom_call_target="tpu_custom_call" | custom-call | tf_op jit(solution)/shard_map/add/pallas_call | solution.py:875
Async XLA Ops:
  0.6 7.5 %copy-start = (f32[2]{0:T(128)S(1)}, f32[2]{0:T(128)}, u32[]{:S(2)}) copy-start(f32[2]{0:T(128)} %freq_sq.1) | copy-start | bytes 28
  3.3 10.5 %collective-permute-start.1 = (f32[154,4,128]{2,1,0:T(4,128)S(1)}, f32[154,4,128]{2,1,0:T(4,128)S(1)}, u32[]{:S(2)}, u32[]{:S(2)}) collective-permute-start(f32[154,4,128]{2,1,0:T(4,128)S(1)} %get-tuple-element.76), channel_id=1, source_target_pairs={{0,2},{1,3},{2,0},{3,1},{4,6},{5,7},{6,4},{7,5},{8,10},{9,11},{10,... | collective-permute-start | bytes 946184 | tf_op jit(solution)/shard_map/ppermute | solution.py:901
  6.4 7.4 %collective-permute-start.2 = (f32[154,4,128]{2,1,0:T(4,128)S(1)}, f32[154,4,128]{2,1,0:T(4,128)S(1)}, u32[]{:S(2)}, u32[]{:S(2)}) collective-permute-start(f32[154,4,128]{2,1,0:T(4,128)S(1)} %get-tuple-element.77), channel_id=1, source_target_pairs={{0,1},{1,0},{2,4},{3,5},{4,2},{5,3},{6,7},{7,6},{8,9},{9,8},{10,12... | collective-permute-start | bytes 946184 | tf_op jit(solution)/shard_map/ppermute | solution.py:901
  6.4 15.1 %collective-permute-start.4 = (f32[616,128]{1,0:T(8,128)S(1)}, f32[616,128]{1,0:T(8,128)S(1)}, u32[]{:S(2)}, u32[]{:S(2)}) collective-permute-start(f32[616,128]{1,0:T(8,128)S(1)} %get-tuple-element.86), channel_id=1, source_target_pairs={{0,8},{1,9},{2,10},{3,11},{4,12},{5,13},{6,14},{7,15},{8,0},{9,1},... | collective-permute-start | bytes 946184 | tf_op jit(solution)/shard_map/ppermute | solution.py:901
  7.9 17.3 %collective-permute-start = (f32[616,128]{1,0:T(8,128)S(1)}, f32[616,128]{1,0:T(8,128)S(1)}, u32[]{:S(2)}, u32[]{:S(2)}) collective-permute-start(f32[616,128]{1,0:T(8,128)S(1)} %get-tuple-element.75), channel_id=1, source_target_pairs={{0,1},{1,0},{2,3},{3,2},{4,5},{5,4},{6,7},{7,6},{8,16},{9,17},{10,... | collective-permute-start | bytes 946184 | tf_op jit(solution)/shard_map/ppermute | solution.py:901
  16.3 7.8 %collective-permute-start.5 = (f32[8,8,128]{2,1,0:T(8,128)S(1)}, f32[8,8,128]{2,1,0:T(8,128)S(1)}, u32[]{:S(2)}, u32[]{:S(2)}) collective-permute-start(f32[8,8,128]{2,1,0:T(8,128)S(1)} %get-tuple-element.87), channel_id=1, source_target_pairs={{0,8},{1,9},{2,10},{3,11},{4,12},{5,13},{6,14},{7,15},{8,0},{9,1},... | collective-permute-start | bytes 98312 | tf_op jit(solution)/shard_map/ppermute | solution.py:901
  18.0 7.2 %collective-permute-start.3 = (f32[8,8,128]{2,1,0:T(8,128)S(1)}, f32[8,8,128]{2,1,0:T(8,128)S(1)}, u32[]{:S(2)}, u32[]{:S(2)}) collective-permute-start(f32[8,8,128]{2,1,0:T(8,128)S(1)} %get-tuple-element.85), channel_id=1, source_target_pairs={{0,1},{1,0},{2,3},{3,2},{4,5},{5,4},{6,7},{7,6},{8,16},{9,17},{10,... | collective-permute-start | bytes 98312 | tf_op jit(solution)/shard_map/ppermute | solution.py:901
  40.5 2.0 %collective-permute-start.6 = (f32[32,32,128]{2,1,0:T(8,128)S(1)}, f32[32,32,128]{2,1,0:T(8,128)S(1)}, u32[]{:S(2)}, u32[]{:S(2)}) collective-permute-start(f32[32,32,128]{2,1,0:T(8,128)S(1)} %gradient_part.1.one), channel_id=1, source_target_pairs={{0,1},{1,0},{2,3},{3,2},{4,5},{5,4},{6,7},{7,6},{8,9},{9,8},{10,11... | collective-permute-start | bytes 1572872 | tf_op jit(solution)/shard_map/ppermute | solution.py:922

commit v10 on v9

--- a/solution.py
+++ b/solution.py
@@ -728,9 +728,10 @@
             both = acc[f][m] + moments[f, m]
             rows.append(jnp.sum(both, axis=0, keepdims=True))
     sums = jnp.sum(jnp.concatenate(rows, axis=0), axis=1, keepdims=True)
-    sums = jnp.broadcast_to(sums, (4 * freqs, nz))
-    for peer in range(peers):
-        out[peer] = sums
+    lane = lax.broadcasted_iota(jnp.int32, (4 * freqs, nz), 1)
+    sub = lax.broadcasted_iota(jnp.int32, (4 * freqs, nz), 0)
+    sums = jnp.where(lane == sub, jnp.broadcast_to(sums, (4 * freqs, nz)), 0.0)
+    out[...] = jnp.broadcast_to(jnp.sum(sums, axis=0, keepdims=True), out.shape)
 
 
 def edge_part(side, peers, freqs, nx, ny, freq_sq, xb, cb, state, moments):
@@ -739,7 +740,7 @@
     if side == 0:
         last = pltpu.VMEM(moments.shape, F32)
     else:
-        last = jax.ShapeDtypeStruct((peers, 4 * freqs, nz), F32)
+        last = jax.ShapeDtypeStruct((peers, nz), F32)
     *state, out = pl.pallas_call(
         functools.partial(edge_kernel, side, peers, freqs, nx, ny),
         out_shape=outs + (last,),
@@ -756,12 +757,12 @@
 
 
 def steps(sums, freqs):
-    total = jnp.sum(sums[...], axis=0)
+    total = jnp.sum(sums[...], axis=0, keepdims=True)
     shape = (8, total.shape[1])
     out = []
     for f in range(freqs):
         m0, m1, m2, m3 = (
-            jnp.broadcast_to(total[4 * f + k : 4 * f + k + 1, :], shape)
+            jnp.broadcast_to(total[:, 4 * f + k : 4 * f + k + 1], shape)
             for k in range(4)
         )
         first = m0 / m1

time: 43.5 us -> 43.3 us (level)
  transfers between devices with their start and end apart: 7 -> 7, of which waited for: 3 -> 3; matrix products, arithmetic and copies ran while one was open for 0% -> 0% of each run, Pallas kernels for 27% -> 28%
where the time goes in v10:
time: 43.3 us; the launch traced here: 43.1 us
  Pallas kernels  17.7 us (41%)
  blocking collectives  12.8 us (30%)
  starting transfers between devices  6.6 us (15%)
  waiting for transfers between devices  5.28 us (12%)
  between operations  0.72 us (2%)
    all_to_all x1, blocking collectives, on_device(): sums = lax.all_to_all(part, ('gx', 'gy'), 0, 0)  12.8 us
    ppermute x6, starting transfers between devices, swap(): return lax.ppermute(cells, names, pairs)  6.53 us
    ppermute x6, waiting for transfers between devices, swap(): return lax.ppermute(cells, names, pairs)  4.91 us
    pallas_call x1, Pallas kernels, rest(): pl.pallas_call(functools.partial(inner_kernel, freqs, nx, ny, 1, None), o...  3.45 us
    pallas_call x1, Pallas kernels, early(): pl.pallas_call(functools.partial(early_kernel, freqs, nx, ny), out_shape=...  3.43 us
    pallas_call x1, Pallas kernels, load(): pl.pallas_call(load_kernel, out_shape=(pltpu.VMEM((2, nx + 2 * HALO, ny +...  2.63 us
    pallas_call x1, Pallas kernels, inner_part(): pl.pallas_call(functools.partial(inner_kernel, freqs, nx, ny, 0), out_sha...  2.41 us
    pallas_call x2, Pallas kernels, edge_part(): pl.pallas_call(functools.partial(edge_kernel, side, peers, freqs, nx, ny)...  2.33 us
  transfers between devices with their start and end apart: 7, of which 3 were waited for; matrix products, arithmetic and copies ran while one was open for 0% of the time, Pallas kernels for 28%

profile of v10, /device:TPU:0, one launch (start us, length us, event | category | flops | bytes accessed | tf_op | source)
XLA Modules:
  0.0 43.1 jit_solution(17889078246720349832)
XLA Ops:
  0.6 0.0 copy-start
  0.6 2.6 %load.1 = (f32[2,40,40,128]{3,2,1,0:T(8,128)S(1)}, f32[2,40,40,128]{3,2,1,0:T(8,128)S(1)}, f32[32,40,128]{2,1,0:T(8,128)S(1)}, f32[5,40,128]{2,1,0:T(8,128)S(1)}...) custom-call(f32[2,2,32,32,128]{4,3,2,1,0:T(8,128)} %source.1, ...), custom_call_target="tpu_custom_call" | custom-call | tf_op jit(solution)/shard_map/load/pallas_call | solution.py:165
  3.3 3.1 %collective-permute-start.1 = (f32[154,4,128]{2,1,0:T(4,128)S(1)}, f32[154,4,128]{2,1,0:T(4,128)S(1)}, u32[]{:S(2)}, u32[]{:S(2)}) collective-permute-start(f32[154,4,128]{2,1,0:T(4,128)S(1)} %get-tuple-element.76), channel_id=1, source_target_pairs={{0,2},{1,3},{2,0},{3,1},{4,6},{5,7},{6,4},{7,5},{8,10},{9,11},{10,... | collective-permute-start | bytes 946184 | tf_op jit(solution)/shard_map/ppermute | solution.py:902
  6.4 0.0 collective-permute-start.2
  6.4 1.5 %collective-permute-start.4 = (f32[616,128]{1,0:T(8,128)S(1)}, f32[616,128]{1,0:T(8,128)S(1)}, u32[]{:S(2)}, u32[]{:S(2)}) collective-permute-start(f32[616,128]{1,0:T(8,128)S(1)} %get-tuple-element.86), channel_id=1, source_target_pairs={{0,8},{1,9},{2,10},{3,11},{4,12},{5,13},{6,14},{7,15},{8,0},{9,1},... | collective-permute-start | bytes 946184 | tf_op jit(solution)/shard_map/ppermute | solution.py:902
  7.9 0.2 collective-permute-start
  8.1 0.0 copy-done
  8.1 3.4 %early.1 = (f32[2,40,40,128]{3,2,1,0:T(8,128)S(1)}, f32[40,5,8,128]{3,2,1,0:T(8,128)S(1)}, f32[40,5,8,128]{3,2,1,0:T(8,128)S(1)}, f32[2,40,40,128]{3,2,1,0:T(8,1...) custom-call(f32[2]{0:T(128)S(1)} %copy-done, ...), custom_call_target="tpu_custom_call" | custom-call | tf_op jit(solution)/shard_map/early/pallas_call | solution.py:427
  11.5 2.3 %collective-permute-done.1.refs_0_ = f32[154,4,128]{2,1,0:T(4,128)S(1)} collective-permute-done((f32[154,4,128]{2,1,0:T(4,128)S(1)}, f32[154,4,128]{2,1,0:T(4,128)S(1)}, u32[]{:S(2)}, u32[]{:S(2)}) %collective-permute-start.1) | collective-permute-done | bytes 315424 | tf_op jit(solution)/shard_map/ppermute | solution.py:902
  13.8 0.0 collective-permute-done.2.refs_1_
  13.8 2.4 %inner_first.1 = (f32[2,40,40,128]{3,2,1,0:T(8,128)S(1)}, f32[2,40,40,128]{3,2,1,0:T(8,128)S(1)}, f32[32,40,128]{2,1,0:T(8,128)S(1)}, f32[5,40,128]{2,1,0:T(8,12...) custom-call(f32[2,8,128]{2,1,0:T(8,128)S(1)} %get-tuple-element.74.f, ...), custom_call_target="tpu_custom_call", output_to_operand_aliasing={{0}: (3, {}), {1}: (4, {}), {2}: (5, {}), {3}: (6, {}), {4}... | custom-call | tf_op jit(solution)/shard_map/inner_first/pallas_call | solution.py:618
  16.2 1.7 %collective-permute-start.5 = (f32[8,8,128]{2,1,0:T(8,128)S(1)}, f32[8,8,128]{2,1,0:T(8,128)S(1)}, u32[]{:S(2)}, u32[]{:S(2)}) collective-permute-start(f32[8,8,128]{2,1,0:T(8,128)S(1)} %get-tuple-element.87), channel_id=1, source_target_pairs={{0,8},{1,9},{2,10},{3,11},{4,12},{5,13},{6,14},{7,15},{8,0},{9,1},... | collective-permute-start | bytes 98312 | tf_op jit(solution)/shard_map/ppermute | solution.py:902
  18.0 0.0 collective-permute-start.3
  18.0 3.4 %inner_second.1 = (f32[2,40,40,128]{3,2,1,0:T(8,128)S(1)}, f32[2,40,40,128]{3,2,1,0:T(8,128)S(1)}, f32[2,40,40,128]{3,2,1,0:T(8,128)S(1)}, f32[2,40,40,128]{3,2,...) custom-call(f32[2,40,40,128]{3,2,1,0:T(8,128)S(1)} %get-tuple-elemen, ...), custom_call_target="tpu_custom_call", output_to_operand_aliasing={{0}: (9, {}), {1}: (10, {}), {2}: (11, {}), {3}: (12, {}), ... | custom-call | tf_op jit(solution)/shard_map/inner_second/pallas_call | solution.py:633
  21.4 0.0 collective-permute-done.4.xb
  21.4 2.6 %collective-permute-done.5.cb = f32[8,8,128]{2,1,0:T(8,128)S(1)} collective-permute-done((f32[8,8,128]{2,1,0:T(8,128)S(1)}, f32[8,8,128]{2,1,0:T(8,128)S(1)}, u32[]{:S(2)}, u32[]{:S(2)}) %collective-permute-start.5) | collective-permute-done | bytes 32800 | tf_op jit(solution)/shard_map/ppermute | solution.py:902
  24.0 1.1 %edge_even.1 = (f32[2,40,40,128]{3,2,1,0:T(8,128)S(1)}, f32[2,40,40,128]{3,2,1,0:T(8,128)S(1)}, f32[2,40,40,128]{3,2,1,0:T(8,128)S(1)}, f32[2,40,40,128]{3,2,1,0...) custom-call(f32[2,8,128]{2,1,0:T(8,128)S(1)} %get-tuple-element.74.f, ...), custom_call_target="tpu_custom_call", output_to_operand_aliasing={{0}: (3, {}), {1}: (4, {}), {2}: (5, {}), {3}: (6, {}), {4}... | custom-call | tf_op jit(solution)/shard_map/edge_even/pallas_call | solution.py:744
  25.2 0.0 collective-permute-done.xb
  25.2 0.0 collective-permute-done.3.cb
  25.2 1.2 %edge_odd.1 = (f32[2,40,40,128]{3,2,1,0:T(8,128)S(1)}, f32[2,40,40,128]{3,2,1,0:T(8,128)S(1)}, f32[2,40,40,128]{3,2,1,0:T(8,128)S(1)}, f32[2,40,40,128]{3,2,1,0:...) custom-call(f32[2,8,128]{2,1,0:T(8,128)S(1)} %get-tuple-element.74.f, ...), custom_call_target="tpu_custom_call", output_to_operand_aliasing={{0}: (3, {}), {1}: (4, {}), {2}: (5, {}), {3}: (6, {}), {4}... | custom-call | tf_op jit(solution)/shard_map/edge_odd/pallas_call | solution.py:744
  26.4 12.8 %all_to_all.11 = f32[16,1,128]{2,1,0:T(1,128)S(1)} all-to-all(f32[16,1,128]{2,1,0:T(1,128)S(1)} %bitcast.6), channel_id=1, replica_groups=mesh['gx'=4,'gy'=4,'af'=2] {'gx','gy'}, dimensions={0} | all-to-all | bytes 16384 | tf_op jit(solution)/shard_map/all_to_all | solution.py:920
  39.2 1.1 %gradient_part.1.one = f32[32,32,128]{2,1,0:T(8,128)S(1)} custom-call(f32[2,8,128]{2,1,0:T(8,128)S(1)} %get-tuple-element.74.freq_sq, f32[16,128]{1,0:T(8,128)S(1)} %bitcast.4, f32[2,40,40,128]{3,2,1,0:T(8,128)S(1)} %get-tuple-element.132.refs_0_, f32[2,40,40,128]{3,2,1,0:T(8,128)S(1)} %get-tuple-element.128.refs_0_.refs_1_, ...), custom_call_target="tpu_custom_call" | custom-call | tf_op jit(solution)/shard_map/gradient_part/pallas_call | solution.py:833
  40.3 0.1 collective-permute-start.6
  40.4 1.5 %wavefield.1 = f32[2,2,32,32,128]{4,3,2,1,0:T(8,128)} custom-call(f32[16,128]{1,0:T(8,128)S(1)} %bitcast.5, f32[2,40,40,128]{3,2,1,0:T(8,128)S(1)} %get-tuple-element.128.refs_0_.refs_1_, f32[2,40,40,128]{3,2,1,0:T(8,128)S(1)} %get-tuple-element.129.refs_1_.refs_3_, f32[2,40,40,128]{3,2,1,0:T(8,128)S(1)} %get-tuple-element.130.refs_2_.refs_6_, ...), custom_call_target="tpu_custom_call" | custom-call | tf_op jit(solution)/shard_map/wavefield/pallas_call | solution.py:841
  41.9 0.4 collective-permute-done.6.two
  42.3 0.8 %add.1 = f32[32,32,128]{2,1,0:T(8,128)} custom-call(f32[32,32,128]{2,1,0:T(8,128)S(1)} %gradient_part.1.one, f32[32,32,128]{2,1,0:T(8,128)S(1)} %collective-permute-done.6.two), custom_call_target="tpu_custom_call" | custom-call | tf_op jit(solution)/shard_map/add/pallas_call | solution.py:876
Async XLA Ops:
  0.6 7.5 %copy-start = (f32[2]{0:T(128)S(1)}, f32[2]{0:T(128)}, u32[]{:S(2)}) copy-start(f32[2]{0:T(128)} %freq_sq.1) | copy-start | bytes 28
  3.3 10.5 %collective-permute-start.1 = (f32[154,4,128]{2,1,0:T(4,128)S(1)}, f32[154,4,128]{2,1,0:T(4,128)S(1)}, u32[]{:S(2)}, u32[]{:S(2)}) collective-permute-start(f32[154,4,128]{2,1,0:T(4,128)S(1)} %get-tuple-element.76), channel_id=1, source_target_pairs={{0,2},{1,3},{2,0},{3,1},{4,6},{5,7},{6,4},{7,5},{8,10},{9,11},{10,... | collective-permute-start | bytes 946184 | tf_op jit(solution)/shard_map/ppermute | solution.py:902
  6.4 7.4 %collective-permute-start.2 = (f32[154,4,128]{2,1,0:T(4,128)S(1)}, f32[154,4,128]{2,1,0:T(4,128)S(1)}, u32[]{:S(2)}, u32[]{:S(2)}) collective-permute-start(f32[154,4,128]{2,1,0:T(4,128)S(1)} %get-tuple-element.77), channel_id=1, source_target_pairs={{0,1},{1,0},{2,4},{3,5},{4,2},{5,3},{6,7},{7,6},{8,9},{9,8},{10,12... | collective-permute-start | bytes 946184 | tf_op jit(solution)/shard_map/ppermute | solution.py:902
  6.4 15.0 %collective-permute-start.4 = (f32[616,128]{1,0:T(8,128)S(1)}, f32[616,128]{1,0:T(8,128)S(1)}, u32[]{:S(2)}, u32[]{:S(2)}) collective-permute-start(f32[616,128]{1,0:T(8,128)S(1)} %get-tuple-element.86), channel_id=1, source_target_pairs={{0,8},{1,9},{2,10},{3,11},{4,12},{5,13},{6,14},{7,15},{8,0},{9,1},... | collective-permute-start | bytes 946184 | tf_op jit(solution)/shard_map/ppermute | solution.py:902
  7.9 17.3 %collective-permute-start = (f32[616,128]{1,0:T(8,128)S(1)}, f32[616,128]{1,0:T(8,128)S(1)}, u32[]{:S(2)}, u32[]{:S(2)}) collective-permute-start(f32[616,128]{1,0:T(8,128)S(1)} %get-tuple-element.75), channel_id=1, source_target_pairs={{0,1},{1,0},{2,3},{3,2},{4,5},{5,4},{6,7},{7,6},{8,16},{9,17},{10,... | collective-permute-start | bytes 946184 | tf_op jit(solution)/shard_map/ppermute | solution.py:902
  16.2 7.8 %collective-permute-start.5 = (f32[8,8,128]{2,1,0:T(8,128)S(1)}, f32[8,8,128]{2,1,0:T(8,128)S(1)}, u32[]{:S(2)}, u32[]{:S(2)}) collective-permute-start(f32[8,8,128]{2,1,0:T(8,128)S(1)} %get-tuple-element.87), channel_id=1, source_target_pairs={{0,8},{1,9},{2,10},{3,11},{4,12},{5,13},{6,14},{7,15},{8,0},{9,1},... | collective-permute-start | bytes 98312 | tf_op jit(solution)/shard_map/ppermute | solution.py:902
  18.0 7.2 %collective-permute-start.3 = (f32[8,8,128]{2,1,0:T(8,128)S(1)}, f32[8,8,128]{2,1,0:T(8,128)S(1)}, u32[]{:S(2)}, u32[]{:S(2)}) collective-permute-start(f32[8,8,128]{2,1,0:T(8,128)S(1)} %get-tuple-element.85), channel_id=1, source_target_pairs={{0,1},{1,0},{2,3},{3,2},{4,5},{5,4},{6,7},{7,6},{8,16},{9,17},{10,... | collective-permute-start | bytes 98312 | tf_op jit(solution)/shard_map/ppermute | solution.py:902
  40.3 2.0 %collective-permute-start.6 = (f32[32,32,128]{2,1,0:T(8,128)S(1)}, f32[32,32,128]{2,1,0:T(8,128)S(1)}, u32[]{:S(2)}, u32[]{:S(2)}) collective-permute-start(f32[32,32,128]{2,1,0:T(8,128)S(1)} %gradient_part.1.one), channel_id=1, source_target_pairs={{0,1},{1,0},{2,3},{3,2},{4,5},{5,4},{6,7},{7,6},{8,9},{9,8},{10,11... | collective-permute-start | bytes 1572872 | tf_op jit(solution)/shard_map/ppermute | solution.py:923

commit v11 on v10

--- a/solution.py
+++ b/solution.py
@@ -799,7 +799,7 @@
             out[x, at, :] = total
         return 0
 
-    lax.fori_loop(0, nx, row, 0, unroll=2)
+    lax.fori_loop(0, nx, row, 0, unroll=4)
 
 
 def wave_kernel(freqs, nx, ny, sums, *refs):
@@ -878,7 +878,7 @@
         out_shape=jax.ShapeDtypeStruct(one.shape, F32),
         in_specs=[VMEM] * 2,
         out_specs=HBM,
-        scratch_shapes=[pltpu.VMEM(one.shape, F32), pltpu.SemaphoreType.DMA((2,))],
+        scratch_shapes=[pltpu.VMEM(one.shape, F32), pltpu.SemaphoreType.DMA((4,))],
         compiler_params=params(4),
         name="add",
     )(one, two)

time: 43.3 us -> 43.2 us (level)
  no operation moved by 1% of the time
where the time goes in v11:
time: 43.2 us; the launch traced here: 43 us
  Pallas kernels  17.6 us (41%)
  blocking collectives  12.8 us (30%)
  starting transfers between devices  6.6 us (15%)
  waiting for transfers between devices  5.28 us (12%)
  between operations  0.72 us (2%)
    all_to_all x1, blocking collectives, on_device(): sums = lax.all_to_all(part, ('gx', 'gy'), 0, 0)  12.8 us
    ppermute x6, starting transfers between devices, swap(): return lax.ppermute(cells, names, pairs)  6.53 us
    ppermute x6, waiting for transfers between devices, swap(): return lax.ppermute(cells, names, pairs)  4.91 us
    pallas_call x1, Pallas kernels, rest(): pl.pallas_call(functools.partial(inner_kernel, freqs, nx, ny, 1, None), o...  3.45 us
    pallas_call x1, Pallas kernels, early(): pl.pallas_call(functools.partial(early_kernel, freqs, nx, ny), out_shape=...  3.43 us
    pallas_call x1, Pallas kernels, load(): pl.pallas_call(load_kernel, out_shape=(pltpu.VMEM((2, nx + 2 * HALO, ny +...  2.63 us
    pallas_call x1, Pallas kernels, inner_part(): pl.pallas_call(functools.partial(inner_kernel, freqs, nx, ny, 0), out_sha...  2.41 us
    pallas_call x2, Pallas kernels, edge_part(): pl.pallas_call(functools.partial(edge_kernel, side, peers, freqs, nx, ny)...  2.33 us
  transfers between devices with their start and end apart: 7, of which 3 were waited for; matrix products, arithmetic and copies ran while one was open for 0% of the time, Pallas kernels for 28%

profile of v11, /device:TPU:0, one launch (start us, length us, event | category | flops | bytes accessed | tf_op | source)
XLA Modules:
  0.0 43.0 jit_solution(7779922951558580937)
XLA Ops:
  0.6 0.0 copy-start
  0.6 2.6 %load.1 = (f32[2,40,40,128]{3,2,1,0:T(8,128)S(1)}, f32[2,40,40,128]{3,2,1,0:T(8,128)S(1)}, f32[32,40,128]{2,1,0:T(8,128)S(1)}, f32[5,40,128]{2,1,0:T(8,128)S(1)}...) custom-call(f32[2,2,32,32,128]{4,3,2,1,0:T(8,128)} %source.1, ...), custom_call_target="tpu_custom_call" | custom-call | tf_op jit(solution)/shard_map/load/pallas_call | solution.py:165
  3.3 3.1 %collective-permute-start.1 = (f32[154,4,128]{2,1,0:T(4,128)S(1)}, f32[154,4,128]{2,1,0:T(4,128)S(1)}, u32[]{:S(2)}, u32[]{:S(2)}) collective-permute-start(f32[154,4,128]{2,1,0:T(4,128)S(1)} %get-tuple-element.76), channel_id=1, source_target_pairs={{0,2},{1,3},{2,0},{3,1},{4,6},{5,7},{6,4},{7,5},{8,10},{9,11},{10,... | collective-permute-start | bytes 946184 | tf_op jit(solution)/shard_map/ppermute | solution.py:902
  6.4 0.0 collective-permute-start.2
  6.4 1.5 %collective-permute-start.4 = (f32[616,128]{1,0:T(8,128)S(1)}, f32[616,128]{1,0:T(8,128)S(1)}, u32[]{:S(2)}, u32[]{:S(2)}) collective-permute-start(f32[616,128]{1,0:T(8,128)S(1)} %get-tuple-element.86), channel_id=1, source_target_pairs={{0,8},{1,9},{2,10},{3,11},{4,12},{5,13},{6,14},{7,15},{8,0},{9,1},... | collective-permute-start | bytes 946184 | tf_op jit(solution)/shard_map/ppermute | solution.py:902
  7.9 0.2 collective-permute-start
  8.1 0.0 copy-done
  8.1 3.4 %early.1 = (f32[2,40,40,128]{3,2,1,0:T(8,128)S(1)}, f32[40,5,8,128]{3,2,1,0:T(8,128)S(1)}, f32[40,5,8,128]{3,2,1,0:T(8,128)S(1)}, f32[2,40,40,128]{3,2,1,0:T(8,1...) custom-call(f32[2]{0:T(128)S(1)} %copy-done, ...), custom_call_target="tpu_custom_call" | custom-call | tf_op jit(solution)/shard_map/early/pallas_call | solution.py:427
  11.5 2.3 %collective-permute-done.1.refs_0_ = f32[154,4,128]{2,1,0:T(4,128)S(1)} collective-permute-done((f32[154,4,128]{2,1,0:T(4,128)S(1)}, f32[154,4,128]{2,1,0:T(4,128)S(1)}, u32[]{:S(2)}, u32[]{:S(2)}) %collective-permute-start.1) | collective-permute-done | bytes 315424 | tf_op jit(solution)/shard_map/ppermute | solution.py:902
  13.8 0.0 collective-permute-done.2.refs_1_
  13.8 2.4 %inner_first.1 = (f32[2,40,40,128]{3,2,1,0:T(8,128)S(1)}, f32[2,40,40,128]{3,2,1,0:T(8,128)S(1)}, f32[32,40,128]{2,1,0:T(8,128)S(1)}, f32[5,40,128]{2,1,0:T(8,12...) custom-call(f32[2,8,128]{2,1,0:T(8,128)S(1)} %get-tuple-element.74.f, ...), custom_call_target="tpu_custom_call", output_to_operand_aliasing={{0}: (3, {}), {1}: (4, {}), {2}: (5, {}), {3}: (6, {}), {4}... | custom-call | tf_op jit(solution)/shard_map/inner_first/pallas_call | solution.py:618
  16.2 1.7 %collective-permute-start.5 = (f32[8,8,128]{2,1,0:T(8,128)S(1)}, f32[8,8,128]{2,1,0:T(8,128)S(1)}, u32[]{:S(2)}, u32[]{:S(2)}) collective-permute-start(f32[8,8,128]{2,1,0:T(8,128)S(1)} %get-tuple-element.87), channel_id=1, source_target_pairs={{0,8},{1,9},{2,10},{3,11},{4,12},{5,13},{6,14},{7,15},{8,0},{9,1},... | collective-permute-start | bytes 98312 | tf_op jit(solution)/shard_map/ppermute | solution.py:902
  18.0 0.0 collective-permute-start.3
  18.0 3.4 %inner_second.1 = (f32[2,40,40,128]{3,2,1,0:T(8,128)S(1)}, f32[2,40,40,128]{3,2,1,0:T(8,128)S(1)}, f32[2,40,40,128]{3,2,1,0:T(8,128)S(1)}, f32[2,40,40,128]{3,2,...) custom-call(f32[2,40,40,128]{3,2,1,0:T(8,128)S(1)} %get-tuple-elemen, ...), custom_call_target="tpu_custom_call", output_to_operand_aliasing={{0}: (9, {}), {1}: (10, {}), {2}: (11, {}), {3}: (12, {}), ... | custom-call | tf_op jit(solution)/shard_map/inner_second/pallas_call | solution.py:633
  21.4 0.0 collective-permute-done.4.xb
  21.4 2.6 %collective-permute-done.5.cb = f32[8,8,128]{2,1,0:T(8,128)S(1)} collective-permute-done((f32[8,8,128]{2,1,0:T(8,128)S(1)}, f32[8,8,128]{2,1,0:T(8,128)S(1)}, u32[]{:S(2)}, u32[]{:S(2)}) %collective-permute-start.5) | collective-permute-done | bytes 32800 | tf_op jit(solution)/shard_map/ppermute | solution.py:902
  24.0 1.1 %edge_even.1 = (f32[2,40,40,128]{3,2,1,0:T(8,128)S(1)}, f32[2,40,40,128]{3,2,1,0:T(8,128)S(1)}, f32[2,40,40,128]{3,2,1,0:T(8,128)S(1)}, f32[2,40,40,128]{3,2,1,0...) custom-call(f32[2,8,128]{2,1,0:T(8,128)S(1)} %get-tuple-element.74.f, ...), custom_call_target="tpu_custom_call", output_to_operand_aliasing={{0}: (3, {}), {1}: (4, {}), {2}: (5, {}), {3}: (6, {}), {4}... | custom-call | tf_op jit(solution)/shard_map/edge_even/pallas_call | solution.py:744
  25.2 0.0 collective-permute-done.xb
  25.2 0.0 collective-permute-done.3.cb
  25.2 1.2 %edge_odd.1 = (f32[2,40,40,128]{3,2,1,0:T(8,128)S(1)}, f32[2,40,40,128]{3,2,1,0:T(8,128)S(1)}, f32[2,40,40,128]{3,2,1,0:T(8,128)S(1)}, f32[2,40,40,128]{3,2,1,0:...) custom-call(f32[2,8,128]{2,1,0:T(8,128)S(1)} %get-tuple-element.74.f, ...), custom_call_target="tpu_custom_call", output_to_operand_aliasing={{0}: (3, {}), {1}: (4, {}), {2}: (5, {}), {3}: (6, {}), {4}... | custom-call | tf_op jit(solution)/shard_map/edge_odd/pallas_call | solution.py:744
  26.4 12.8 %all_to_all.11 = f32[16,1,128]{2,1,0:T(1,128)S(1)} all-to-all(f32[16,1,128]{2,1,0:T(1,128)S(1)} %bitcast.6), channel_id=1, replica_groups=mesh['gx'=4,'gy'=4,'af'=2] {'gx','gy'}, dimensions={0} | all-to-all | bytes 16384 | tf_op jit(solution)/shard_map/all_to_all | solution.py:920
  39.2 1.0 %gradient_part.1.one = f32[32,32,128]{2,1,0:T(8,128)S(1)} custom-call(f32[2,8,128]{2,1,0:T(8,128)S(1)} %get-tuple-element.74.freq_sq, f32[16,128]{1,0:T(8,128)S(1)} %bitcast.4, f32[2,40,40,128]{3,2,1,0:T(8,128)S(1)} %get-tuple-element.132.refs_0_, f32[2,40,40,128]{3,2,1,0:T(8,128)S(1)} %get-tuple-element.128.refs_0_.refs_1_, ...), custom_call_target="tpu_custom_call" | custom-call | tf_op jit(solution)/shard_map/gradient_part/pallas_call | solution.py:833
  40.2 0.1 collective-permute-start.6
  40.3 1.5 %wavefield.1 = f32[2,2,32,32,128]{4,3,2,1,0:T(8,128)} custom-call(f32[16,128]{1,0:T(8,128)S(1)} %bitcast.5, f32[2,40,40,128]{3,2,1,0:T(8,128)S(1)} %get-tuple-element.128.refs_0_.refs_1_, f32[2,40,40,128]{3,2,1,0:T(8,128)S(1)} %get-tuple-element.129.refs_1_.refs_3_, f32[2,40,40,128]{3,2,1,0:T(8,128)S(1)} %get-tuple-element.130.refs_2_.refs_6_, ...), custom_call_target="tpu_custom_call" | custom-call | tf_op jit(solution)/shard_map/wavefield/pallas_call | solution.py:841
  41.8 0.4 collective-permute-done.6.two
  42.2 0.8 %add.1 = f32[32,32,128]{2,1,0:T(8,128)} custom-call(f32[32,32,128]{2,1,0:T(8,128)S(1)} %gradient_part.1.one, f32[32,32,128]{2,1,0:T(8,128)S(1)} %collective-permute-done.6.two), custom_call_target="tpu_custom_call" | custom-call | tf_op jit(solution)/shard_map/add/pallas_call | solution.py:876
Async XLA Ops:
  0.6 7.5 %copy-start = (f32[2]{0:T(128)S(1)}, f32[2]{0:T(128)}, u32[]{:S(2)}) copy-start(f32[2]{0:T(128)} %freq_sq.1) | copy-start | bytes 28
  3.3 10.5 %collective-permute-start.1 = (f32[154,4,128]{2,1,0:T(4,128)S(1)}, f32[154,4,128]{2,1,0:T(4,128)S(1)}, u32[]{:S(2)}, u32[]{:S(2)}) collective-permute-start(f32[154,4,128]{2,1,0:T(4,128)S(1)} %get-tuple-element.76), channel_id=1, source_target_pairs={{0,2},{1,3},{2,0},{3,1},{4,6},{5,7},{6,4},{7,5},{8,10},{9,11},{10,... | collective-permute-start | bytes 946184 | tf_op jit(solution)/shard_map/ppermute | solution.py:902
  6.4 7.4 %collective-permute-start.2 = (f32[154,4,128]{2,1,0:T(4,128)S(1)}, f32[154,4,128]{2,1,0:T(4,128)S(1)}, u32[]{:S(2)}, u32[]{:S(2)}) collective-permute-start(f32[154,4,128]{2,1,0:T(4,128)S(1)} %get-tuple-element.77), channel_id=1, source_target_pairs={{0,1},{1,0},{2,4},{3,5},{4,2},{5,3},{6,7},{7,6},{8,9},{9,8},{10,12... | collective-permute-start | bytes 946184 | tf_op jit(solution)/shard_map/ppermute | solution.py:902
  6.4 15.0 %collective-permute-start.4 = (f32[616,128]{1,0:T(8,128)S(1)}, f32[616,128]{1,0:T(8,128)S(1)}, u32[]{:S(2)}, u32[]{:S(2)}) collective-permute-start(f32[616,128]{1,0:T(8,128)S(1)} %get-tuple-element.86), channel_id=1, source_target_pairs={{0,8},{1,9},{2,10},{3,11},{4,12},{5,13},{6,14},{7,15},{8,0},{9,1},... | collective-permute-start | bytes 946184 | tf_op jit(solution)/shard_map/ppermute | solution.py:902
  7.9 17.3 %collective-permute-start = (f32[616,128]{1,0:T(8,128)S(1)}, f32[616,128]{1,0:T(8,128)S(1)}, u32[]{:S(2)}, u32[]{:S(2)}) collective-permute-start(f32[616,128]{1,0:T(8,128)S(1)} %get-tuple-element.75), channel_id=1, source_target_pairs={{0,1},{1,0},{2,3},{3,2},{4,5},{5,4},{6,7},{7,6},{8,16},{9,17},{10,... | collective-permute-start | bytes 946184 | tf_op jit(solution)/shard_map/ppermute | solution.py:902
  16.2 7.8 %collective-permute-start.5 = (f32[8,8,128]{2,1,0:T(8,128)S(1)}, f32[8,8,128]{2,1,0:T(8,128)S(1)}, u32[]{:S(2)}, u32[]{:S(2)}) collective-permute-start(f32[8,8,128]{2,1,0:T(8,128)S(1)} %get-tuple-element.87), channel_id=1, source_target_pairs={{0,8},{1,9},{2,10},{3,11},{4,12},{5,13},{6,14},{7,15},{8,0},{9,1},... | collective-permute-start | bytes 98312 | tf_op jit(solution)/shard_map/ppermute | solution.py:902
  18.0 7.2 %collective-permute-start.3 = (f32[8,8,128]{2,1,0:T(8,128)S(1)}, f32[8,8,128]{2,1,0:T(8,128)S(1)}, u32[]{:S(2)}, u32[]{:S(2)}) collective-permute-start(f32[8,8,128]{2,1,0:T(8,128)S(1)} %get-tuple-element.85), channel_id=1, source_target_pairs={{0,1},{1,0},{2,3},{3,2},{4,5},{5,4},{6,7},{7,6},{8,16},{9,17},{10,... | collective-permute-start | bytes 98312 | tf_op jit(solution)/shard_map/ppermute | solution.py:902
  40.2 2.0 %collective-permute-start.6 = (f32[32,32,128]{2,1,0:T(8,128)S(1)}, f32[32,32,128]{2,1,0:T(8,128)S(1)}, u32[]{:S(2)}, u32[]{:S(2)}) collective-permute-start(f32[32,32,128]{2,1,0:T(8,128)S(1)} %gradient_part.1.one), channel_id=1, source_target_pairs={{0,1},{1,0},{2,3},{3,2},{4,5},{5,4},{6,7},{7,6},{8,9},{9,8},{10,11... | collective-permute-start | bytes 1572872 | tf_op jit(solution)/shard_map/ppermute | solution.py:923

commit v12 on v11

--- a/solution.py
+++ b/solution.py
@@ -144,7 +144,7 @@
             yo[fields * nx + 3 * g + j] = jnp.where(swapped, head, tail)
         return 0
 
-    lax.fori_loop(0, nx // 4, model_rows, 0, unroll=2)
+    lax.fori_loop(0, nx // 4, model_rows, 0, unroll=4)
     for xb, skip, _ in faces:
         x_face(xb, fields * HALO, cells, skip, INNER)
     for k in range(fields):
@@ -538,8 +538,8 @@
                 s[k // 2][k % 2, x, ny:, :] = halo(k * nx + x)
             return 0
 
-        lax.fori_loop(0, nx // 4, model_rows, 0, unroll=2)
-        lax.fori_loop(0, nx, merge, 0, unroll=4)
+        lax.fori_loop(0, nx // 4, model_rows, 0, unroll=4)
+        lax.fori_loop(0, nx, merge, 0, unroll=8)
         for k in range(fields + 1):
             slab, g = divmod(k, nz // nx)
             tile = halo(fields * nx + nx // 4 * 3 + slab)
@@ -588,7 +588,7 @@
     edges = sorted({e for span in spans for e in span} | {middle})
     acc = tuple(tuple(grid.zero() for _ in range(4)) for _ in range(freqs))
     if half == 0:
-        lax.fori_loop(1, nx - 1, heads, 0, unroll=3)
+        lax.fori_loop(1, nx - 1, heads, 0, unroll=5)
     for lo, hi in zip(edges[:-1], edges[1:]):
         if (lo < middle) != (half == 0):
             continue

time: 43.2 us -> 43.2 us (level)
  transfers between devices with their start and end apart: 7 -> 7, of which waited for: 3 -> 3; matrix products, arithmetic and copies ran while one was open for 0% -> 0% of each run, Pallas kernels for 28% -> 27%
where the time goes in v12:
time: 43.2 us; the launch traced here: 43 us
  Pallas kernels  17.3 us (40%)
  blocking collectives  12.8 us (30%)
  starting transfers between devices  6.6 us (15%)
  waiting for transfers between devices  5.58 us (13%)
  between operations  0.72 us (2%)
    all_to_all x1, blocking collectives, on_device(): sums = lax.all_to_all(part, ('gx', 'gy'), 0, 0)  12.8 us
    ppermute x6, starting transfers between devices, swap(): return lax.ppermute(cells, names, pairs)  6.53 us
    ppermute x6, waiting for transfers between devices, swap(): return lax.ppermute(cells, names, pairs)  5.21 us
    pallas_call x1, Pallas kernels, rest(): pl.pallas_call(functools.partial(inner_kernel, freqs, nx, ny, 1, None), o...  3.45 us
    pallas_call x1, Pallas kernels, early(): pl.pallas_call(functools.partial(early_kernel, freqs, nx, ny), out_shape=...  3.43 us
    pallas_call x1, Pallas kernels, load(): pl.pallas_call(load_kernel, out_shape=(pltpu.VMEM((2, nx + 2 * HALO, ny +...  2.63 us
    pallas_call x2, Pallas kernels, edge_part(): pl.pallas_call(functools.partial(edge_kernel, side, peers, freqs, nx, ny)...  2.33 us
    pallas_call x1, Pallas kernels, inner_part(): pl.pallas_call(functools.partial(inner_kernel, freqs, nx, ny, 0), out_sha...  2.11 us
  transfers between devices with their start and end apart: 7, of which 3 were waited for; matrix products, arithmetic and copies ran while one was open for 0% of the time, Pallas kernels for 27%

profile of v12, /device:TPU:0, one launch (start us, length us, event | category | flops | bytes accessed | tf_op | source)
XLA Modules:
  0.0 43.0 jit_solution(11009348430224361810)
XLA Ops:
  0.6 0.0 copy-start
  0.6 2.6 %load.1 = (f32[2,40,40,128]{3,2,1,0:T(8,128)S(1)}, f32[2,40,40,128]{3,2,1,0:T(8,128)S(1)}, f32[32,40,128]{2,1,0:T(8,128)S(1)}, f32[5,40,128]{2,1,0:T(8,128)S(1)}...) custom-call(f32[2,2,32,32,128]{4,3,2,1,0:T(8,128)} %source.1, ...), custom_call_target="tpu_custom_call" | custom-call | tf_op jit(solution)/shard_map/load/pallas_call | solution.py:165
  3.3 3.1 %collective-permute-start.1 = (f32[154,4,128]{2,1,0:T(4,128)S(1)}, f32[154,4,128]{2,1,0:T(4,128)S(1)}, u32[]{:S(2)}, u32[]{:S(2)}) collective-permute-start(f32[154,4,128]{2,1,0:T(4,128)S(1)} %get-tuple-element.76), channel_id=1, source_target_pairs={{0,2},{1,3},{2,0},{3,1},{4,6},{5,7},{6,4},{7,5},{8,10},{9,11},{10,... | collective-permute-start | bytes 946184 | tf_op jit(solution)/shard_map/ppermute | solution.py:902
  6.4 0.0 collective-permute-start.2
  6.4 1.5 %collective-permute-start.4 = (f32[616,128]{1,0:T(8,128)S(1)}, f32[616,128]{1,0:T(8,128)S(1)}, u32[]{:S(2)}, u32[]{:S(2)}) collective-permute-start(f32[616,128]{1,0:T(8,128)S(1)} %get-tuple-element.86), channel_id=1, source_target_pairs={{0,8},{1,9},{2,10},{3,11},{4,12},{5,13},{6,14},{7,15},{8,0},{9,1},... | collective-permute-start | bytes 946184 | tf_op jit(solution)/shard_map/ppermute | solution.py:902
  7.9 0.2 collective-permute-start
  8.1 0.0 copy-done
  8.1 3.4 %early.1 = (f32[2,40,40,128]{3,2,1,0:T(8,128)S(1)}, f32[40,5,8,128]{3,2,1,0:T(8,128)S(1)}, f32[40,5,8,128]{3,2,1,0:T(8,128)S(1)}, f32[2,40,40,128]{3,2,1,0:T(8,1...) custom-call(f32[2]{0:T(128)S(1)} %copy-done, ...), custom_call_target="tpu_custom_call" | custom-call | tf_op jit(solution)/shard_map/early/pallas_call | solution.py:427
  11.5 2.3 %collective-permute-done.1.refs_0_ = f32[154,4,128]{2,1,0:T(4,128)S(1)} collective-permute-done((f32[154,4,128]{2,1,0:T(4,128)S(1)}, f32[154,4,128]{2,1,0:T(4,128)S(1)}, u32[]{:S(2)}, u32[]{:S(2)}) %collective-permute-start.1) | collective-permute-done | bytes 315424 | tf_op jit(solution)/shard_map/ppermute | solution.py:902
  13.8 0.0 collective-permute-done.2.refs_1_
  13.8 2.1 %inner_first.1 = (f32[2,40,40,128]{3,2,1,0:T(8,128)S(1)}, f32[2,40,40,128]{3,2,1,0:T(8,128)S(1)}, f32[32,40,128]{2,1,0:T(8,128)S(1)}, f32[5,40,128]{2,1,0:T(8,12...) custom-call(f32[2,8,128]{2,1,0:T(8,128)S(1)} %get-tuple-element.74.f, ...), custom_call_target="tpu_custom_call", output_to_operand_aliasing={{0}: (3, {}), {1}: (4, {}), {2}: (5, {}), {3}: (6, {}), {4}... | custom-call | tf_op jit(solution)/shard_map/inner_first/pallas_call | solution.py:618
  15.9 1.7 %collective-permute-start.5 = (f32[8,8,128]{2,1,0:T(8,128)S(1)}, f32[8,8,128]{2,1,0:T(8,128)S(1)}, u32[]{:S(2)}, u32[]{:S(2)}) collective-permute-start(f32[8,8,128]{2,1,0:T(8,128)S(1)} %get-tuple-element.87), channel_id=1, source_target_pairs={{0,8},{1,9},{2,10},{3,11},{4,12},{5,13},{6,14},{7,15},{8,0},{9,1},... | collective-permute-start | bytes 98312 | tf_op jit(solution)/shard_map/ppermute | solution.py:902
  17.7 0.0 collective-permute-start.3
  17.7 3.4 %inner_second.1 = (f32[2,40,40,128]{3,2,1,0:T(8,128)S(1)}, f32[2,40,40,128]{3,2,1,0:T(8,128)S(1)}, f32[2,40,40,128]{3,2,1,0:T(8,128)S(1)}, f32[2,40,40,128]{3,2,...) custom-call(f32[2,40,40,128]{3,2,1,0:T(8,128)S(1)} %get-tuple-elemen, ...), custom_call_target="tpu_custom_call", output_to_operand_aliasing={{0}: (9, {}), {1}: (10, {}), {2}: (11, {}), {3}: (12, {}), ... | custom-call | tf_op jit(solution)/shard_map/inner_second/pallas_call | solution.py:633
  21.1 0.0 collective-permute-done.4.xb
  21.1 2.9 %collective-permute-done.5.cb = f32[8,8,128]{2,1,0:T(8,128)S(1)} collective-permute-done((f32[8,8,128]{2,1,0:T(8,128)S(1)}, f32[8,8,128]{2,1,0:T(8,128)S(1)}, u32[]{:S(2)}, u32[]{:S(2)}) %collective-permute-start.5) | collective-permute-done | bytes 32800 | tf_op jit(solution)/shard_map/ppermute | solution.py:902
  24.0 1.1 %edge_even.1 = (f32[2,40,40,128]{3,2,1,0:T(8,128)S(1)}, f32[2,40,40,128]{3,2,1,0:T(8,128)S(1)}, f32[2,40,40,128]{3,2,1,0:T(8,128)S(1)}, f32[2,40,40,128]{3,2,1,0...) custom-call(f32[2,8,128]{2,1,0:T(8,128)S(1)} %get-tuple-element.74.f, ...), custom_call_target="tpu_custom_call", output_to_operand_aliasing={{0}: (3, {}), {1}: (4, {}), {2}: (5, {}), {3}: (6, {}), {4}... | custom-call | tf_op jit(solution)/shard_map/edge_even/pallas_call | solution.py:744
  25.2 0.0 collective-permute-done.xb
  25.2 0.0 collective-permute-done.3.cb
  25.2 1.2 %edge_odd.1 = (f32[2,40,40,128]{3,2,1,0:T(8,128)S(1)}, f32[2,40,40,128]{3,2,1,0:T(8,128)S(1)}, f32[2,40,40,128]{3,2,1,0:T(8,128)S(1)}, f32[2,40,40,128]{3,2,1,0:...) custom-call(f32[2,8,128]{2,1,0:T(8,128)S(1)} %get-tuple-element.74.f, ...), custom_call_target="tpu_custom_call", output_to_operand_aliasing={{0}: (3, {}), {1}: (4, {}), {2}: (5, {}), {3}: (6, {}), {4}... | custom-call | tf_op jit(solution)/shard_map/edge_odd/pallas_call | solution.py:744
  26.4 12.8 %all_to_all.11 = f32[16,1,128]{2,1,0:T(1,128)S(1)} all-to-all(f32[16,1,128]{2,1,0:T(1,128)S(1)} %bitcast.6), channel_id=1, replica_groups=mesh['gx'=4,'gy'=4,'af'=2] {'gx','gy'}, dimensions={0} | all-to-all | bytes 16384 | tf_op jit(solution)/shard_map/all_to_all | solution.py:920
  39.2 1.0 %gradient_part.1.one = f32[32,32,128]{2,1,0:T(8,128)S(1)} custom-call(f32[2,8,128]{2,1,0:T(8,128)S(1)} %get-tuple-element.74.freq_sq, f32[16,128]{1,0:T(8,128)S(1)} %bitcast.4, f32[2,40,40,128]{3,2,1,0:T(8,128)S(1)} %get-tuple-element.132.refs_0_, f32[2,40,40,128]{3,2,1,0:T(8,128)S(1)} %get-tuple-element.128.refs_0_.refs_1_, ...), custom_call_target="tpu_custom_call" | custom-call | tf_op jit(solution)/shard_map/gradient_part/pallas_call | solution.py:833
  40.2 0.1 collective-permute-start.6
  40.3 1.5 %wavefield.1 = f32[2,2,32,32,128]{4,3,2,1,0:T(8,128)} custom-call(f32[16,128]{1,0:T(8,128)S(1)} %bitcast.5, f32[2,40,40,128]{3,2,1,0:T(8,128)S(1)} %get-tuple-element.128.refs_0_.refs_1_, f32[2,40,40,128]{3,2,1,0:T(8,128)S(1)} %get-tuple-element.129.refs_1_.refs_3_, f32[2,40,40,128]{3,2,1,0:T(8,128)S(1)} %get-tuple-element.130.refs_2_.refs_6_, ...), custom_call_target="tpu_custom_call" | custom-call | tf_op jit(solution)/shard_map/wavefield/pallas_call | solution.py:841
  41.8 0.4 collective-permute-done.6.two
  42.2 0.8 %add.1 = f32[32,32,128]{2,1,0:T(8,128)} custom-call(f32[32,32,128]{2,1,0:T(8,128)S(1)} %gradient_part.1.one, f32[32,32,128]{2,1,0:T(8,128)S(1)} %collective-permute-done.6.two), custom_call_target="tpu_custom_call" | custom-call | tf_op jit(solution)/shard_map/add/pallas_call | solution.py:876
Async XLA Ops:
  0.6 7.5 %copy-start = (f32[2]{0:T(128)S(1)}, f32[2]{0:T(128)}, u32[]{:S(2)}) copy-start(f32[2]{0:T(128)} %freq_sq.1) | copy-start | bytes 28
  3.3 10.5 %collective-permute-start.1 = (f32[154,4,128]{2,1,0:T(4,128)S(1)}, f32[154,4,128]{2,1,0:T(4,128)S(1)}, u32[]{:S(2)}, u32[]{:S(2)}) collective-permute-start(f32[154,4,128]{2,1,0:T(4,128)S(1)} %get-tuple-element.76), channel_id=1, source_target_pairs={{0,2},{1,3},{2,0},{3,1},{4,6},{5,7},{6,4},{7,5},{8,10},{9,11},{10,... | collective-permute-start | bytes 946184 | tf_op jit(solution)/shard_map/ppermute | solution.py:902
  6.4 7.4 %collective-permute-start.2 = (f32[154,4,128]{2,1,0:T(4,128)S(1)}, f32[154,4,128]{2,1,0:T(4,128)S(1)}, u32[]{:S(2)}, u32[]{:S(2)}) collective-permute-start(f32[154,4,128]{2,1,0:T(4,128)S(1)} %get-tuple-element.77), channel_id=1, source_target_pairs={{0,1},{1,0},{2,4},{3,5},{4,2},{5,3},{6,7},{7,6},{8,9},{9,8},{10,12... | collective-permute-start | bytes 946184 | tf_op jit(solution)/shard_map/ppermute | solution.py:902
  6.4 14.7 %collective-permute-start.4 = (f32[616,128]{1,0:T(8,128)S(1)}, f32[616,128]{1,0:T(8,128)S(1)}, u32[]{:S(2)}, u32[]{:S(2)}) collective-permute-start(f32[616,128]{1,0:T(8,128)S(1)} %get-tuple-element.86), channel_id=1, source_target_pairs={{0,8},{1,9},{2,10},{3,11},{4,12},{5,13},{6,14},{7,15},{8,0},{9,1},... | collective-permute-start | bytes 946184 | tf_op jit(solution)/shard_map/ppermute | solution.py:902
  7.9 17.3 %collective-permute-start = (f32[616,128]{1,0:T(8,128)S(1)}, f32[616,128]{1,0:T(8,128)S(1)}, u32[]{:S(2)}, u32[]{:S(2)}) collective-permute-start(f32[616,128]{1,0:T(8,128)S(1)} %get-tuple-element.75), channel_id=1, source_target_pairs={{0,1},{1,0},{2,3},{3,2},{4,5},{5,4},{6,7},{7,6},{8,16},{9,17},{10,... | collective-permute-start | bytes 946184 | tf_op jit(solution)/shard_map/ppermute | solution.py:902
  15.9 8.1 %collective-permute-start.5 = (f32[8,8,128]{2,1,0:T(8,128)S(1)}, f32[8,8,128]{2,1,0:T(8,128)S(1)}, u32[]{:S(2)}, u32[]{:S(2)}) collective-permute-start(f32[8,8,128]{2,1,0:T(8,128)S(1)} %get-tuple-element.87), channel_id=1, source_target_pairs={{0,8},{1,9},{2,10},{3,11},{4,12},{5,13},{6,14},{7,15},{8,0},{9,1},... | collective-permute-start | bytes 98312 | tf_op jit(solution)/shard_map/ppermute | solution.py:902
  17.7 7.5 %collective-permute-start.3 = (f32[8,8,128]{2,1,0:T(8,128)S(1)}, f32[8,8,128]{2,1,0:T(8,128)S(1)}, u32[]{:S(2)}, u32[]{:S(2)}) collective-permute-start(f32[8,8,128]{2,1,0:T(8,128)S(1)} %get-tuple-element.85), channel_id=1, source_target_pairs={{0,1},{1,0},{2,3},{3,2},{4,5},{5,4},{6,7},{7,6},{8,16},{9,17},{10,... | collective-permute-start | bytes 98312 | tf_op jit(solution)/shard_map/ppermute | solution.py:902
  40.2 2.0 %collective-permute-start.6 = (f32[32,32,128]{2,1,0:T(8,128)S(1)}, f32[32,32,128]{2,1,0:T(8,128)S(1)}, u32[]{:S(2)}, u32[]{:S(2)}) collective-permute-start(f32[32,32,128]{2,1,0:T(8,128)S(1)} %gradient_part.1.one), channel_id=1, source_target_pairs={{0,1},{1,0},{2,3},{3,2},{4,5},{5,4},{6,7},{7,6},{8,9},{9,8},{10,11... | collective-permute-start | bytes 1572872 | tf_op jit(solution)/shard_map/ppermute | solution.py:923
